TPU v7x, 256 devices: a whole 4x4x8 slice. The times are simulated.
256 devices in a mesh: grp: 8 (over y, core), fsdp: 32 (over z, x).
Axes of the slice: x: 4, y: 4, z: 8, core: 2. Of those that a mesh axis runs over, the one named last changes fastest.
Arguments:
- gradient: float32 [8, 2048, 7168], P('grp', None, 'fsdp'), may hold values from -20000 to 20000
- master: float32 [8, 2048, 7168], P('grp', 'fsdp'), may hold values from -6 to 6
- first_moment: float32 [8, 2048, 7168], P('grp', 'fsdp'), may hold values from -0.3 to 0.3
- second_moment: float32 [8, 2048, 7168], P('grp', 'fsdp'), may hold values from 0.0005 to 0.05
- slot_expert: int32 [8, 4], P('grp'), may hold values from -1 to 7, as said below
Outputs:
- rollout: bfloat16 [32, 2048, 7168], P('grp', None, 'fsdp')
Inputs may be any that keep to these rules, and one draw needn't show every extreme that they name: `slot_expert`: each rollout group has 4 slots; its live slots come first and the rest hold -1; no expert stands twice in one group; every expert stands in at least one slot; at least one group has all 4 slots live.
All inputs are finite; a program needn't handle non-finite values.
Results may differ from a plain program's by a relative error of at most 0.00185.
Values may be sent and summed in bfloat16 or wider, within the bound.
No kernel may reach another device: no remote copies, remote signals or barrier semaphores. Data moves between devices by JAX's collectives and lax.ppermute only.
A program may use at most 128 MiB of HBM per device.

v0:
```python
import jax
import jax.numpy as jnp
from jax import lax
from jax.sharding import PartitionSpec as P

D = 7168
FF = 2048


first_decay = 0.9
second_decay = 0.95
first_bias = 1.0 - 0.9**10
second_bias = 1.0 - 0.95**10
learn_rate = 0.2
shrink = 0.98
epsilon = 1e-08
stabilizer = 1e-06
clip_level = 1.0


def adam_weights(gradient, master, first_moment, second_moment, factor):
    scaled = factor * gradient
    first_new = first_decay * first_moment + (1.0 - first_decay) * scaled
    second_new = second_decay * second_moment + (1.0 - second_decay) * scaled * scaled
    update = first_new / first_bias / (jnp.sqrt(second_new / second_bias) + epsilon)
    return (shrink * master - learn_rate * update).astype(jnp.bfloat16)


def place_slots(weights, slot_ids):
    blank_slots = jnp.zeros((slot_ids.shape[0],) + weights.shape[1:], jnp.bfloat16)
    arrived = lax.all_gather(weights, "grp", axis=0, tiled=True)
    inside = (slot_ids >= 0) & (slot_ids < arrived.shape[0])
    picked = jnp.take(arrived, jnp.clip(slot_ids, 0, arrived.shape[0] - 1), axis=0)
    return jnp.where(inside[:, None, None], picked, blank_slots)


def to_columns(owned_rows):
    return lax.all_to_all(owned_rows, "fsdp", split_axis=2, concat_axis=1, tiled=True)


def body(gradient, master, first_moment, second_moment, slot_expert):
    entries = lax.axis_size("grp") * master.shape[0] * FF * D
    slot_ids = slot_expert.reshape(-1)
    grad_here = lax.all_to_all(
        gradient.astype(jnp.bfloat16), "fsdp", split_axis=1, concat_axis=2, tiled=True
    ).astype(gradient.dtype)
    master_here, first_here, second_here = (master, first_moment, second_moment)
    square_total = lax.psum(jnp.sum(grad_here * grad_here), ("grp", "fsdp"))
    factor = jnp.minimum(1.0, clip_level / jnp.sqrt(square_total / entries + stabilizer))
    weights = adam_weights(grad_here, master_here, first_here, second_here, factor)
    rollout = to_columns(place_slots(weights, slot_ids))
    return rollout


def solution(mesh):
    in_specs = (
        P("grp", None, "fsdp"),
        P("grp", "fsdp", None),
        P("grp", "fsdp", None),
        P("grp", "fsdp", None),
        P("grp", None),
    )
    out_specs = P("grp", None, "fsdp")
    return jax.shard_map(body, mesh=mesh, in_specs=in_specs, out_specs=out_specs, check_vma=False)
```

profile of v0, /device:TPU:1, one launch (start us, length us, event | category | flops | bytes accessed | tf_op | source)
XLA Modules:
  0.0 362.4 jit_solution(1137351037920003439)
XLA Ops:
  6.5 0.0 all-gather.2.cloned.1.call-start
  6.5 1.6 convert_element_type.28
  8.2 1.7 copy.15
  9.8 0.5 broadcast.137
  10.4 11.6 %reduce.3 = bf16[2048,224]{1,0:T(8,128)(2,1)S(1)} reduce(bf16[2048,1,224]{2,1,0:T(2,128)(2,1)S(1)} %bitcast.26, bf16[]{:T(256)} %broadcast.137), dimensions={1}, to_apply=%bitcast.17.reduce_sub_computation | reduce | bytes 1835010
  22.0 1.7 reshape.97
  23.7 35.1 %all_to_all.27 = bf16[32,2,7168]{2,1,0:T(2,128)(2,1)S(1)} all-to-all(bf16[32,2,7168]{2,1,0:T(2,128)(2,1)S(1)} %reshape.97), channel_id=1, replica_groups=mesh['grp'=8,'fsdp'=32] {'fsdp'}, dimensions={0} | all-to-all | bytes 1835008 | tf_op jit(solution)/shard_map/all_to_all | solution.py:44
  58.8 2.2 reshape.98
  61.0 1.1 fusion
  62.2 77.2 %psum.7 = f32[]{:T(128)} all-reduce(f32[]{:T(128)} %fusion), channel_id=1, replica_groups=mesh['grp'=8,'fsdp'=32] {'grp','fsdp'}, use_global_device_ids=true, to_apply=%region_1.0 | all-reduce | flops 1 | bytes 8 | tf_op jit(solution)/shard_map/psum | solution.py:48
  140.1 0.1 convert_multiply_fusion
  140.3 1.2 copy.17
  141.5 2.7 mul.107
  144.1 5.4 %fusion.8 = bf16[1,64,7168]{2,1,0:T(8,128)(2,1)} fusion(f32[1,64,7168]{2,1,0:T(8,128)} %mul.107, f32[1,64,7168]{2,1,0:T(8,128)} %param.8, f32[1,64,7168]{2,1,0:T(8,128)} %param.7, f32[1,64,7168]{2,1,0:T(8,128)} %param.6), kind=kLoop, calls=%fused_computation.13 | loop fusion | flops 6881280 | bytes 8257536 | tf_op jit(solution)/shard_map/convert_element_type | solution.py:26
  149.6 0.0 all-gather.2.cloned.1.call-update
  149.6 44.2 %all-gather.2.cloned.1.call-done = bf16[8,64,7168]{2,1,0:T(8,128)(2,1)} async-done(((bf16[1,64,7168]{2,1,0:T(8,128)(2,1)}), bf16[8,64,7168]{2,1,0:T(8,128)(2,1)}) %all-gather.2.cloned.1.call-update) | async-done | bytes 7340048 | tf_op jit(solution)/shard_map/all_gather | solution.py:31
  193.8 5.7 %gather_fusion = bf16[4,64,7168]{2,1,0:T(8,128)(2,1)} fusion(bf16[8,64,7168]{2,1,0:T(8,128)(2,1)} %all-gather.2.cloned.1.call-done, s32[1024]{0:T(1024)S(1)} %pad_clamp_fusion), kind=kCustom, calls=%fused_computation | custom fusion | bytes 7340048 | tf_op jit(solution)/shard_map/jit(_take)/gather | solution.py:33
  199.5 4.3 %select_select_fusion = bf16[4,64,7168]{2,1,0:T(8,128)(2,1)} fusion(bf16[4,64,7168]{2,1,0:T(8,128)(2,1)} %gather_fusion, pred[4]{0:T(512)(128)(4,1)S(1)} %compare_and_fusion, pred[4]{0:T(512)(128)(4,1)S(1)} %and_bitcast_fusion), kind=kLoop, calls=%fused_computation.1 | loop fusion | flops 3670016 | bytes 7340040 | tf_op jit(solution)/shard_map/jit(_where)/select_n | solution.py:34
  203.9 11.2 %copy.18 = bf16[4,64,7168]{1,0,2:T(4,128)(2,1)} copy(bf16[4,64,7168]{2,1,0:T(8,128)(2,1)} %select_select_fusion) | data formatting | bytes 7340032 | tf_op jit(solution)/shard_map/jit(_where)/select_n | solution.py:34
  215.1 13.7 %reshape.99 = bf16[32,2,28672]{2,1,0:T(2,128)(2,1)} reshape(bf16[7168,4,64]{2,1,0:T(4,128)(2,1)} %bitcast.21) | data formatting | bytes 7340032
  228.8 93.9 %all_to_all.28 = bf16[32,2,28672]{2,1,0:T(2,128)(2,1)} all-to-all(bf16[32,2,28672]{2,1,0:T(2,128)(2,1)} %reshape.99), channel_id=1, replica_groups=mesh['grp'=8,'fsdp'=32] {'fsdp'}, dimensions={0} | all-to-all | bytes 7340032 | tf_op jit(solution)/shard_map/all_to_all | solution.py:38
  322.7 14.4 %reshape.100 = bf16[7168,4,64]{2,1,0:T(4,128)(2,1)} reshape(bf16[32,2,28672]{2,1,0:T(2,128)(2,1)} %all_to_all.28) | data formatting | bytes 7340032
  337.0 12.4 %copy.19 = bf16[4,64,32,224]{3,1,2,0:T(8,128)(2,1)} copy(bf16[4,64,32,224]{1,0,3,2:T(4,128)(2,1)} %bitcast.22) | data formatting | bytes 7340032 | tf_op jit(solution)/shard_map/all_to_all | solution.py:38
  349.5 6.1 %copy.20 = bf16[4,2048,224]{1,2,0:T(8,128)(2,1)} copy(bf16[4,2048,224]{2,1,0:T(8,128)(2,1)} %bitcast.25) | data formatting | bytes 7340032 | tf_op jit(solution)/shard_map/all_to_all | solution.py:38
  (6 shorter events, 0.0 us)
Async XLA Ops:
  6.5 187.3 %all-gather.2.cloned.1.call-start = ((), (), s32[]{:S(2)}) async-start(), calls=%async_computation.2 | async-start | bytes 8257536 | tf_op jit(solution)/shard_map/all_gather | solution.py:31
  144.1 5.4 %copy-start = (s32[1,4]{1,0:T(1,128)S(1)}, s32[1,4]{1,0:T(1,128)}, u32[]{:S(2)}) copy-start(s32[1,4]{1,0:T(1,128)} %param.9) | copy-start | bytes 52
Sparse Core Ops, SparseCore 0:
  149.7 44.0 all-gather.1
where the time goes:
time: 364 us; the launch traced here: 362 us
  blocking collectives  206 us (57%)
  local copies, waits for them, and re-layouts  73.5 us (20%)
  waiting for transfers between devices  44.2 us (12%)
  other arithmetic  24.3 us (7%)
  between operations  14.2 us (4%)
    all_to_all x1, blocking collectives, to_columns(): lax.all_to_all(owned_rows, 'fsdp', split_axis=2, concat_axis=1, tiled=True)  93.9 us
    psum x1, blocking collectives, body(): square_total = lax.psum(jnp.sum(grad_here * grad_here), ('grp', 'fsdp'))  77.2 us
    all_gather x1, waiting for transfers between devices, place_slots(): arrived = lax.all_gather(weights, 'grp', axis=0, tiled=True)  44.2 us
    all_to_all x1, blocking collectives, body(): lax.all_to_all(gradient.astype(jnp.bfloat16), 'fsdp', split_axis=1, conca...  35.1 us
    unnamed x7, local copies, waits for them, and re-layouts  32.6 us
    all_to_all x2, local copies, waits for them, and re-layouts, to_columns(): lax.all_to_all(owned_rows, 'fsdp', split_axis=2, concat_axis=1, tiled=True)  18.5 us
    unnamed x1, other arithmetic  11.6 us
    select_n x1, local copies, waits for them, and re-layouts, place_slots(): return jnp.where(inside[:, None, None], picked, blank_slots)  11.2 us
  transfers between devices with their start and end apart: 1, of which 1 were waited for; matrix products, arithmetic and copies ran while one was open for 0% of the time, Pallas kernels for 0%

commit v1 on v0

v1 whole, which is shorter than its diff:
```python
import functools

import jax
import jax.numpy as jnp
from jax import lax
from jax.experimental import pallas as pl
from jax.experimental.pallas import tpu as pltpu
from jax.sharding import PartitionSpec as P

D = 7168
FF = 2048


first_decay = 0.9
second_decay = 0.95
first_bias = 1.0 - 0.9**10
second_bias = 1.0 - 0.95**10
learn_rate = 0.2
shrink = 0.98
epsilon = 1e-08
stabilizer = 1e-06
clip_level = 1.0

LANES = 128
HALF = 64
VMEM_LIMIT = 48 * 1024 * 1024


def low_halves(a, b):
    return jnp.concatenate([a[:, :HALF], b[:, :HALF]], axis=1)


def high_halves(a, b):
    return jnp.concatenate([a[:, HALF:], b[:, HALF:]], axis=1)


def pack_kernel(grad_ref, block_ref, square_ref):
    step = pl.program_id(0)
    middle = grad_ref.shape[0] // 2
    squares = jnp.zeros((8, LANES), jnp.float32)
    for pair in range(grad_ref.shape[1] // LANES):
        lanes = slice(LANES * pair, LANES * (pair + 1))
        first, second = grad_ref[:middle, lanes], grad_ref[middle:, lanes]
        squares += jnp.sum((first * first + second * second).reshape(-1, 8, LANES), axis=0)
        block_ref[2 * pair] = low_halves(first, second).astype(jnp.bfloat16)
        block_ref[2 * pair + 1] = high_halves(first, second).astype(jnp.bfloat16)

    squares = jnp.sum(squares, axis=0, keepdims=True)

    @pl.when(step == 0)
    def _():
        square_ref[...] = squares

    @pl.when(step > 0)
    def _():
        square_ref[...] += squares


def pack(grad_columns):
    columns, rows = grad_columns.shape
    steps = 4
    return pl.pallas_call(
        pack_kernel,
        grid=(steps,),
        in_specs=[pl.BlockSpec((columns, rows // steps), lambda i: (0, i))],
        out_specs=[
            pl.BlockSpec((rows // HALF // steps, columns // 2, LANES), lambda i: (i, 0, 0)),
            pl.BlockSpec((1, LANES), lambda i: (0, 0)),
        ],
        out_shape=[
            jax.ShapeDtypeStruct((rows // HALF, columns // 2, LANES), jnp.bfloat16),
            jax.ShapeDtypeStruct((1, LANES), jnp.float32),
        ],
        compiler_params=pltpu.CompilerParams(vmem_limit_bytes=VMEM_LIMIT),
    )(grad_columns)


def adam_weights(gradient, master, first_moment, second_moment, factor):
    scaled = factor * gradient
    first_new = first_decay * first_moment + (1.0 - first_decay) * scaled
    second_new = second_decay * second_moment + (1.0 - second_decay) * scaled * scaled
    update = first_new / first_bias / (jnp.sqrt(second_new / second_bias) + epsilon)
    return shrink * master - learn_rate * update


def adam_kernel(entries, squares_ref, grad_ref, master_ref, first_ref, second_ref, out_ref, flat_ref):
    sources, middle = grad_ref.shape[0], grad_ref.shape[1]
    square_total = jnp.sum(squares_ref[...])
    factor = jnp.minimum(1.0, clip_level / jnp.sqrt(square_total / entries + stabilizer))
    half_sources = sources // 2
    for s in range(half_sources):
        low, high = grad_ref[s].astype(jnp.float32), grad_ref[half_sources + s].astype(jnp.float32)
        at = 2 * middle * s
        flat_ref[at : at + middle] = low_halves(low, high)
        flat_ref[at + middle : at + 2 * middle] = high_halves(low, high)
    count = flat_ref.shape[0]
    for j in range(count // LANES):
        here = slice(LANES * j, LANES * (j + 1))
        there = slice(count + LANES * j, count + LANES * (j + 1))
        both = lambda ref: jnp.concatenate([ref[:, here], ref[:, there]], axis=0)
        weights = adam_weights(flat_ref[here].T, both(master_ref), both(first_ref), both(second_ref), factor)
        flat_ref[here] = weights.T
    for s in range(half_sources):
        at = 2 * middle * s
        first, second = flat_ref[at : at + middle], flat_ref[at + middle : at + 2 * middle]
        out_ref[s] = low_halves(first, second).astype(jnp.bfloat16)
        out_ref[half_sources + s] = high_halves(first, second).astype(jnp.bfloat16)


def adam(entries, squares, grad_blocks, master, first_moment, second_moment):
    peers, middle, _ = grad_blocks.shape
    steps = 4
    state = pl.BlockSpec((HALF, D // steps), lambda i: (0, i))
    blocks = pl.BlockSpec((peers // steps, middle, LANES), lambda i: (i, 0, 0))
    return pl.pallas_call(
        functools.partial(adam_kernel, entries),
        grid=(steps,),
        in_specs=[pl.BlockSpec((1, LANES), lambda i: (0, 0)), blocks, state, state, state],
        out_specs=blocks,
        out_shape=jax.ShapeDtypeStruct(grad_blocks.shape, jnp.bfloat16),
        scratch_shapes=[pltpu.VMEM((D // steps // 2, LANES), jnp.float32)],
        compiler_params=pltpu.CompilerParams(vmem_limit_bytes=VMEM_LIMIT),
    )(squares, grad_blocks, master, first_moment, second_moment)


def place_kernel(slot_ref, block_ref, out_ref):
    live = slot_ref[pl.program_id(0)] >= 0
    middle = block_ref.shape[2]

    @pl.when(live)
    def _():
        for pair in range(block_ref.shape[1] // 2):
            lanes = slice(LANES * pair, LANES * (pair + 1))
            first = block_ref[0, 2 * pair].astype(jnp.float32)
            second = block_ref[0, 2 * pair + 1].astype(jnp.float32)
            out_ref[0, :middle, lanes] = low_halves(first, second).astype(jnp.bfloat16)
            out_ref[0, middle:, lanes] = high_halves(first, second).astype(jnp.bfloat16)

    @pl.when(jnp.logical_not(live))
    def _():
        out_ref[...] = jnp.zeros_like(out_ref)


def place(slot_ids, experts):
    n_experts, peers, middle, _ = experts.shape
    slots = slot_ids.shape[0]
    steps = 2
    return pl.pallas_call(
        place_kernel,
        grid_spec=pltpu.PrefetchScalarGridSpec(
            num_scalar_prefetch=1,
            grid=(slots, steps),
            in_specs=[
                pl.BlockSpec(
                    (1, peers // steps, middle, LANES),
                    lambda s, i, ids: (jnp.clip(ids[s], 0, n_experts - 1), i, 0, 0),
                )
            ],
            out_specs=pl.BlockSpec((1, 2 * middle, peers * HALF // steps), lambda s, i, ids: (s, 0, i)),
        ),
        out_shape=jax.ShapeDtypeStruct((slots, 2 * middle, peers * HALF), jnp.bfloat16),
        compiler_params=pltpu.CompilerParams(vmem_limit_bytes=VMEM_LIMIT),
    )(slot_ids, experts)


def total_everywhere(partial):
    for axis in ("grp", "fsdp"):
        size, apart = lax.axis_size(axis), 1
        while apart < size:
            partial += lax.ppermute(partial, axis, [(i, i ^ apart) for i in range(size)])
            apart *= 2
    return partial


def body(gradient, master, first_moment, second_moment, slot_expert):
    entries = lax.axis_size("grp") * master.shape[0] * FF * D
    slot_ids = slot_expert.reshape(-1)
    grad_blocks, squares = pack(jnp.swapaxes(gradient[0], 0, 1))
    grad_here = lax.all_to_all(grad_blocks, "fsdp", 0, 0, tiled=True)
    squares = total_everywhere(squares)
    weights = adam(entries, squares, grad_here, master[0], first_moment[0], second_moment[0])
    columns = lax.all_to_all(weights, "fsdp", 0, 0, tiled=True)
    experts = lax.all_gather(columns, "grp", axis=0, tiled=False)
    rollout = place(slot_ids, experts)
    return jnp.swapaxes(rollout, 1, 2)


def solution(mesh):
    in_specs = (
        P("grp", None, "fsdp"),
        P("grp", "fsdp", None),
        P("grp", "fsdp", None),
        P("grp", "fsdp", None),
        P("grp", None),
    )
    out_specs = P("grp", None, "fsdp")
    return jax.shard_map(body, mesh=mesh, in_specs=in_specs, out_specs=out_specs, check_vma=False)
```

time: 364 us -> 153 us (0.42)
  blocking collectives: 206 us -> 28.4 us
  local copies, waits for them, and re-layouts: 73.5 us -> 3.92 us
  starting transfers between devices: 0.01 us -> 30.1 us
  other arithmetic: 24.3 us -> 0.03 us
  waiting for transfers between devices: 44.2 us -> 63.2 us
  Pallas kernels: 0 us -> 13.6 us
    all_to_all x2 -> x1, blocking collectives: 129 us -> 28.4 us  [body(): columns = lax.all_to_all(weights, 'fsdp', 0, 0, tiled=True)]
    psum x1 -> x0, blocking collectives: 77.2 us -> none  [body(): square_total = lax.psum(jnp.sum(grad_here * grad_here), ('grp', 'fsdp'))]
    unnamed x7 -> x10, local copies, waits for them, and re-layouts: 32.6 us -> 3.92 us
    all_to_all x2 -> x0, local copies, waits for them, and re-layouts: 18.5 us -> none  [to_columns(): lax.all_to_all(owned_rows, 'fsdp', split_axis=2, concat_axis=1, tiled=True)]
    ppermute x0 -> x8, starting transfers between devices: none -> 18.2 us  [total_everywhere(): lax.ppermute(partial, axis, [(i, i ^ apart) for i in range(size)])]
    pallas_call x0 -> x3, Pallas kernels: none -> 13.6 us  [the longest x1 7.23 us: place(): pl.pallas_call(place_kernel, grid_spec=pltpu.PrefetchScalarGridSpec(num_s...]
    all_to_all x0 -> x1, starting transfers between devices: none -> 11.9 us  [body(): grad_here = lax.all_to_all(grad_blocks, 'fsdp', 0, 0, tiled=True)]
    unnamed x1 -> x0, other arithmetic: 11.6 us -> none
  transfers between devices with their start and end apart: 1 -> 10, of which waited for: 1 -> 9; matrix products, arithmetic and copies ran while one was open for 0% -> 0% of each run, Pallas kernels for 0% -> 0%
where the time goes in v1:
time: 153 us
  waiting for transfers between devices  63.2 us (41%)
  starting transfers between devices  30.1 us (20%)
  blocking collectives  28.4 us (19%)
  Pallas kernels  13.6 us (9%)
  between operations  13.5 us (9%)
  local copies, waits for them, and re-layouts  3.92 us (3%)
    all_gather x1, waiting for transfers between devices, body(): experts = lax.all_gather(columns, 'grp', axis=0, tiled=False)  51.9 us
    all_to_all x1, blocking collectives, body(): columns = lax.all_to_all(weights, 'fsdp', 0, 0, tiled=True)  28.4 us
    ppermute x8, starting transfers between devices, total_everywhere(): lax.ppermute(partial, axis, [(i, i ^ apart) for i in range(size)])  18.2 us
    all_to_all x1, starting transfers between devices, body(): grad_here = lax.all_to_all(grad_blocks, 'fsdp', 0, 0, tiled=True)  11.9 us
    ppermute x8, waiting for transfers between devices, total_everywhere(): lax.ppermute(partial, axis, [(i, i ^ apart) for i in range(size)])  11.2 us
    pallas_call x1, Pallas kernels, place(): pl.pallas_call(place_kernel, grid_spec=pltpu.PrefetchScalarGridSpec(num_s...  7.23 us
    pallas_call x1, Pallas kernels, adam(): pl.pallas_call(functools.partial(adam_kernel, entries), grid=(steps,), in...  5.63 us
    unnamed x10, local copies, waits for them, and re-layouts  3.92 us
  transfers between devices with their start and end apart: 10, of which 9 were waited for; matrix products, arithmetic and copies ran while one was open for 0% of the time, Pallas kernels for 0%

profile of v1, /device:TPU:1, one launch (start us, length us, event | category | flops | bytes accessed | tf_op | source)
XLA Modules:
  0.0 152.6 jit_solution(4436049244890781811)
XLA Ops:
  6.5 1.5 copy-done
  8.8 0.9 copy-done.3
  9.7 11.9 %all-to-all-start = ((bf16[32,112,128]{2,1,0:T(8,128)(2,1)}), bf16[32,112,128]{2,1,0:T(8,128)(2,1)S(1)}, u32[]{:S(2)}, u32[]{:S(2)}) async-start(bf16[32,112,128]{2,1,0:T(8,128)(2,1)} %copy-done.3), calls=%async_computation | async-start | bytes 1835008 | tf_op jit(solution)/shard_map/all_to_all | solution.py:179
  21.6 1.0 collective-permute-start
  22.7 0.8 collective-permute-done
  23.5 1.3 collective-permute-start.1
  24.8 1.4 collective-permute-done.1
  26.2 2.9 %collective-permute-start.2 = (f32[1,128]{1,0:T(1,128)S(1)}, f32[1,128]{1,0:T(1,128)S(1)}, u32[]{:S(2)}, u32[]{:S(2)}) collective-permute-start(f32[1,128]{1,0:T(1,128)S(1)} %add.25), channel_id=1, source_target_pairs={{0,128},{32,160},{64,192},{96,224},{128,0},{160,32},{192,64},{224,... | collective-permute-start | bytes 1544 | tf_op jit(solution)/shard_map/ppermute | solution.py:170
  29.1 1.3 collective-permute-done.2
  30.4 1.5 collective-permute-start.3
  31.9 1.2 collective-permute-done.3
  33.1 3.0 %collective-permute-start.4 = (f32[1,128]{1,0:T(1,128)S(1)}, f32[1,128]{1,0:T(1,128)S(1)}, u32[]{:S(2)}, u32[]{:S(2)}) collective-permute-start(f32[1,128]{1,0:T(1,128)S(1)} %add.27), channel_id=1, source_target_pairs={{0,2},{1,3},{2,0},{3,1},{4,6},{5,7},{6,4},{7,5},{8,10},{9,11},{10,... | collective-permute-start | bytes 1544 | tf_op jit(solution)/shard_map/ppermute | solution.py:170
  36.1 1.2 collective-permute-done.4
  37.3 1.5 collective-permute-start.5
  38.8 2.4 %collective-permute-done.5 = f32[1,128]{1,0:T(1,128)S(1)} collective-permute-done((f32[1,128]{1,0:T(1,128)S(1)}, f32[1,128]{1,0:T(1,128)S(1)}, u32[]{:S(2)}, u32[]{:S(2)}) %collective-permute-start.5) | collective-permute-done | bytes 544 | tf_op jit(solution)/shard_map/ppermute | solution.py:170
  41.2 2.2 %collective-permute-start.6 = (f32[1,128]{1,0:T(1,128)S(1)}, f32[1,128]{1,0:T(1,128)S(1)}, u32[]{:S(2)}, u32[]{:S(2)}) collective-permute-start(f32[1,128]{1,0:T(1,128)S(1)} %add.29), channel_id=1, source_target_pairs={{0,8},{1,9},{2,10},{3,11},{4,12},{5,13},{6,14},{7,15},{8,0},{9,1},... | collective-permute-start | bytes 1544 | tf_op jit(solution)/shard_map/ppermute | solution.py:170
  43.4 1.3 collective-permute-done.6
  44.8 4.8 %collective-permute-start.7 = (f32[1,128]{1,0:T(1,128)S(1)}, f32[1,128]{1,0:T(1,128)S(1)}, u32[]{:S(2)}, u32[]{:S(2)}) collective-permute-start(f32[1,128]{1,0:T(1,128)S(1)} %add.30), channel_id=1, source_target_pairs={{0,16},{1,17},{2,18},{3,19},{4,20},{5,21},{6,22},{7,23},{8,24},{9,... | collective-permute-start | bytes 1544 | tf_op jit(solution)/shard_map/ppermute | solution.py:170
  49.5 1.5 %collective-permute-done.7 = f32[1,128]{1,0:T(1,128)S(1)} collective-permute-done((f32[1,128]{1,0:T(1,128)S(1)}, f32[1,128]{1,0:T(1,128)S(1)}, u32[]{:S(2)}, u32[]{:S(2)}) %collective-permute-start.7) | collective-permute-done | bytes 544 | tf_op jit(solution)/shard_map/ppermute | solution.py:170
  51.1 1.5 copy-done.2
  52.6 5.6 %shard_map.56 = bf16[32,112,128]{2,1,0:T(8,128)(2,1)S(1)} custom-call(f32[1,128]{1,0:T(1,128)S(1)} %add.31.squares_ref, bf16[32,112,128]{2,1,0:T(8,128)(2,1)S(1)} %all-to-all-done.grad_ref, f32[64,7168]{1,0:T(8,128)S(1)} %bitcast.10, f32[64,7168]{1,0:T(8,128)S(1)} %bitcast.11, f32[64,7168]{1,0:T(8,128)} %bitcast.14), custom_call_target="tpu_custom_call" | custom-call | tf_op jit(solution)/shard_map/pallas_call | solution.py:115
  58.2 28.4 %all_to_all.10 = bf16[32,112,128]{2,1,0:T(8,128)(2,1)} all-to-all(bf16[32,112,128]{2,1,0:T(8,128)(2,1)S(1)} %shard_map.56), channel_id=1, replica_groups=mesh['grp'=8,'fsdp'=32] {'fsdp'}, dimensions={0} | all-to-all | bytes 1835008 | tf_op jit(solution)/shard_map/all_to_all | solution.py:182
  86.6 51.9 %all-gather.3.cloned.1.call-done = bf16[256,112,128]{2,1,0:T(8,128)(2,1)} async-done(((bf16[32,112,128]{2,1,0:T(8,128)(2,1)}), bf16[256,112,128]{2,1,0:T(8,128)(2,1)}) %all-gather.3.cloned.1.call-update) | async-done | bytes 7340048 | tf_op jit(solution)/shard_map/all_gather | solution.py:183
  138.6 7.2 %shard_map.57 = bf16[4,224,2048]{2,1,0:T(8,128)(2,1)} custom-call(s32[4]{0:T(128)S(1)} %bitcast.12, bf16[8,32,112,128]{3,2,1,0:T(8,128)(2,1)} %bitcast.13), custom_call_target="tpu_custom_call" | custom-call | tf_op jit(solution)/shard_map/pallas_call | solution.py:148
  (19 shorter events, 0.8 us)
Async XLA Ops:
  6.5 1.5 copy-start
  8.0 43.1 %copy-start.1 = (f32[1,64,7168]{2,1,0:T(8,128)S(1)}, f32[1,64,7168]{2,1,0:T(8,128)}, u32[]{:S(2)}) copy-start(f32[1,64,7168]{2,1,0:T(8,128)} %param.6) | copy-start | bytes 5505028
  8.8 0.9 copy-start.3
  9.7 41.4 %all-to-all-start = ((bf16[32,112,128]{2,1,0:T(8,128)(2,1)}), bf16[32,112,128]{2,1,0:T(8,128)(2,1)S(1)}, u32[]{:S(2)}, u32[]{:S(2)}) async-start(bf16[32,112,128]{2,1,0:T(8,128)(2,1)} %copy-done.3), calls=%async_computation | async-start | bytes 1835008 | tf_op jit(solution)/shard_map/all_to_all | solution.py:179
  21.6 117.0 %all-gather.3.cloned.1.call-start = ((), (), s32[]{:S(2)}) async-start(), calls=%async_computation.2 | async-start | bytes 8257536 | tf_op jit(solution)/shard_map/all_gather | solution.py:183
  21.6 1.9 %collective-permute-start = (f32[1,128]{1,0:T(1,128)S(1)}, f32[1,128]{1,0:T(1,128)S(1)}, u32[]{:S(2)}, u32[]{:S(2)}) collective-permute-start(f32[1,128]{1,0:T(1,128)S(1)} %get-tuple-element.7), channel_id=1, source_target_pairs={{0,32},{32,0},{64,96},{96,64},{128,160},{160,128},{192,224},{224,1... | collective-permute-start | bytes 1544 | tf_op jit(solution)/shard_map/ppermute | solution.py:170
  23.5 2.7 %collective-permute-start.1 = (f32[1,128]{1,0:T(1,128)S(1)}, f32[1,128]{1,0:T(1,128)S(1)}, u32[]{:S(2)}, u32[]{:S(2)}) collective-permute-start(f32[1,128]{1,0:T(1,128)S(1)} %add.24), channel_id=1, source_target_pairs={{0,64},{32,96},{64,0},{96,32},{128,192},{160,224},{192,128},{224,1... | collective-permute-start | bytes 1544 | tf_op jit(solution)/shard_map/ppermute | solution.py:170
  26.2 4.2 %collective-permute-start.2 = (f32[1,128]{1,0:T(1,128)S(1)}, f32[1,128]{1,0:T(1,128)S(1)}, u32[]{:S(2)}, u32[]{:S(2)}) collective-permute-start(f32[1,128]{1,0:T(1,128)S(1)} %add.25), channel_id=1, source_target_pairs={{0,128},{32,160},{64,192},{96,224},{128,0},{160,32},{192,64},{224,... | collective-permute-start | bytes 1544 | tf_op jit(solution)/shard_map/ppermute | solution.py:170
  30.4 2.7 %collective-permute-start.3 = (f32[1,128]{1,0:T(1,128)S(1)}, f32[1,128]{1,0:T(1,128)S(1)}, u32[]{:S(2)}, u32[]{:S(2)}) collective-permute-start(f32[1,128]{1,0:T(1,128)S(1)} %add.26), channel_id=1, source_target_pairs={{0,1},{1,0},{2,3},{3,2},{4,5},{5,4},{6,7},{7,6},{8,9},{9,8},{10,11... | collective-permute-start | bytes 1544 | tf_op jit(solution)/shard_map/ppermute | solution.py:170
  33.1 4.2 %collective-permute-start.4 = (f32[1,128]{1,0:T(1,128)S(1)}, f32[1,128]{1,0:T(1,128)S(1)}, u32[]{:S(2)}, u32[]{:S(2)}) collective-permute-start(f32[1,128]{1,0:T(1,128)S(1)} %add.27), channel_id=1, source_target_pairs={{0,2},{1,3},{2,0},{3,1},{4,6},{5,7},{6,4},{7,5},{8,10},{9,11},{10,... | collective-permute-start | bytes 1544 | tf_op jit(solution)/shard_map/ppermute | solution.py:170
  37.3 3.9 %collective-permute-start.5 = (f32[1,128]{1,0:T(1,128)S(1)}, f32[1,128]{1,0:T(1,128)S(1)}, u32[]{:S(2)}, u32[]{:S(2)}) collective-permute-start(f32[1,128]{1,0:T(1,128)S(1)} %add.28), channel_id=1, source_target_pairs={{0,4},{1,5},{2,6},{3,7},{4,0},{5,1},{6,2},{7,3},{8,12},{9,13},{10,... | collective-permute-start | bytes 1544 | tf_op jit(solution)/shard_map/ppermute | solution.py:170
  41.2 3.6 %collective-permute-start.6 = (f32[1,128]{1,0:T(1,128)S(1)}, f32[1,128]{1,0:T(1,128)S(1)}, u32[]{:S(2)}, u32[]{:S(2)}) collective-permute-start(f32[1,128]{1,0:T(1,128)S(1)} %add.29), channel_id=1, source_target_pairs={{0,8},{1,9},{2,10},{3,11},{4,12},{5,13},{6,14},{7,15},{8,0},{9,1},... | collective-permute-start | bytes 1544 | tf_op jit(solution)/shard_map/ppermute | solution.py:170
  44.8 6.3 %collective-permute-start.7 = (f32[1,128]{1,0:T(1,128)S(1)}, f32[1,128]{1,0:T(1,128)S(1)}, u32[]{:S(2)}, u32[]{:S(2)}) collective-permute-start(f32[1,128]{1,0:T(1,128)S(1)} %add.30), channel_id=1, source_target_pairs={{0,16},{1,17},{2,18},{3,19},{4,20},{5,21},{6,22},{7,23},{8,24},{9,... | collective-permute-start | bytes 1544 | tf_op jit(solution)/shard_map/ppermute | solution.py:170
  51.1 1.5 copy-start.2
  58.2 80.3 %copy-start.4 = (s32[1,4]{1,0:T(1,128)S(1)}, s32[1,4]{1,0:T(1,128)}, u32[]{:S(2)}) copy-start(s32[1,4]{1,0:T(1,128)} %param.9) | copy-start | bytes 52
Sparse Core Ops, SparseCore 0:
  86.8 51.7 all-gather.2

commit v2 on v1

--- a/solution.py
+++ b/solution.py
@@ -23,7 +23,7 @@
 
 LANES = 128
 HALF = 64
-VMEM_LIMIT = 48 * 1024 * 1024
+VMEM_LIMIT = 16 * 1024 * 1024
 
 
 def low_halves(a, b):
@@ -123,44 +123,89 @@
     )(squares, grad_blocks, master, first_moment, second_moment)
 
 
-def place_kernel(slot_ref, block_ref, out_ref):
-    live = slot_ref[pl.program_id(0)] >= 0
-    middle = block_ref.shape[2]
-
-    @pl.when(live)
-    def _():
-        for pair in range(block_ref.shape[1] // 2):
-            lanes = slice(LANES * pair, LANES * (pair + 1))
-            first = block_ref[0, 2 * pair].astype(jnp.float32)
-            second = block_ref[0, 2 * pair + 1].astype(jnp.float32)
-            out_ref[0, :middle, lanes] = low_halves(first, second).astype(jnp.bfloat16)
-            out_ref[0, middle:, lanes] = high_halves(first, second).astype(jnp.bfloat16)
-
-    @pl.when(jnp.logical_not(live))
-    def _():
-        out_ref[...] = jnp.zeros_like(out_ref)
+def unpack_kernel(block_ref, low_ref, high_ref):
+    for pair in range(block_ref.shape[0] // 2):
+        lanes = slice(LANES * pair, LANES * (pair + 1))
+        first = block_ref[2 * pair].astype(jnp.float32)
+        second = block_ref[2 * pair + 1].astype(jnp.float32)
+        low_ref[:, lanes] = low_halves(first, second).astype(jnp.bfloat16)
+        high_ref[:, lanes] = high_halves(first, second).astype(jnp.bfloat16)
+
+
+def unpack(blocks):
+    peers, middle, _ = blocks.shape
+    steps = 4
+    half = pl.BlockSpec((middle, peers * HALF // steps), lambda i: (0, i))
+    return pl.pallas_call(
+        unpack_kernel,
+        grid=(steps,),
+        in_specs=[pl.BlockSpec((peers // steps, middle, LANES), lambda i: (i, 0, 0))],
+        out_specs=[half, half],
+        out_shape=[jax.ShapeDtypeStruct((middle, peers * HALF), jnp.bfloat16)] * 2,
+        compiler_params=pltpu.CompilerParams(vmem_limit_bytes=VMEM_LIMIT),
+    )(blocks)
+
+
+def shift(array, chips):
+    size = lax.axis_size("grp")
+    return lax.ppermute(array, "grp", [(i, (i + 2 * chips) % size) for i in range(size)])
+
+
+def other_core(array):
+    return lax.ppermute(array, "grp", [(i, i ^ 1) for i in range(lax.axis_size("grp"))])
+
+
+def gather_experts(mine, onward):
+    after, before = shift(mine, -1), shift(mine, 1)
+    far = shift(before if onward > 0 else after, onward)
+    by_chip = [mine, after, far, before]
+    return [held for near in by_chip for held in (near, other_core(near))]
+
+
+def place_kernel(halves, slot_ref, *refs):
+    held, out_ref, blank_ref, sems = refs[:-3], refs[-3], refs[-2], refs[-1]
+    slots, columns = out_ref.shape[0], out_ref.shape[1] // halves
+    sources = len(held) // halves
+    me = lax.axis_index("grp")
+
+    def copy(source, slot, half):
+        target = out_ref.at[slot, pl.ds(half * columns, columns)]
+        return pltpu.make_async_copy(source, target, sems.at[slot, half])
+
+    blank_ref[...] = jnp.zeros_like(blank_ref)
+    for slot in range(slots):
+        expert = slot_ref[slot]
+        chips = (expert // 2 - me // 2 + sources // 2) % (sources // 2)
+        place = jnp.where(expert < 0, -1, 2 * chips + (expert + me) % 2)
+        for half in range(halves):
+
+            @pl.when(place < 0)
+            def _():
+                copy(blank_ref, slot, half).start()
+
+            for source in range(sources):
+
+                @pl.when(place == source)
+                def _():
+                    copy(held[half * sources + source], slot, half).start()
+
+    for slot in range(slots):
+        for half in range(halves):
+            copy(blank_ref, slot, half).wait()
 
 
 def place(slot_ids, experts):
-    n_experts, peers, middle, _ = experts.shape
-    slots = slot_ids.shape[0]
-    steps = 2
-    return pl.pallas_call(
-        place_kernel,
-        grid_spec=pltpu.PrefetchScalarGridSpec(
-            num_scalar_prefetch=1,
-            grid=(slots, steps),
-            in_specs=[
-                pl.BlockSpec(
-                    (1, peers // steps, middle, LANES),
-                    lambda s, i, ids: (jnp.clip(ids[s], 0, n_experts - 1), i, 0, 0),
-                )
-            ],
-            out_specs=pl.BlockSpec((1, 2 * middle, peers * HALF // steps), lambda s, i, ids: (s, 0, i)),
-        ),
-        out_shape=jax.ShapeDtypeStruct((slots, 2 * middle, peers * HALF), jnp.bfloat16),
-        compiler_params=pltpu.CompilerParams(vmem_limit_bytes=VMEM_LIMIT),
-    )(slot_ids, experts)
+    slots, halves = slot_ids.shape[0], len(experts)
+    columns, rows = experts[0][0].shape
+    held = [array for half in experts for array in half]
+    return pl.pallas_call(
+        functools.partial(place_kernel, halves),
+        in_specs=[pl.BlockSpec(memory_space=pltpu.SMEM)] + [pl.BlockSpec(memory_space=pl.ANY)] * len(held),
+        out_specs=pl.BlockSpec(memory_space=pl.ANY),
+        out_shape=jax.ShapeDtypeStruct((slots, halves * columns, rows), jnp.bfloat16),
+        scratch_shapes=[pltpu.VMEM((columns, rows), jnp.bfloat16), pltpu.SemaphoreType.DMA((slots, halves))],
+        compiler_params=pltpu.CompilerParams(vmem_limit_bytes=VMEM_LIMIT),
+    )(slot_ids, *held)
 
 
 def total_everywhere(partial):
@@ -180,8 +225,8 @@
     squares = total_everywhere(squares)
     weights = adam(entries, squares, grad_here, master[0], first_moment[0], second_moment[0])
     columns = lax.all_to_all(weights, "fsdp", 0, 0, tiled=True)
-    experts = lax.all_gather(columns, "grp", axis=0, tiled=False)
-    rollout = place(slot_ids, experts)
+    low, high = unpack(columns)
+    rollout = place(slot_ids, [gather_experts(low, 1), gather_experts(high, -1)])
     return jnp.swapaxes(rollout, 1, 2)
 
 

time: 153 us -> 123 us (0.80)
  waiting for transfers between devices: 63.2 us -> 18.2 us
  starting transfers between devices: 30.1 us -> 62.1 us
  between operations: 13.5 us -> 0.26 us
  Pallas kernels: 13.6 us -> 8.63 us
    all_gather x1 -> x0, waiting for transfers between devices: 51.9 us -> none  [body(): experts = lax.all_gather(columns, 'grp', axis=0, tiled=False)]
    ppermute x0 -> x14, starting transfers between devices: none -> 32 us  [the longest x8 22.8 us: other_core(): lax.ppermute(array, 'grp', [(i, i ^ 1) for i in range(lax.axis_size('grp'...]
    ppermute x0 -> x14, waiting for transfers between devices: none -> 6.89 us  [the longest x6 5.16 us: shift(): lax.ppermute(array, 'grp', [(i, (i + 2 * chips) % size) for i in range(si...]
    pallas_call x1 -> x2, Pallas kernels: 7.23 us -> 3.11 us  [the longest x1 2.49 us: place(): pl.pallas_call(functools.partial(place_kernel, halves), in_specs=[pl.Bloc...]
    unnamed x10 -> x12, local copies, waits for them, and re-layouts: 3.92 us -> 5.42 us
  transfers between devices with their start and end apart: 10 -> 23, of which waited for: 9 -> 11; matrix products, arithmetic and copies ran while one was open for 0% -> 0% of each run, Pallas kernels for 0% -> 0%
where the time goes in v2:
time: 123 us
  starting transfers between devices  62.1 us (50%)
  blocking collectives  28.1 us (23%)
  waiting for transfers between devices  18.2 us (15%)
  Pallas kernels  8.63 us (7%)
  local copies, waits for them, and re-layouts  5.42 us (4%)
    all_to_all x1, blocking collectives, body(): columns = lax.all_to_all(weights, 'fsdp', 0, 0, tiled=True)  28.1 us
    ppermute x8, starting transfers between devices, other_core(): lax.ppermute(array, 'grp', [(i, i ^ 1) for i in range(lax.axis_size('grp'...  22.8 us
    ppermute x8, starting transfers between devices, total_everywhere(): lax.ppermute(partial, axis, [(i, i ^ apart) for i in range(size)])  18.2 us
    all_to_all x1, starting transfers between devices, body(): grad_here = lax.all_to_all(grad_blocks, 'fsdp', 0, 0, tiled=True)  11.9 us
    ppermute x8, waiting for transfers between devices, total_everywhere(): lax.ppermute(partial, axis, [(i, i ^ apart) for i in range(size)])  11.3 us
    ppermute x6, starting transfers between devices, shift(): lax.ppermute(array, 'grp', [(i, (i + 2 * chips) % size) for i in range(si...  9.23 us
    unnamed x12, local copies, waits for them, and re-layouts  5.42 us
    ppermute x6, waiting for transfers between devices, shift(): lax.ppermute(array, 'grp', [(i, (i + 2 * chips) % size) for i in range(si...  5.16 us
  transfers between devices with their start and end apart: 23, of which 11 were waited for; matrix products, arithmetic and copies ran while one was open for 0% of the time, Pallas kernels for 0%

profile of v2, /device:TPU:1, one launch (start us, length us, event | category | flops | bytes accessed | tf_op | source)
XLA Modules:
  0.0 122.7 jit_solution(17622996229045167899)
XLA Ops:
  0.0 1.5 %copy-done = f32[1,2048,224]{1,2,0:T(8,128)S(1)} copy-done((f32[1,2048,224]{1,2,0:T(8,128)S(1)}, f32[1,2048,224]{1,2,0:T(8,128)}, u32[]{:S(2)}) %copy-start) | copy-done | bytes 1835032
  3.2 11.9 %all-to-all-start = ((bf16[32,112,128]{2,1,0:T(8,128)(2,1)}), bf16[32,112,128]{2,1,0:T(8,128)(2,1)S(1)}, u32[]{:S(2)}, u32[]{:S(2)}) async-start(bf16[32,112,128]{2,1,0:T(8,128)(2,1)} %copy-done.4), calls=%async_computation | async-start | bytes 1835008 | tf_op jit(solution)/shard_map/all_to_all | solution.py:224
  19.6 2.9 %collective-permute-start.2 = (f32[1,128]{1,0:T(1,128)S(1)}, f32[1,128]{1,0:T(1,128)S(1)}, u32[]{:S(2)}, u32[]{:S(2)}) collective-permute-start(f32[1,128]{1,0:T(1,128)S(1)} %add.25), channel_id=1, source_target_pairs={{0,128},{32,160},{64,192},{96,224},{128,0},{160,32},{192,64},{224,... | collective-permute-start | bytes 1544 | tf_op jit(solution)/shard_map/ppermute | solution.py:215
  23.8 1.5 %collective-permute-start.3 = (f32[1,128]{1,0:T(1,128)S(1)}, f32[1,128]{1,0:T(1,128)S(1)}, u32[]{:S(2)}, u32[]{:S(2)}) collective-permute-start(f32[1,128]{1,0:T(1,128)S(1)} %add.26), channel_id=1, source_target_pairs={{0,1},{1,0},{2,3},{3,2},{4,5},{5,4},{6,7},{7,6},{8,9},{9,8},{10,11... | collective-permute-start | bytes 1544 | tf_op jit(solution)/shard_map/ppermute | solution.py:215
  26.5 3.0 %collective-permute-start.4 = (f32[1,128]{1,0:T(1,128)S(1)}, f32[1,128]{1,0:T(1,128)S(1)}, u32[]{:S(2)}, u32[]{:S(2)}) collective-permute-start(f32[1,128]{1,0:T(1,128)S(1)} %add.27), channel_id=1, source_target_pairs={{0,2},{1,3},{2,0},{3,1},{4,6},{5,7},{6,4},{7,5},{8,10},{9,11},{10,... | collective-permute-start | bytes 1544 | tf_op jit(solution)/shard_map/ppermute | solution.py:215
  30.7 1.5 %collective-permute-start.5 = (f32[1,128]{1,0:T(1,128)S(1)}, f32[1,128]{1,0:T(1,128)S(1)}, u32[]{:S(2)}, u32[]{:S(2)}) collective-permute-start(f32[1,128]{1,0:T(1,128)S(1)} %add.28), channel_id=1, source_target_pairs={{0,4},{1,5},{2,6},{3,7},{4,0},{5,1},{6,2},{7,3},{8,12},{9,13},{10,... | collective-permute-start | bytes 1544 | tf_op jit(solution)/shard_map/ppermute | solution.py:215
  32.2 2.5 %collective-permute-done.5 = f32[1,128]{1,0:T(1,128)S(1)} collective-permute-done((f32[1,128]{1,0:T(1,128)S(1)}, f32[1,128]{1,0:T(1,128)S(1)}, u32[]{:S(2)}, u32[]{:S(2)}) %collective-permute-start.5) | collective-permute-done | bytes 544 | tf_op jit(solution)/shard_map/ppermute | solution.py:215
  34.7 2.2 %collective-permute-start.6 = (f32[1,128]{1,0:T(1,128)S(1)}, f32[1,128]{1,0:T(1,128)S(1)}, u32[]{:S(2)}, u32[]{:S(2)}) collective-permute-start(f32[1,128]{1,0:T(1,128)S(1)} %add.29), channel_id=1, source_target_pairs={{0,8},{1,9},{2,10},{3,11},{4,12},{5,13},{6,14},{7,15},{8,0},{9,1},... | collective-permute-start | bytes 1544 | tf_op jit(solution)/shard_map/ppermute | solution.py:215
  38.2 4.8 %collective-permute-start.7 = (f32[1,128]{1,0:T(1,128)S(1)}, f32[1,128]{1,0:T(1,128)S(1)}, u32[]{:S(2)}, u32[]{:S(2)}) collective-permute-start(f32[1,128]{1,0:T(1,128)S(1)} %add.30), channel_id=1, source_target_pairs={{0,16},{1,17},{2,18},{3,19},{4,20},{5,21},{6,22},{7,23},{8,24},{9,... | collective-permute-start | bytes 1544 | tf_op jit(solution)/shard_map/ppermute | solution.py:215
  43.0 1.5 %collective-permute-done.7 = f32[1,128]{1,0:T(1,128)S(1)} collective-permute-done((f32[1,128]{1,0:T(1,128)S(1)}, f32[1,128]{1,0:T(1,128)S(1)}, u32[]{:S(2)}, u32[]{:S(2)}) %collective-permute-start.7) | collective-permute-done | bytes 544 | tf_op jit(solution)/shard_map/ppermute | solution.py:215
  44.6 1.5 %copy-done.2 = f32[1,64,7168]{2,1,0:T(8,128)S(1)} copy-done((f32[1,64,7168]{2,1,0:T(8,128)S(1)}, f32[1,64,7168]{2,1,0:T(8,128)}, u32[]{:S(2)}) %copy-start.2) | copy-done | bytes 1835032
  46.1 1.5 %copy-done.3 = f32[1,64,7168]{2,1,0:T(8,128)S(1)} copy-done((f32[1,64,7168]{2,1,0:T(8,128)S(1)}, f32[1,64,7168]{2,1,0:T(8,128)}, u32[]{:S(2)}) %copy-start.3) | copy-done | bytes 1835032
  47.6 4.8 %shard_map.56 = bf16[32,112,128]{2,1,0:T(8,128)(2,1)S(1)} custom-call(f32[1,128]{1,0:T(1,128)S(1)} %add.31.squares_ref, bf16[32,112,128]{2,1,0:T(8,128)(2,1)S(1)} %all-to-all-done.grad_ref, f32[64,7168]{1,0:T(8,128)S(1)} %bitcast.9, f32[64,7168]{1,0:T(8,128)S(1)} %bitcast.10, f32[64,7168]{1,0:T(8,128)S(1)} %bitcast.11), custom_call_target="tpu_custom_call" | custom-call | tf_op jit(solution)/shard_map/pallas_call | solution.py:115
  52.4 28.1 %all_to_all.10.block_ref = bf16[32,112,128]{2,1,0:T(8,128)(2,1)S(1)} all-to-all(bf16[32,112,128]{2,1,0:T(8,128)(2,1)S(1)} %shard_map.56), channel_id=1, replica_groups=mesh['grp'=8,'fsdp'=32] {'fsdp'}, dimensions={0} | all-to-all | bytes 1835008 | tf_op jit(solution)/shard_map/all_to_all | solution.py:227
  82.5 1.5 %collective-permute-start.9 = (bf16[112,2048]{1,0:T(8,128)(2,1)S(1)}, bf16[112,2048]{1,0:T(8,128)(2,1)S(1)}, u32[]{:S(2)}, u32[]{:S(2)}) collective-permute-start(bf16[112,2048]{1,0:T(8,128)(2,1)S(1)} %get-tuple-element.11.refs_0_), channel_id=1, source_target_pairs={{0,192},{32,224},{64,0},{96,32},{128,64},{160,96},{192,128},{224,1... | collective-permute-start | bytes 1376264 | tf_op jit(solution)/shard_map/ppermute | solution.py:151
  84.0 7.8 %collective-permute-start.8 = (bf16[112,2048]{1,0:T(8,128)(2,1)S(1)}, bf16[112,2048]{1,0:T(8,128)(2,1)S(1)}, u32[]{:S(2)}, u32[]{:S(2)}) collective-permute-start(bf16[112,2048]{1,0:T(8,128)(2,1)S(1)} %get-tuple-element.11.refs_0_), channel_id=1, source_target_pairs={{0,32},{32,0},{64,96},{96,64},{128,160},{160,128},{192,224},{224,1... | collective-permute-start | bytes 1376264 | tf_op jit(solution)/shard_map/ppermute | solution.py:155
  91.8 1.5 %collective-permute-start.16 = (bf16[112,2048]{1,0:T(8,128)(2,1)S(1)}, bf16[112,2048]{1,0:T(8,128)(2,1)S(1)}, u32[]{:S(2)}, u32[]{:S(2)}) collective-permute-start(bf16[112,2048]{1,0:T(8,128)(2,1)S(1)} %get-tuple-element.12.refs_8_), channel_id=1, source_target_pairs={{0,192},{32,224},{64,0},{96,32},{128,64},{160,96},{192,128},{224,1... | collective-permute-start | bytes 1376264 | tf_op jit(solution)/shard_map/ppermute | solution.py:151
  93.3 5.5 %collective-permute-start.15 = (bf16[112,2048]{1,0:T(8,128)(2,1)S(1)}, bf16[112,2048]{1,0:T(8,128)(2,1)S(1)}, u32[]{:S(2)}, u32[]{:S(2)}) collective-permute-start(bf16[112,2048]{1,0:T(8,128)(2,1)S(1)} %get-tuple-element.12.refs_8_), channel_id=1, source_target_pairs={{0,32},{32,0},{64,96},{96,64},{128,160},{160,128},{192,224},{224,1... | collective-permute-start | bytes 1376264 | tf_op jit(solution)/shard_map/ppermute | solution.py:155
  98.8 3.5 %collective-permute-start.14 = (bf16[112,2048]{1,0:T(8,128)(2,1)S(1)}, bf16[112,2048]{1,0:T(8,128)(2,1)S(1)}, u32[]{:S(2)}, u32[]{:S(2)}) collective-permute-start(bf16[112,2048]{1,0:T(8,128)(2,1)S(1)} %collective-permute-done.11.refs_6_), channel_id=1, source_target_pairs={{0,32},{32,0},{64,96},{96,64},{128,160},{160,128},{192,224},{224,1... | collective-permute-start | bytes 1376264 | tf_op jit(solution)/shard_map/ppermute | solution.py:155
  102.3 2.5 %collective-permute-start.12 = (bf16[112,2048]{1,0:T(8,128)(2,1)S(1)}, bf16[112,2048]{1,0:T(8,128)(2,1)S(1)}, u32[]{:S(2)}, u32[]{:S(2)}) collective-permute-start(bf16[112,2048]{1,0:T(8,128)(2,1)S(1)} %collective-permute-done.11.refs_6_), channel_id=1, source_target_pairs={{0,64},{32,96},{64,128},{96,160},{128,192},{160,224},{192,0},{224,... | collective-permute-start | bytes 1376264 | tf_op jit(solution)/shard_map/ppermute | solution.py:151
  104.8 2.3 %collective-permute-start.18 = (bf16[112,2048]{1,0:T(8,128)(2,1)S(1)}, bf16[112,2048]{1,0:T(8,128)(2,1)S(1)}, u32[]{:S(2)}, u32[]{:S(2)}) collective-permute-start(bf16[112,2048]{1,0:T(8,128)(2,1)S(1)} %collective-permute-done.16.refs_10_), channel_id=1, source_target_pairs={{0,192},{32,224},{64,0},{96,32},{128,64},{160,96},{192,128},{224,1... | collective-permute-start | bytes 1376264 | tf_op jit(solution)/shard_map/ppermute | solution.py:151
  107.2 4.2 %collective-permute-start.17 = (bf16[112,2048]{1,0:T(8,128)(2,1)S(1)}, bf16[112,2048]{1,0:T(8,128)(2,1)S(1)}, u32[]{:S(2)}, u32[]{:S(2)}) collective-permute-start(bf16[112,2048]{1,0:T(8,128)(2,1)S(1)} %collective-permute-done.16.refs_10_), channel_id=1, source_target_pairs={{0,32},{32,0},{64,96},{96,64},{128,160},{160,128},{192,224},{224,1... | collective-permute-start | bytes 1376264 | tf_op jit(solution)/shard_map/ppermute | solution.py:155
  111.9 5.1 %collective-permute-done.12.refs_4_ = bf16[112,2048]{1,0:T(8,128)(2,1)S(1)} collective-permute-done((bf16[112,2048]{1,0:T(8,128)(2,1)S(1)}, bf16[112,2048]{1,0:T(8,128)(2,1)S(1)}, u32[]{:S(2)}, u32[]{:S(2)}) %collective-permute-start.12) | collective-permute-done | bytes 458784 | tf_op jit(solution)/shard_map/ppermute | solution.py:151
  120.0 2.5 %shard_map.58 = bf16[4,224,2048]{2,1,0:T(8,128)(2,1)} custom-call(s32[4]{0:T(128)S(1)} %bitcast.12, bf16[112,2048]{1,0:T(8,128)(2,1)S(1)} %get-tuple-element.11.refs_0_, bf16[112,2048]{1,0:T(8,128)(2,1)S(1)} %collective-permute-done.8.refs_1_, bf16[112,2048]{1,0:T(8,128)(2,1)S(1)} %collective-permute-done.9.refs_2_, ...), custom_call_target="tpu_custom_call" | custom-call | tf_op jit(solution)/shard_map/pallas_call | solution.py:201
  (47 shorter events, 16.9 us)
Async XLA Ops:
  3.2 41.4 %all-to-all-start = ((bf16[32,112,128]{2,1,0:T(8,128)(2,1)}), bf16[32,112,128]{2,1,0:T(8,128)(2,1)S(1)}, u32[]{:S(2)}, u32[]{:S(2)}) async-start(bf16[32,112,128]{2,1,0:T(8,128)(2,1)} %copy-done.4), calls=%async_computation | async-start | bytes 1835008 | tf_op jit(solution)/shard_map/all_to_all | solution.py:224
  15.0 1.9 %collective-permute-start = (f32[1,128]{1,0:T(1,128)S(1)}, f32[1,128]{1,0:T(1,128)S(1)}, u32[]{:S(2)}, u32[]{:S(2)}) collective-permute-start(f32[1,128]{1,0:T(1,128)S(1)} %get-tuple-element.9), channel_id=1, source_target_pairs={{0,32},{32,0},{64,96},{96,64},{128,160},{160,128},{192,224},{224,1... | collective-permute-start | bytes 1544 | tf_op jit(solution)/shard_map/ppermute | solution.py:215
  16.9 2.7 %collective-permute-start.1 = (f32[1,128]{1,0:T(1,128)S(1)}, f32[1,128]{1,0:T(1,128)S(1)}, u32[]{:S(2)}, u32[]{:S(2)}) collective-permute-start(f32[1,128]{1,0:T(1,128)S(1)} %add.24), channel_id=1, source_target_pairs={{0,64},{32,96},{64,0},{96,32},{128,192},{160,224},{192,128},{224,1... | collective-permute-start | bytes 1544 | tf_op jit(solution)/shard_map/ppermute | solution.py:215
  19.6 4.2 %collective-permute-start.2 = (f32[1,128]{1,0:T(1,128)S(1)}, f32[1,128]{1,0:T(1,128)S(1)}, u32[]{:S(2)}, u32[]{:S(2)}) collective-permute-start(f32[1,128]{1,0:T(1,128)S(1)} %add.25), channel_id=1, source_target_pairs={{0,128},{32,160},{64,192},{96,224},{128,0},{160,32},{192,64},{224,... | collective-permute-start | bytes 1544 | tf_op jit(solution)/shard_map/ppermute | solution.py:215
  23.8 2.7 %collective-permute-start.3 = (f32[1,128]{1,0:T(1,128)S(1)}, f32[1,128]{1,0:T(1,128)S(1)}, u32[]{:S(2)}, u32[]{:S(2)}) collective-permute-start(f32[1,128]{1,0:T(1,128)S(1)} %add.26), channel_id=1, source_target_pairs={{0,1},{1,0},{2,3},{3,2},{4,5},{5,4},{6,7},{7,6},{8,9},{9,8},{10,11... | collective-permute-start | bytes 1544 | tf_op jit(solution)/shard_map/ppermute | solution.py:215
  26.5 4.2 %collective-permute-start.4 = (f32[1,128]{1,0:T(1,128)S(1)}, f32[1,128]{1,0:T(1,128)S(1)}, u32[]{:S(2)}, u32[]{:S(2)}) collective-permute-start(f32[1,128]{1,0:T(1,128)S(1)} %add.27), channel_id=1, source_target_pairs={{0,2},{1,3},{2,0},{3,1},{4,6},{5,7},{6,4},{7,5},{8,10},{9,11},{10,... | collective-permute-start | bytes 1544 | tf_op jit(solution)/shard_map/ppermute | solution.py:215
  30.7 3.9 %collective-permute-start.5 = (f32[1,128]{1,0:T(1,128)S(1)}, f32[1,128]{1,0:T(1,128)S(1)}, u32[]{:S(2)}, u32[]{:S(2)}) collective-permute-start(f32[1,128]{1,0:T(1,128)S(1)} %add.28), channel_id=1, source_target_pairs={{0,4},{1,5},{2,6},{3,7},{4,0},{5,1},{6,2},{7,3},{8,12},{9,13},{10,... | collective-permute-start | bytes 1544 | tf_op jit(solution)/shard_map/ppermute | solution.py:215
  34.7 3.6 %collective-permute-start.6 = (f32[1,128]{1,0:T(1,128)S(1)}, f32[1,128]{1,0:T(1,128)S(1)}, u32[]{:S(2)}, u32[]{:S(2)}) collective-permute-start(f32[1,128]{1,0:T(1,128)S(1)} %add.29), channel_id=1, source_target_pairs={{0,8},{1,9},{2,10},{3,11},{4,12},{5,13},{6,14},{7,15},{8,0},{9,1},... | collective-permute-start | bytes 1544 | tf_op jit(solution)/shard_map/ppermute | solution.py:215
  38.2 6.3 %collective-permute-start.7 = (f32[1,128]{1,0:T(1,128)S(1)}, f32[1,128]{1,0:T(1,128)S(1)}, u32[]{:S(2)}, u32[]{:S(2)}) collective-permute-start(f32[1,128]{1,0:T(1,128)S(1)} %add.30), channel_id=1, source_target_pairs={{0,16},{1,17},{2,18},{3,19},{4,20},{5,21},{6,22},{7,23},{8,24},{9,... | collective-permute-start | bytes 1544 | tf_op jit(solution)/shard_map/ppermute | solution.py:215
  52.4 67.7 %copy-start.5 = (s32[1,4]{1,0:T(1,128)S(1)}, s32[1,4]{1,0:T(1,128)}, u32[]{:S(2)}) copy-start(s32[1,4]{1,0:T(1,128)} %param.9) | copy-start | bytes 52
  81.1 12.3 %collective-permute-start.11 = (bf16[112,2048]{1,0:T(8,128)(2,1)S(1)}, bf16[112,2048]{1,0:T(8,128)(2,1)S(1)}, u32[]{:S(2)}, u32[]{:S(2)}) collective-permute-start(bf16[112,2048]{1,0:T(8,128)(2,1)S(1)} %get-tuple-element.11.refs_0_), channel_id=1, source_target_pairs={{0,64},{32,96},{64,128},{96,160},{128,192},{160,224},{192,0},{224,... | collective-permute-start | bytes 1376264 | tf_op jit(solution)/shard_map/ppermute | solution.py:151
  82.5 16.4 %collective-permute-start.9 = (bf16[112,2048]{1,0:T(8,128)(2,1)S(1)}, bf16[112,2048]{1,0:T(8,128)(2,1)S(1)}, u32[]{:S(2)}, u32[]{:S(2)}) collective-permute-start(bf16[112,2048]{1,0:T(8,128)(2,1)S(1)} %get-tuple-element.11.refs_0_), channel_id=1, source_target_pairs={{0,192},{32,224},{64,0},{96,32},{128,64},{160,96},{192,128},{224,1... | collective-permute-start | bytes 1376264 | tf_op jit(solution)/shard_map/ppermute | solution.py:151
  84.0 18.3 %collective-permute-start.8 = (bf16[112,2048]{1,0:T(8,128)(2,1)S(1)}, bf16[112,2048]{1,0:T(8,128)(2,1)S(1)}, u32[]{:S(2)}, u32[]{:S(2)}) collective-permute-start(bf16[112,2048]{1,0:T(8,128)(2,1)S(1)} %get-tuple-element.11.refs_0_), channel_id=1, source_target_pairs={{0,32},{32,0},{64,96},{96,64},{128,160},{160,128},{192,224},{224,1... | collective-permute-start | bytes 1376264 | tf_op jit(solution)/shard_map/ppermute | solution.py:155
  91.8 13.0 %collective-permute-start.16 = (bf16[112,2048]{1,0:T(8,128)(2,1)S(1)}, bf16[112,2048]{1,0:T(8,128)(2,1)S(1)}, u32[]{:S(2)}, u32[]{:S(2)}) collective-permute-start(bf16[112,2048]{1,0:T(8,128)(2,1)S(1)} %get-tuple-element.12.refs_8_), channel_id=1, source_target_pairs={{0,192},{32,224},{64,0},{96,32},{128,64},{160,96},{192,128},{224,1... | collective-permute-start | bytes 1376264 | tf_op jit(solution)/shard_map/ppermute | solution.py:151
  93.3 13.8 %collective-permute-start.20 = (bf16[112,2048]{1,0:T(8,128)(2,1)S(1)}, bf16[112,2048]{1,0:T(8,128)(2,1)S(1)}, u32[]{:S(2)}, u32[]{:S(2)}) collective-permute-start(bf16[112,2048]{1,0:T(8,128)(2,1)S(1)} %get-tuple-element.12.refs_8_), channel_id=1, source_target_pairs={{0,64},{32,96},{64,128},{96,160},{128,192},{160,224},{192,0},{224,... | collective-permute-start | bytes 1376264 | tf_op jit(solution)/shard_map/ppermute | solution.py:151
  93.3 18.0 %collective-permute-start.15 = (bf16[112,2048]{1,0:T(8,128)(2,1)S(1)}, bf16[112,2048]{1,0:T(8,128)(2,1)S(1)}, u32[]{:S(2)}, u32[]{:S(2)}) collective-permute-start(bf16[112,2048]{1,0:T(8,128)(2,1)S(1)} %get-tuple-element.12.refs_8_), channel_id=1, source_target_pairs={{0,32},{32,0},{64,96},{96,64},{128,160},{160,128},{192,224},{224,1... | collective-permute-start | bytes 1376264 | tf_op jit(solution)/shard_map/ppermute | solution.py:155
  98.8 12.6 %collective-permute-start.14 = (bf16[112,2048]{1,0:T(8,128)(2,1)S(1)}, bf16[112,2048]{1,0:T(8,128)(2,1)S(1)}, u32[]{:S(2)}, u32[]{:S(2)}) collective-permute-start(bf16[112,2048]{1,0:T(8,128)(2,1)S(1)} %collective-permute-done.11.refs_6_), channel_id=1, source_target_pairs={{0,32},{32,0},{64,96},{96,64},{128,160},{160,128},{192,224},{224,1... | collective-permute-start | bytes 1376264 | tf_op jit(solution)/shard_map/ppermute | solution.py:155
  102.3 14.7 %collective-permute-start.12 = (bf16[112,2048]{1,0:T(8,128)(2,1)S(1)}, bf16[112,2048]{1,0:T(8,128)(2,1)S(1)}, u32[]{:S(2)}, u32[]{:S(2)}) collective-permute-start(bf16[112,2048]{1,0:T(8,128)(2,1)S(1)} %collective-permute-done.11.refs_6_), channel_id=1, source_target_pairs={{0,64},{32,96},{64,128},{96,160},{128,192},{160,224},{192,0},{224,... | collective-permute-start | bytes 1376264 | tf_op jit(solution)/shard_map/ppermute | solution.py:151
  104.8 13.1 %collective-permute-start.18 = (bf16[112,2048]{1,0:T(8,128)(2,1)S(1)}, bf16[112,2048]{1,0:T(8,128)(2,1)S(1)}, u32[]{:S(2)}, u32[]{:S(2)}) collective-permute-start(bf16[112,2048]{1,0:T(8,128)(2,1)S(1)} %collective-permute-done.16.refs_10_), channel_id=1, source_target_pairs={{0,192},{32,224},{64,0},{96,32},{128,64},{160,96},{192,128},{224,1... | collective-permute-start | bytes 1376264 | tf_op jit(solution)/shard_map/ppermute | solution.py:151
  107.2 11.2 %collective-permute-start.17 = (bf16[112,2048]{1,0:T(8,128)(2,1)S(1)}, bf16[112,2048]{1,0:T(8,128)(2,1)S(1)}, u32[]{:S(2)}, u32[]{:S(2)}) collective-permute-start(bf16[112,2048]{1,0:T(8,128)(2,1)S(1)} %collective-permute-done.16.refs_10_), channel_id=1, source_target_pairs={{0,32},{32,0},{64,96},{96,64},{128,160},{160,128},{192,224},{224,1... | collective-permute-start | bytes 1376264 | tf_op jit(solution)/shard_map/ppermute | solution.py:155
  111.3 7.0 %collective-permute-start.10 = (bf16[112,2048]{1,0:T(8,128)(2,1)S(1)}, bf16[112,2048]{1,0:T(8,128)(2,1)S(1)}, u32[]{:S(2)}, u32[]{:S(2)}) collective-permute-start(bf16[112,2048]{1,0:T(8,128)(2,1)S(1)} %collective-permute-done.9.refs_2_), channel_id=1, source_target_pairs={{0,32},{32,0},{64,96},{96,64},{128,160},{160,128},{192,224},{224,1... | collective-permute-start | bytes 1376264 | tf_op jit(solution)/shard_map/ppermute | solution.py:155
  111.4 6.9 %collective-permute-start.21 = (bf16[112,2048]{1,0:T(8,128)(2,1)S(1)}, bf16[112,2048]{1,0:T(8,128)(2,1)S(1)}, u32[]{:S(2)}, u32[]{:S(2)}) collective-permute-start(bf16[112,2048]{1,0:T(8,128)(2,1)S(1)} %collective-permute-done.20.refs_14_), channel_id=1, source_target_pairs={{0,32},{32,0},{64,96},{96,64},{128,160},{160,128},{192,224},{224,1... | collective-permute-start | bytes 1376264 | tf_op jit(solution)/shard_map/ppermute | solution.py:155
  117.0 2.4 %collective-permute-start.13 = (bf16[112,2048]{1,0:T(8,128)(2,1)S(1)}, bf16[112,2048]{1,0:T(8,128)(2,1)S(1)}, u32[]{:S(2)}, u32[]{:S(2)}) collective-permute-start(bf16[112,2048]{1,0:T(8,128)(2,1)S(1)} %collective-permute-done.12.refs_4_), channel_id=1, source_target_pairs={{0,32},{32,0},{64,96},{96,64},{128,160},{160,128},{192,224},{224,1... | collective-permute-start | bytes 1376264 | tf_op jit(solution)/shard_map/ppermute | solution.py:155
  117.9 2.1 %collective-permute-start.19 = (bf16[112,2048]{1,0:T(8,128)(2,1)S(1)}, bf16[112,2048]{1,0:T(8,128)(2,1)S(1)}, u32[]{:S(2)}, u32[]{:S(2)}) collective-permute-start(bf16[112,2048]{1,0:T(8,128)(2,1)S(1)} %collective-permute-done.18.refs_12_), channel_id=1, source_target_pairs={{0,32},{32,0},{64,96},{96,64},{128,160},{160,128},{192,224},{224,1... | collective-permute-start | bytes 1376264 | tf_op jit(solution)/shard_map/ppermute | solution.py:155
  (5 other events, 48.5 us)

commit v3 on v2

--- a/solution.py
+++ b/solution.py
@@ -23,6 +23,8 @@
 
 LANES = 128
 HALF = 64
+CHUNKS = 4
+EXCHANGES = (("grp", 1, 2), ("grp", 2, 4), ("fsdp", 1, 4), ("fsdp", 4, 4), ("fsdp", 16, 2))
 VMEM_LIMIT = 16 * 1024 * 1024
 
 
@@ -34,45 +36,81 @@
     return jnp.concatenate([a[:, HALF:], b[:, HALF:]], axis=1)
 
 
-def pack_kernel(grad_ref, block_ref, square_ref):
-    step = pl.program_id(0)
-    middle = grad_ref.shape[0] // 2
+def pack_kernel(grad_hbm, block_hbm, square_ref, grad_ref, block_ref, in_sems, out_sems):
+    steps, columns, rows = in_sems.shape[0], grad_hbm.shape[0], grad_hbm.shape[1]
+    middle, width, owners = columns // 2, rows // steps, rows // steps // HALF
+    arrive, leave = [], []
+    for i in range(steps):
+        lanes, blocks = pl.ds(i * width, width), pl.ds(i * owners, owners)
+        arrive.append(pltpu.make_async_copy(grad_hbm.at[:, lanes], grad_ref.at[:, lanes], in_sems.at[i]))
+        leave.append(pltpu.make_async_copy(block_ref.at[blocks], block_hbm.at[blocks], out_sems.at[i]))
+        arrive[i].start()
     squares = jnp.zeros((8, LANES), jnp.float32)
-    for pair in range(grad_ref.shape[1] // LANES):
-        lanes = slice(LANES * pair, LANES * (pair + 1))
-        first, second = grad_ref[:middle, lanes], grad_ref[middle:, lanes]
-        squares += jnp.sum((first * first + second * second).reshape(-1, 8, LANES), axis=0)
-        block_ref[2 * pair] = low_halves(first, second).astype(jnp.bfloat16)
-        block_ref[2 * pair + 1] = high_halves(first, second).astype(jnp.bfloat16)
-
-    squares = jnp.sum(squares, axis=0, keepdims=True)
-
-    @pl.when(step == 0)
-    def _():
-        square_ref[...] = squares
-
-    @pl.when(step > 0)
-    def _():
-        square_ref[...] += squares
+    for i in range(steps):
+        arrive[i].wait()
+        for pair in range(i * owners // 2, (i + 1) * owners // 2):
+            lanes = slice(LANES * pair, LANES * (pair + 1))
+            first, second = grad_ref[:middle, lanes], grad_ref[middle:, lanes]
+            squares += jnp.sum((first * first + second * second).reshape(-1, 8, LANES), axis=0)
+            block_ref[2 * pair] = low_halves(first, second).astype(jnp.bfloat16)
+            block_ref[2 * pair + 1] = high_halves(first, second).astype(jnp.bfloat16)
+        leave[i].start()
+    square_ref[...] = jnp.sum(squares, axis=0, keepdims=True)
+    for copy in leave:
+        copy.wait()
 
 
 def pack(grad_columns):
     columns, rows = grad_columns.shape
     steps = 4
+    block = (rows // HALF, columns // 2, LANES)
+    far = pl.BlockSpec(memory_space=pltpu.HBM)
     return pl.pallas_call(
         pack_kernel,
-        grid=(steps,),
-        in_specs=[pl.BlockSpec((columns, rows // steps), lambda i: (0, i))],
-        out_specs=[
-            pl.BlockSpec((rows // HALF // steps, columns // 2, LANES), lambda i: (i, 0, 0)),
-            pl.BlockSpec((1, LANES), lambda i: (0, 0)),
+        in_specs=[far],
+        out_specs=[far, pl.BlockSpec(memory_space=pltpu.VMEM)],
+        out_shape=[jax.ShapeDtypeStruct(block, jnp.bfloat16), jax.ShapeDtypeStruct((1, LANES), jnp.float32)],
+        scratch_shapes=[
+            pltpu.VMEM((columns, rows), jnp.float32),
+            pltpu.VMEM(block, jnp.bfloat16),
+            pltpu.SemaphoreType.DMA((steps,)),
+            pltpu.SemaphoreType.DMA((steps,)),
         ],
-        out_shape=[
-            jax.ShapeDtypeStruct((rows // HALF, columns // 2, LANES), jnp.bfloat16),
-            jax.ShapeDtypeStruct((1, LANES), jnp.float32),
-        ],
-        compiler_params=pltpu.CompilerParams(vmem_limit_bytes=VMEM_LIMIT),
-    )(grad_columns)
+        compiler_params=pltpu.CompilerParams(vmem_limit_bytes=VMEM_LIMIT),
+    )(pltpu.with_memory_space_constraint(grad_columns, pltpu.HBM))
+
+
+def turn_kernel(grad_ref, master_hbm, first_hbm, second_hbm, turned_ref, master_ref, first_ref, second_ref, flat_ref, sems):
+    held = ((master_hbm, master_ref), (first_hbm, first_ref), (second_hbm, second_ref))
+    copies = [pltpu.make_async_copy(source, target, sems.at[k]) for k, (source, target) in enumerate(held)]
+    for copy in copies:
+        copy.start()
+    middle, sources = grad_ref.shape[1], grad_ref.shape[0] // CHUNKS
+    squares = turned_ref.shape[0] // CHUNKS
+    for i in range(CHUNKS):
+        for s in range(sources // 2):
+            low = grad_ref[sources * i + s].astype(jnp.float32)
+            high = grad_ref[sources * i + sources // 2 + s].astype(jnp.float32)
+            at = 2 * middle * s
+            flat_ref[at : at + middle] = low_halves(low, high)
+            flat_ref[at + middle : at + 2 * middle] = high_halves(low, high)
+        for j in range(squares):
+            turned_ref[squares * i + j] = flat_ref[LANES * j : LANES * (j + 1)].T
+    for copy in copies:
+        copy.wait()
+
+
+def turn(grad_blocks, *states):
+    near, far = pl.BlockSpec(memory_space=pltpu.VMEM), pl.BlockSpec(memory_space=pltpu.HBM)
+    state = jax.ShapeDtypeStruct(states[0].shape, jnp.float32)
+    return pl.pallas_call(
+        turn_kernel,
+        in_specs=[near, far, far, far],
+        out_specs=[near] * 4,
+        out_shape=[jax.ShapeDtypeStruct((D // LANES // 2, LANES, LANES), jnp.float32)] + [state] * 3,
+        scratch_shapes=[pltpu.VMEM((D // CHUNKS // 2, LANES), jnp.float32), pltpu.SemaphoreType.DMA((3,))],
+        compiler_params=pltpu.CompilerParams(vmem_limit_bytes=VMEM_LIMIT),
+    )(grad_blocks, *[pltpu.with_memory_space_constraint(a, pltpu.HBM) for a in states])
 
 
 def adam_weights(gradient, master, first_moment, second_moment, factor):
@@ -83,44 +121,37 @@
     return shrink * master - learn_rate * update
 
 
-def adam_kernel(entries, squares_ref, grad_ref, master_ref, first_ref, second_ref, out_ref, flat_ref):
-    sources, middle = grad_ref.shape[0], grad_ref.shape[1]
+def adam_kernel(entries, squares_ref, turned_ref, master_ref, first_ref, second_ref, out_ref, flat_ref):
     square_total = jnp.sum(squares_ref[...])
     factor = jnp.minimum(1.0, clip_level / jnp.sqrt(square_total / entries + stabilizer))
-    half_sources = sources // 2
-    for s in range(half_sources):
-        low, high = grad_ref[s].astype(jnp.float32), grad_ref[half_sources + s].astype(jnp.float32)
-        at = 2 * middle * s
-        flat_ref[at : at + middle] = low_halves(low, high)
-        flat_ref[at + middle : at + 2 * middle] = high_halves(low, high)
-    count = flat_ref.shape[0]
-    for j in range(count // LANES):
-        here = slice(LANES * j, LANES * (j + 1))
-        there = slice(count + LANES * j, count + LANES * (j + 1))
-        both = lambda ref: jnp.concatenate([ref[:, here], ref[:, there]], axis=0)
-        weights = adam_weights(flat_ref[here].T, both(master_ref), both(first_ref), both(second_ref), factor)
-        flat_ref[here] = weights.T
-    for s in range(half_sources):
-        at = 2 * middle * s
-        first, second = flat_ref[at : at + middle], flat_ref[at + middle : at + 2 * middle]
-        out_ref[s] = low_halves(first, second).astype(jnp.bfloat16)
-        out_ref[half_sources + s] = high_halves(first, second).astype(jnp.bfloat16)
-
-
-def adam(entries, squares, grad_blocks, master, first_moment, second_moment):
-    peers, middle, _ = grad_blocks.shape
-    steps = 4
-    state = pl.BlockSpec((HALF, D // steps), lambda i: (0, i))
-    blocks = pl.BlockSpec((peers // steps, middle, LANES), lambda i: (i, 0, 0))
+    sources, middle = out_ref.shape[0] // CHUNKS, out_ref.shape[1]
+    width, squares = D // CHUNKS, turned_ref.shape[0] // CHUNKS
+    for i in range(CHUNKS):
+        for j in range(squares):
+            at = width * i + LANES * j
+            beyond = at + width // 2
+            both = lambda ref: jnp.concatenate([ref[:, at : at + LANES], ref[:, beyond : beyond + LANES]], axis=0)
+            gradient = turned_ref[squares * i + j]
+            weights = adam_weights(gradient, both(master_ref), both(first_ref), both(second_ref), factor)
+            flat_ref[LANES * j : LANES * (j + 1)] = weights.T
+        for s in range(sources // 2):
+            at = 2 * middle * s
+            first, second = flat_ref[at : at + middle], flat_ref[at + middle : at + 2 * middle]
+            out_ref[sources * i + s] = low_halves(first, second).astype(jnp.bfloat16)
+            out_ref[sources * i + sources // 2 + s] = high_halves(first, second).astype(jnp.bfloat16)
+
+
+def adam(entries, squares, turned, *states):
+    near = pl.BlockSpec(memory_space=pltpu.VMEM)
+    rows, columns = states[0].shape
     return pl.pallas_call(
         functools.partial(adam_kernel, entries),
-        grid=(steps,),
-        in_specs=[pl.BlockSpec((1, LANES), lambda i: (0, 0)), blocks, state, state, state],
-        out_specs=blocks,
-        out_shape=jax.ShapeDtypeStruct(grad_blocks.shape, jnp.bfloat16),
-        scratch_shapes=[pltpu.VMEM((D // steps // 2, LANES), jnp.float32)],
-        compiler_params=pltpu.CompilerParams(vmem_limit_bytes=VMEM_LIMIT),
-    )(squares, grad_blocks, master, first_moment, second_moment)
+        in_specs=[near] * 5,
+        out_specs=near,
+        out_shape=jax.ShapeDtypeStruct((FF // rows, columns * rows // FF // 2, LANES), jnp.bfloat16),
+        scratch_shapes=[pltpu.VMEM((D // CHUNKS // 2, LANES), jnp.float32)],
+        compiler_params=pltpu.CompilerParams(vmem_limit_bytes=VMEM_LIMIT),
+    )(squares, turned, *states)
 
 
 def unpack_kernel(block_ref, low_ref, high_ref):
@@ -208,13 +239,10 @@
     )(slot_ids, *held)
 
 
-def total_everywhere(partial):
-    for axis in ("grp", "fsdp"):
-        size, apart = lax.axis_size(axis), 1
-        while apart < size:
-            partial += lax.ppermute(partial, axis, [(i, i ^ apart) for i in range(size)])
-            apart *= 2
-    return partial
+def total_over(partial, axis, apart, radix):
+    size = lax.axis_size(axis)
+    others = [lax.ppermute(partial, axis, [(i, i ^ (apart * k)) for i in range(size)]) for k in range(1, radix)]
+    return sum(others, partial)
 
 
 def body(gradient, master, first_moment, second_moment, slot_expert):
@@ -222,8 +250,14 @@
     slot_ids = slot_expert.reshape(-1)
     grad_blocks, squares = pack(jnp.swapaxes(gradient[0], 0, 1))
     grad_here = lax.all_to_all(grad_blocks, "fsdp", 0, 0, tiled=True)
-    squares = total_everywhere(squares)
-    weights = adam(entries, squares, grad_here, master[0], first_moment[0], second_moment[0])
+    for axis, apart, radix in EXCHANGES[:-1]:
+        squares = total_over(squares, axis, apart, radix)
+    turned, *states = turn(grad_here, master[0], first_moment[0], second_moment[0])
+    axis, apart, _ = EXCHANGES[-1]
+    others = lax.ppermute(squares, axis, [(i, i ^ apart) for i in range(lax.axis_size(axis))])
+    others, turned = lax.optimization_barrier((others, turned))
+    squares = squares + others
+    weights = adam(entries, squares, turned, *states)
     columns = lax.all_to_all(weights, "fsdp", 0, 0, tiled=True)
     low, high = unpack(columns)
     rollout = place(slot_ids, [gather_experts(low, 1), gather_experts(high, -1)])

time: 123 us -> 113 us (0.919)
  local copies, waits for them, and re-layouts: 5.42 us -> 0.01 us
  starting transfers between devices: 62.1 us -> 59 us
  blocking collectives: 28.1 us -> 25.6 us
  Pallas kernels: 8.63 us -> 10.1 us
    unnamed x12 -> x2, local copies, waits for them, and re-layouts: 5.42 us -> 0.01 us
    ppermute x8 -> x11, starting transfers between devices: 18.2 us -> 15.2 us  [the longest x10 11.5 us: total_over(): lax.ppermute(partial, axis, [(i, i ^ apart * k) for i in range(size)])]
    all_to_all x1, blocking collectives: 28.1 us -> 25.6 us  [body(): columns = lax.all_to_all(weights, 'fsdp', 0, 0, tiled=True)]
    ppermute x8, starting transfers between devices: 22.8 us -> 20.7 us  [other_core(): lax.ppermute(array, 'grp', [(i, i ^ 1) for i in range(lax.axis_size('grp'...]
    ppermute x6, starting transfers between devices: 9.23 us -> 11.1 us  [shift(): lax.ppermute(array, 'grp', [(i, (i + 2 * chips) % size) for i in range(si...]
    pallas_call x2 -> x3, Pallas kernels: 5.52 us -> 7.04 us  [the longest x1 2.63 us: turn(): pl.pallas_call(turn_kernel, in_specs=[near, far, far, far], out_specs=[ne...]
    ppermute x8 -> x11, waiting for transfers between devices: 11.3 us -> 11 us  [the longest x10 11 us: total_over(): lax.ppermute(partial, axis, [(i, i ^ apart * k) for i in range(size)])]
  transfers between devices with their start and end apart: 23 -> 26, of which waited for: 11 -> 10; matrix products, arithmetic and copies ran while one was open for 0% -> 0% of each run, Pallas kernels for 0% -> 2%
where the time goes in v3:
time: 113 us
  starting transfers between devices  59 us (52%)
  blocking collectives  25.6 us (23%)
  waiting for transfers between devices  17.9 us (16%)
  Pallas kernels  10.1 us (9%)
    all_to_all x1, blocking collectives, body(): columns = lax.all_to_all(weights, 'fsdp', 0, 0, tiled=True)  25.6 us
    ppermute x8, starting transfers between devices, other_core(): lax.ppermute(array, 'grp', [(i, i ^ 1) for i in range(lax.axis_size('grp'...  20.7 us
    all_to_all x1, starting transfers between devices, body(): grad_here = lax.all_to_all(grad_blocks, 'fsdp', 0, 0, tiled=True)  11.9 us
    ppermute x10, starting transfers between devices, total_over(): lax.ppermute(partial, axis, [(i, i ^ apart * k) for i in range(size)])  11.5 us
    ppermute x6, starting transfers between devices, shift(): lax.ppermute(array, 'grp', [(i, (i + 2 * chips) % size) for i in range(si...  11.1 us
    ppermute x10, waiting for transfers between devices, total_over(): lax.ppermute(partial, axis, [(i, i ^ apart * k) for i in range(size)])  11 us
    ppermute x6, waiting for transfers between devices, shift(): lax.ppermute(array, 'grp', [(i, (i + 2 * chips) % size) for i in range(si...  5.27 us
    ppermute x1, starting transfers between devices, body(): lax.ppermute(squares, axis, [(i, i ^ apart) for i in range(lax.axis_size(...  3.75 us
  transfers between devices with their start and end apart: 26, of which 10 were waited for; matrix products, arithmetic and copies ran while one was open for 0% of the time, Pallas kernels for 2%

profile of v3, /device:TPU:1, one launch (start us, length us, event | category | flops | bytes accessed | tf_op | source)
XLA Modules:
  0.0 112.9 jit_solution(6585549562635669281)
XLA Ops:
  0.0 2.3 %shard_map.55 = (bf16[32,112,128]{2,1,0:T(8,128)(2,1)}, f32[1,128]{1,0:T(1,128)S(1)}) custom-call(f32[224,2048]{1,0:T(8,128)} %bitcast.9), custom_call_target="tpu_custom_call" | custom-call | tf_op jit(solution)/shard_map/pallas_call | solution.py:68
  2.3 11.9 %all-to-all-start = ((bf16[32,112,128]{2,1,0:T(8,128)(2,1)}), bf16[32,112,128]{2,1,0:T(8,128)(2,1)S(1)}, u32[]{:S(2)}, u32[]{:S(2)}) async-start(bf16[32,112,128]{2,1,0:T(8,128)(2,1)} %get-tuple-element.16), calls=%async_computation | async-start | bytes 1835008 | tf_op jit(solution)/shard_map/all_to_all | solution.py:252
  14.2 1.0 collective-permute-start
  16.1 2.7 %collective-permute-start.3 = (f32[1,128]{1,0:T(1,128)S(1)}, f32[1,128]{1,0:T(1,128)S(1)}, u32[]{:S(2)}, u32[]{:S(2)}) collective-permute-start(f32[1,128]{1,0:T(1,128)S(1)} %add.33), channel_id=1, source_target_pairs={{0,192},{32,224},{64,128},{96,160},{128,64},{160,96},{192,0},{224,... | collective-permute-start | bytes 1544 | tf_op jit(solution)/shard_map/ppermute | solution.py:244
  20.0 3.0 %collective-permute-done.2 = f32[1,128]{1,0:T(1,128)S(1)} collective-permute-done((f32[1,128]{1,0:T(1,128)S(1)}, f32[1,128]{1,0:T(1,128)S(1)}, u32[]{:S(2)}, u32[]{:S(2)}) %collective-permute-start.2) | collective-permute-done | bytes 544 | tf_op jit(solution)/shard_map/ppermute | solution.py:244
  23.0 2.8 %collective-permute-start.6 = (f32[1,128]{1,0:T(1,128)S(1)}, f32[1,128]{1,0:T(1,128)S(1)}, u32[]{:S(2)}, u32[]{:S(2)}) collective-permute-start(f32[1,128]{1,0:T(1,128)S(1)} %add_add_fusion.2), channel_id=1, source_target_pairs={{0,3},{1,2},{2,1},{3,0},{4,7},{5,6},{6,5},{7,4},{8,11},{9,10},{10,... | collective-permute-start | bytes 1544 | tf_op jit(solution)/shard_map/ppermute | solution.py:244
  27.1 3.0 %collective-permute-done.5 = f32[1,128]{1,0:T(1,128)S(1)} collective-permute-done((f32[1,128]{1,0:T(1,128)S(1)}, f32[1,128]{1,0:T(1,128)S(1)}, u32[]{:S(2)}, u32[]{:S(2)}) %collective-permute-start.5) | collective-permute-done | bytes 544 | tf_op jit(solution)/shard_map/ppermute | solution.py:244
  30.0 3.1 %collective-permute-start.9 = (f32[1,128]{1,0:T(1,128)S(1)}, f32[1,128]{1,0:T(1,128)S(1)}, u32[]{:S(2)}, u32[]{:S(2)}) collective-permute-start(f32[1,128]{1,0:T(1,128)S(1)} %add_add_fusion.1), channel_id=1, source_target_pairs={{0,12},{1,13},{2,14},{3,15},{4,8},{5,9},{6,10},{7,11},{8,4},{9,5},... | collective-permute-start | bytes 1544 | tf_op jit(solution)/shard_map/ppermute | solution.py:244
  34.4 2.3 %collective-permute-done.8 = f32[1,128]{1,0:T(1,128)S(1)} collective-permute-done((f32[1,128]{1,0:T(1,128)S(1)}, f32[1,128]{1,0:T(1,128)S(1)}, u32[]{:S(2)}, u32[]{:S(2)}) %collective-permute-start.8) | collective-permute-done | bytes 544 | tf_op jit(solution)/shard_map/ppermute | solution.py:244
  36.7 3.8 %collective-permute-start.10 = (f32[1,128]{1,0:T(1,128)S(1)}, f32[1,128]{1,0:T(1,128)S(1)}, u32[]{:S(2)}, u32[]{:S(2)}) collective-permute-start(f32[1,128]{1,0:T(1,128)S(1)} %add_add_fusion), channel_id=1, source_target_pairs={{0,16},{1,17},{2,18},{3,19},{4,20},{5,21},{6,22},{7,23},{8,24},{9,... | collective-permute-start | bytes 1544 | tf_op jit(solution)/shard_map/ppermute | solution.py:257
  40.5 2.6 %shard_map.56 = (f32[28,128,128]{2,1,0:T(8,128)S(1)}, f32[64,7168]{1,0:T(8,128)S(1)}, f32[64,7168]{1,0:T(8,128)S(1)}, f32[64,7168]{1,0:T(8,128)S(1)}) custom-call(bf16[32,112,128]{2,1,0:T(8,128)(2,1)S(1)} %all-to-all-done.grad_ref, f32[64,7168]{1,0:T(8,128)} %bitcast.10, f32[64,7168]{1,0:T(8,128)} %bitcast.11, f32[64,7168]{1,0:T(8,128)} %bitcast.12), custom_call_target="tpu_custom_call" | custom-call | tf_op jit(solution)/shard_map/pallas_call | solution.py:106
  43.1 2.1 %shard_map.57 = bf16[32,112,128]{2,1,0:T(8,128)(2,1)S(1)} custom-call(f32[1,128]{1,0:T(1,128)S(1)} %add.43.squares_ref, f32[28,128,128]{2,1,0:T(8,128)S(1)} %get-tuple-element.19.turned_ref, f32[64,7168]{1,0:T(8,128)S(1)} %get-tuple-element.20.master_ref, f32[64,7168]{1,0:T(8,128)S(1)} %get-tuple-element.21.first_ref, ...), custom_call_target="tpu_custom_call" | custom-call | tf_op jit(solution)/shard_map/pallas_call | solution.py:147
  45.2 25.6 %all_to_all.10.block_ref = bf16[32,112,128]{2,1,0:T(8,128)(2,1)S(1)} all-to-all(bf16[32,112,128]{2,1,0:T(8,128)(2,1)S(1)} %shard_map.57), channel_id=1, replica_groups=mesh['grp'=8,'fsdp'=32] {'fsdp'}, dimensions={0} | all-to-all | bytes 1835008 | tf_op jit(solution)/shard_map/all_to_all | solution.py:261
  71.4 2.4 %collective-permute-start.14 = (bf16[112,2048]{1,0:T(8,128)(2,1)S(1)}, bf16[112,2048]{1,0:T(8,128)(2,1)S(1)}, u32[]{:S(2)}, u32[]{:S(2)}) collective-permute-start(bf16[112,2048]{1,0:T(8,128)(2,1)S(1)} %get-tuple-element.23.refs_0_), channel_id=1, source_target_pairs={{0,64},{32,96},{64,128},{96,160},{128,192},{160,224},{192,0},{224,... | collective-permute-start | bytes 1376264 | tf_op jit(solution)/shard_map/ppermute | solution.py:182
  73.8 2.2 %collective-permute-start.12 = (bf16[112,2048]{1,0:T(8,128)(2,1)S(1)}, bf16[112,2048]{1,0:T(8,128)(2,1)S(1)}, u32[]{:S(2)}, u32[]{:S(2)}) collective-permute-start(bf16[112,2048]{1,0:T(8,128)(2,1)S(1)} %get-tuple-element.23.refs_0_), channel_id=1, source_target_pairs={{0,192},{32,224},{64,0},{96,32},{128,64},{160,96},{192,128},{224,1... | collective-permute-start | bytes 1376264 | tf_op jit(solution)/shard_map/ppermute | solution.py:182
  76.0 6.1 %collective-permute-start.11 = (bf16[112,2048]{1,0:T(8,128)(2,1)S(1)}, bf16[112,2048]{1,0:T(8,128)(2,1)S(1)}, u32[]{:S(2)}, u32[]{:S(2)}) collective-permute-start(bf16[112,2048]{1,0:T(8,128)(2,1)S(1)} %get-tuple-element.23.refs_0_), channel_id=1, source_target_pairs={{0,32},{32,0},{64,96},{96,64},{128,160},{160,128},{192,224},{224,1... | collective-permute-start | bytes 1376264 | tf_op jit(solution)/shard_map/ppermute | solution.py:186
  82.1 1.7 %collective-permute-start.19 = (bf16[112,2048]{1,0:T(8,128)(2,1)S(1)}, bf16[112,2048]{1,0:T(8,128)(2,1)S(1)}, u32[]{:S(2)}, u32[]{:S(2)}) collective-permute-start(bf16[112,2048]{1,0:T(8,128)(2,1)S(1)} %get-tuple-element.24.refs_8_), channel_id=1, source_target_pairs={{0,192},{32,224},{64,0},{96,32},{128,64},{160,96},{192,128},{224,1... | collective-permute-start | bytes 1376264 | tf_op jit(solution)/shard_map/ppermute | solution.py:182
  83.8 5.1 %collective-permute-start.18 = (bf16[112,2048]{1,0:T(8,128)(2,1)S(1)}, bf16[112,2048]{1,0:T(8,128)(2,1)S(1)}, u32[]{:S(2)}, u32[]{:S(2)}) collective-permute-start(bf16[112,2048]{1,0:T(8,128)(2,1)S(1)} %get-tuple-element.24.refs_8_), channel_id=1, source_target_pairs={{0,32},{32,0},{64,96},{96,64},{128,160},{160,128},{192,224},{224,1... | collective-permute-start | bytes 1376264 | tf_op jit(solution)/shard_map/ppermute | solution.py:186
  88.8 3.8 %collective-permute-start.17 = (bf16[112,2048]{1,0:T(8,128)(2,1)S(1)}, bf16[112,2048]{1,0:T(8,128)(2,1)S(1)}, u32[]{:S(2)}, u32[]{:S(2)}) collective-permute-start(bf16[112,2048]{1,0:T(8,128)(2,1)S(1)} %collective-permute-done.14.refs_6_), channel_id=1, source_target_pairs={{0,32},{32,0},{64,96},{96,64},{128,160},{160,128},{192,224},{224,1... | collective-permute-start | bytes 1376264 | tf_op jit(solution)/shard_map/ppermute | solution.py:186
  92.7 2.3 %collective-permute-start.15 = (bf16[112,2048]{1,0:T(8,128)(2,1)S(1)}, bf16[112,2048]{1,0:T(8,128)(2,1)S(1)}, u32[]{:S(2)}, u32[]{:S(2)}) collective-permute-start(bf16[112,2048]{1,0:T(8,128)(2,1)S(1)} %collective-permute-done.14.refs_6_), channel_id=1, source_target_pairs={{0,64},{32,96},{64,128},{96,160},{128,192},{160,224},{192,0},{224,... | collective-permute-start | bytes 1376264 | tf_op jit(solution)/shard_map/ppermute | solution.py:182
  95.0 2.6 %collective-permute-start.21 = (bf16[112,2048]{1,0:T(8,128)(2,1)S(1)}, bf16[112,2048]{1,0:T(8,128)(2,1)S(1)}, u32[]{:S(2)}, u32[]{:S(2)}) collective-permute-start(bf16[112,2048]{1,0:T(8,128)(2,1)S(1)} %collective-permute-done.19.refs_10_), channel_id=1, source_target_pairs={{0,192},{32,224},{64,0},{96,32},{128,64},{160,96},{192,128},{224,1... | collective-permute-start | bytes 1376264 | tf_op jit(solution)/shard_map/ppermute | solution.py:182
  97.6 4.0 %collective-permute-start.20 = (bf16[112,2048]{1,0:T(8,128)(2,1)S(1)}, bf16[112,2048]{1,0:T(8,128)(2,1)S(1)}, u32[]{:S(2)}, u32[]{:S(2)}) collective-permute-start(bf16[112,2048]{1,0:T(8,128)(2,1)S(1)} %collective-permute-done.19.refs_10_), channel_id=1, source_target_pairs={{0,32},{32,0},{64,96},{96,64},{128,160},{160,128},{192,224},{224,1... | collective-permute-start | bytes 1376264 | tf_op jit(solution)/shard_map/ppermute | solution.py:186
  102.1 5.3 %collective-permute-done.15.refs_4_ = bf16[112,2048]{1,0:T(8,128)(2,1)S(1)} collective-permute-done((bf16[112,2048]{1,0:T(8,128)(2,1)S(1)}, bf16[112,2048]{1,0:T(8,128)(2,1)S(1)}, u32[]{:S(2)}, u32[]{:S(2)}) %collective-permute-start.15) | collective-permute-done | bytes 458784 | tf_op jit(solution)/shard_map/ppermute | solution.py:182
  110.2 2.5 %shard_map.59 = bf16[4,224,2048]{2,1,0:T(8,128)(2,1)} custom-call(s32[4]{0:T(128)S(1)} %bitcast.8, bf16[112,2048]{1,0:T(8,128)(2,1)S(1)} %get-tuple-element.23.refs_0_, bf16[112,2048]{1,0:T(8,128)(2,1)S(1)} %collective-permute-done.11.refs_1_, bf16[112,2048]{1,0:T(8,128)(2,1)S(1)} %collective-permute-done.12.refs_2_, ...), custom_call_target="tpu_custom_call" | custom-call | tf_op jit(solution)/shard_map/pallas_call | solution.py:232
  (41 shorter events, 8.6 us)
Async XLA Ops:
  2.3 38.1 %all-to-all-start = ((bf16[32,112,128]{2,1,0:T(8,128)(2,1)}), bf16[32,112,128]{2,1,0:T(8,128)(2,1)S(1)}, u32[]{:S(2)}, u32[]{:S(2)}) async-start(bf16[32,112,128]{2,1,0:T(8,128)(2,1)} %get-tuple-element.16), calls=%async_computation | async-start | bytes 1835008 | tf_op jit(solution)/shard_map/all_to_all | solution.py:252
  16.1 4.0 %collective-permute-start.3 = (f32[1,128]{1,0:T(1,128)S(1)}, f32[1,128]{1,0:T(1,128)S(1)}, u32[]{:S(2)}, u32[]{:S(2)}) collective-permute-start(f32[1,128]{1,0:T(1,128)S(1)} %add.33), channel_id=1, source_target_pairs={{0,192},{32,224},{64,128},{96,160},{128,64},{160,96},{192,0},{224,... | collective-permute-start | bytes 1544 | tf_op jit(solution)/shard_map/ppermute | solution.py:244
  18.8 4.2 %collective-permute-start.2 = (f32[1,128]{1,0:T(1,128)S(1)}, f32[1,128]{1,0:T(1,128)S(1)}, u32[]{:S(2)}, u32[]{:S(2)}) collective-permute-start(f32[1,128]{1,0:T(1,128)S(1)} %add.33), channel_id=1, source_target_pairs={{0,128},{32,160},{64,192},{96,224},{128,0},{160,32},{192,64},{224,... | collective-permute-start | bytes 1544 | tf_op jit(solution)/shard_map/ppermute | solution.py:244
  19.2 3.8 %collective-permute-start.1 = (f32[1,128]{1,0:T(1,128)S(1)}, f32[1,128]{1,0:T(1,128)S(1)}, u32[]{:S(2)}, u32[]{:S(2)}) collective-permute-start(f32[1,128]{1,0:T(1,128)S(1)} %add.33), channel_id=1, source_target_pairs={{0,64},{32,96},{64,0},{96,32},{128,192},{160,224},{192,128},{224,1... | collective-permute-start | bytes 1544 | tf_op jit(solution)/shard_map/ppermute | solution.py:244
  23.0 4.0 %collective-permute-start.6 = (f32[1,128]{1,0:T(1,128)S(1)}, f32[1,128]{1,0:T(1,128)S(1)}, u32[]{:S(2)}, u32[]{:S(2)}) collective-permute-start(f32[1,128]{1,0:T(1,128)S(1)} %add_add_fusion.2), channel_id=1, source_target_pairs={{0,3},{1,2},{2,1},{3,0},{4,7},{5,6},{6,5},{7,4},{8,11},{9,10},{10,... | collective-permute-start | bytes 1544 | tf_op jit(solution)/shard_map/ppermute | solution.py:244
  25.8 4.2 %collective-permute-start.5 = (f32[1,128]{1,0:T(1,128)S(1)}, f32[1,128]{1,0:T(1,128)S(1)}, u32[]{:S(2)}, u32[]{:S(2)}) collective-permute-start(f32[1,128]{1,0:T(1,128)S(1)} %add_add_fusion.2), channel_id=1, source_target_pairs={{0,2},{1,3},{2,0},{3,1},{4,6},{5,7},{6,4},{7,5},{8,10},{9,11},{10,... | collective-permute-start | bytes 1544 | tf_op jit(solution)/shard_map/ppermute | solution.py:244
  26.4 3.6 %collective-permute-start.4 = (f32[1,128]{1,0:T(1,128)S(1)}, f32[1,128]{1,0:T(1,128)S(1)}, u32[]{:S(2)}, u32[]{:S(2)}) collective-permute-start(f32[1,128]{1,0:T(1,128)S(1)} %add_add_fusion.2), channel_id=1, source_target_pairs={{0,1},{1,0},{2,3},{3,2},{4,5},{5,4},{6,7},{7,6},{8,9},{9,8},{10,11... | collective-permute-start | bytes 1544 | tf_op jit(solution)/shard_map/ppermute | solution.py:244
  30.0 4.4 %collective-permute-start.9 = (f32[1,128]{1,0:T(1,128)S(1)}, f32[1,128]{1,0:T(1,128)S(1)}, u32[]{:S(2)}, u32[]{:S(2)}) collective-permute-start(f32[1,128]{1,0:T(1,128)S(1)} %add_add_fusion.1), channel_id=1, source_target_pairs={{0,12},{1,13},{2,14},{3,15},{4,8},{5,9},{6,10},{7,11},{8,4},{9,5},... | collective-permute-start | bytes 1544 | tf_op jit(solution)/shard_map/ppermute | solution.py:244
  33.1 3.6 %collective-permute-start.8 = (f32[1,128]{1,0:T(1,128)S(1)}, f32[1,128]{1,0:T(1,128)S(1)}, u32[]{:S(2)}, u32[]{:S(2)}) collective-permute-start(f32[1,128]{1,0:T(1,128)S(1)} %add_add_fusion.1), channel_id=1, source_target_pairs={{0,8},{1,9},{2,10},{3,11},{4,12},{5,13},{6,14},{7,15},{8,0},{9,1},... | collective-permute-start | bytes 1544 | tf_op jit(solution)/shard_map/ppermute | solution.py:244
  33.1 3.6 %collective-permute-start.7 = (f32[1,128]{1,0:T(1,128)S(1)}, f32[1,128]{1,0:T(1,128)S(1)}, u32[]{:S(2)}, u32[]{:S(2)}) collective-permute-start(f32[1,128]{1,0:T(1,128)S(1)} %add_add_fusion.1), channel_id=1, source_target_pairs={{0,4},{1,5},{2,6},{3,7},{4,0},{5,1},{6,2},{7,3},{8,12},{9,13},{10,... | collective-permute-start | bytes 1544 | tf_op jit(solution)/shard_map/ppermute | solution.py:244
  36.7 6.4 %collective-permute-start.10 = (f32[1,128]{1,0:T(1,128)S(1)}, f32[1,128]{1,0:T(1,128)S(1)}, u32[]{:S(2)}, u32[]{:S(2)}) collective-permute-start(f32[1,128]{1,0:T(1,128)S(1)} %add_add_fusion), channel_id=1, source_target_pairs={{0,16},{1,17},{2,18},{3,19},{4,20},{5,21},{6,22},{7,23},{8,24},{9,... | collective-permute-start | bytes 1544 | tf_op jit(solution)/shard_map/ppermute | solution.py:257
  71.4 12.3 %collective-permute-start.14 = (bf16[112,2048]{1,0:T(8,128)(2,1)S(1)}, bf16[112,2048]{1,0:T(8,128)(2,1)S(1)}, u32[]{:S(2)}, u32[]{:S(2)}) collective-permute-start(bf16[112,2048]{1,0:T(8,128)(2,1)S(1)} %get-tuple-element.23.refs_0_), channel_id=1, source_target_pairs={{0,64},{32,96},{64,128},{96,160},{128,192},{160,224},{192,0},{224,... | collective-permute-start | bytes 1376264 | tf_op jit(solution)/shard_map/ppermute | solution.py:182
  73.8 15.0 %collective-permute-start.12 = (bf16[112,2048]{1,0:T(8,128)(2,1)S(1)}, bf16[112,2048]{1,0:T(8,128)(2,1)S(1)}, u32[]{:S(2)}, u32[]{:S(2)}) collective-permute-start(bf16[112,2048]{1,0:T(8,128)(2,1)S(1)} %get-tuple-element.23.refs_0_), channel_id=1, source_target_pairs={{0,192},{32,224},{64,0},{96,32},{128,64},{160,96},{192,128},{224,1... | collective-permute-start | bytes 1376264 | tf_op jit(solution)/shard_map/ppermute | solution.py:182
  76.0 16.6 %collective-permute-start.11 = (bf16[112,2048]{1,0:T(8,128)(2,1)S(1)}, bf16[112,2048]{1,0:T(8,128)(2,1)S(1)}, u32[]{:S(2)}, u32[]{:S(2)}) collective-permute-start(bf16[112,2048]{1,0:T(8,128)(2,1)S(1)} %get-tuple-element.23.refs_0_), channel_id=1, source_target_pairs={{0,32},{32,0},{64,96},{96,64},{128,160},{160,128},{192,224},{224,1... | collective-permute-start | bytes 1376264 | tf_op jit(solution)/shard_map/ppermute | solution.py:186
  82.1 12.9 %collective-permute-start.19 = (bf16[112,2048]{1,0:T(8,128)(2,1)S(1)}, bf16[112,2048]{1,0:T(8,128)(2,1)S(1)}, u32[]{:S(2)}, u32[]{:S(2)}) collective-permute-start(bf16[112,2048]{1,0:T(8,128)(2,1)S(1)} %get-tuple-element.24.refs_8_), channel_id=1, source_target_pairs={{0,192},{32,224},{64,0},{96,32},{128,64},{160,96},{192,128},{224,1... | collective-permute-start | bytes 1376264 | tf_op jit(solution)/shard_map/ppermute | solution.py:182
  83.8 13.8 %collective-permute-start.23 = (bf16[112,2048]{1,0:T(8,128)(2,1)S(1)}, bf16[112,2048]{1,0:T(8,128)(2,1)S(1)}, u32[]{:S(2)}, u32[]{:S(2)}) collective-permute-start(bf16[112,2048]{1,0:T(8,128)(2,1)S(1)} %get-tuple-element.24.refs_8_), channel_id=1, source_target_pairs={{0,64},{32,96},{64,128},{96,160},{128,192},{160,224},{192,0},{224,... | collective-permute-start | bytes 1376264 | tf_op jit(solution)/shard_map/ppermute | solution.py:182
  83.8 17.9 %collective-permute-start.18 = (bf16[112,2048]{1,0:T(8,128)(2,1)S(1)}, bf16[112,2048]{1,0:T(8,128)(2,1)S(1)}, u32[]{:S(2)}, u32[]{:S(2)}) collective-permute-start(bf16[112,2048]{1,0:T(8,128)(2,1)S(1)} %get-tuple-element.24.refs_8_), channel_id=1, source_target_pairs={{0,32},{32,0},{64,96},{96,64},{128,160},{160,128},{192,224},{224,1... | collective-permute-start | bytes 1376264 | tf_op jit(solution)/shard_map/ppermute | solution.py:186
  88.8 12.9 %collective-permute-start.17 = (bf16[112,2048]{1,0:T(8,128)(2,1)S(1)}, bf16[112,2048]{1,0:T(8,128)(2,1)S(1)}, u32[]{:S(2)}, u32[]{:S(2)}) collective-permute-start(bf16[112,2048]{1,0:T(8,128)(2,1)S(1)} %collective-permute-done.14.refs_6_), channel_id=1, source_target_pairs={{0,32},{32,0},{64,96},{96,64},{128,160},{160,128},{192,224},{224,1... | collective-permute-start | bytes 1376264 | tf_op jit(solution)/shard_map/ppermute | solution.py:186
  92.7 14.7 %collective-permute-start.15 = (bf16[112,2048]{1,0:T(8,128)(2,1)S(1)}, bf16[112,2048]{1,0:T(8,128)(2,1)S(1)}, u32[]{:S(2)}, u32[]{:S(2)}) collective-permute-start(bf16[112,2048]{1,0:T(8,128)(2,1)S(1)} %collective-permute-done.14.refs_6_), channel_id=1, source_target_pairs={{0,64},{32,96},{64,128},{96,160},{128,192},{160,224},{192,0},{224,... | collective-permute-start | bytes 1376264 | tf_op jit(solution)/shard_map/ppermute | solution.py:182
  95.0 13.2 %collective-permute-start.21 = (bf16[112,2048]{1,0:T(8,128)(2,1)S(1)}, bf16[112,2048]{1,0:T(8,128)(2,1)S(1)}, u32[]{:S(2)}, u32[]{:S(2)}) collective-permute-start(bf16[112,2048]{1,0:T(8,128)(2,1)S(1)} %collective-permute-done.19.refs_10_), channel_id=1, source_target_pairs={{0,192},{32,224},{64,0},{96,32},{128,64},{160,96},{192,128},{224,1... | collective-permute-start | bytes 1376264 | tf_op jit(solution)/shard_map/ppermute | solution.py:182
  97.6 11.0 %collective-permute-start.20 = (bf16[112,2048]{1,0:T(8,128)(2,1)S(1)}, bf16[112,2048]{1,0:T(8,128)(2,1)S(1)}, u32[]{:S(2)}, u32[]{:S(2)}) collective-permute-start(bf16[112,2048]{1,0:T(8,128)(2,1)S(1)} %collective-permute-done.19.refs_10_), channel_id=1, source_target_pairs={{0,32},{32,0},{64,96},{96,64},{128,160},{160,128},{192,224},{224,1... | collective-permute-start | bytes 1376264 | tf_op jit(solution)/shard_map/ppermute | solution.py:186
  101.6 7.0 %collective-permute-start.13 = (bf16[112,2048]{1,0:T(8,128)(2,1)S(1)}, bf16[112,2048]{1,0:T(8,128)(2,1)S(1)}, u32[]{:S(2)}, u32[]{:S(2)}) collective-permute-start(bf16[112,2048]{1,0:T(8,128)(2,1)S(1)} %collective-permute-done.12.refs_2_), channel_id=1, source_target_pairs={{0,32},{32,0},{64,96},{96,64},{128,160},{160,128},{192,224},{224,1... | collective-permute-start | bytes 1376264 | tf_op jit(solution)/shard_map/ppermute | solution.py:186
  101.7 6.9 %collective-permute-start.24 = (bf16[112,2048]{1,0:T(8,128)(2,1)S(1)}, bf16[112,2048]{1,0:T(8,128)(2,1)S(1)}, u32[]{:S(2)}, u32[]{:S(2)}) collective-permute-start(bf16[112,2048]{1,0:T(8,128)(2,1)S(1)} %collective-permute-done.23.refs_14_), channel_id=1, source_target_pairs={{0,32},{32,0},{64,96},{96,64},{128,160},{160,128},{192,224},{224,1... | collective-permute-start | bytes 1376264 | tf_op jit(solution)/shard_map/ppermute | solution.py:186
  107.4 2.2 %collective-permute-start.16 = (bf16[112,2048]{1,0:T(8,128)(2,1)S(1)}, bf16[112,2048]{1,0:T(8,128)(2,1)S(1)}, u32[]{:S(2)}, u32[]{:S(2)}) collective-permute-start(bf16[112,2048]{1,0:T(8,128)(2,1)S(1)} %collective-permute-done.15.refs_4_), channel_id=1, source_target_pairs={{0,32},{32,0},{64,96},{96,64},{128,160},{160,128},{192,224},{224,1... | collective-permute-start | bytes 1376264 | tf_op jit(solution)/shard_map/ppermute | solution.py:186
  (3 other events, 69.0 us)

commit v4 on v3

--- a/solution.py
+++ b/solution.py
@@ -24,6 +24,9 @@
 LANES = 128
 HALF = 64
 CHUNKS = 4
+FIRST = (-1, 0, 1, 2, 3, 6, 7)
+SECOND = (4, 5)
+COST = 2
 EXCHANGES = (("grp", 1, 2), ("grp", 2, 4), ("fsdp", 1, 4), ("fsdp", 4, 4), ("fsdp", 16, 2))
 VMEM_LIMIT = 16 * 1024 * 1024
 
@@ -186,57 +189,50 @@
     return lax.ppermute(array, "grp", [(i, i ^ 1) for i in range(lax.axis_size("grp"))])
 
 
-def gather_experts(mine, onward):
-    after, before = shift(mine, -1), shift(mine, 1)
-    far = shift(before if onward > 0 else after, onward)
-    by_chip = [mine, after, far, before]
-    return [held for near in by_chip for held in (near, other_core(near))]
-
-
-def place_kernel(halves, slot_ref, *refs):
-    held, out_ref, blank_ref, sems = refs[:-3], refs[-3], refs[-2], refs[-1]
+def place_kernel(keys, halves, slot_ref, *refs):
+    held, out_ref, blank_ref, sems = refs[: len(keys) * halves], refs[-3], refs[-2], refs[-1]
     slots, columns = out_ref.shape[0], out_ref.shape[1] // halves
-    sources = len(held) // halves
-    me = lax.axis_index("grp")
+    me, chips = lax.axis_index("grp"), lax.axis_size("grp") // 2
 
     def copy(source, slot, half):
         target = out_ref.at[slot, pl.ds(half * columns, columns)]
         return pltpu.make_async_copy(source, target, sems.at[slot, half])
 
-    blank_ref[...] = jnp.zeros_like(blank_ref)
+    if -1 in keys:
+        blank_ref[...] = jnp.zeros_like(blank_ref)
+    places = []
     for slot in range(slots):
         expert = slot_ref[slot]
-        chips = (expert // 2 - me // 2 + sources // 2) % (sources // 2)
-        place = jnp.where(expert < 0, -1, 2 * chips + (expert + me) % 2)
-        for half in range(halves):
-
-            @pl.when(place < 0)
-            def _():
-                copy(blank_ref, slot, half).start()
-
-            for source in range(sources):
-
-                @pl.when(place == source)
+        apart = (expert // 2 - me // 2 + chips) % chips
+        places.append(jnp.where(expert < 0, -1, 2 * apart + (expert + me) % 2))
+    for act in ("start", "wait"):
+        for slot in range(slots):
+            for at, key in enumerate(keys):
+
+                @pl.when(places[slot] == key)
                 def _():
-                    copy(held[half * sources + source], slot, half).start()
-
-    for slot in range(slots):
-        for half in range(halves):
-            copy(blank_ref, slot, half).wait()
-
-
-def place(slot_ids, experts):
+                    for half in range(halves):
+                        source = blank_ref if key < 0 else held[half * len(keys) + at]
+                        getattr(copy(source, slot, half), act)()
+
+
+def place(slot_ids, keys, experts, rollout=None):
     slots, halves = slot_ids.shape[0], len(experts)
-    columns, rows = experts[0][0].shape
-    held = [array for half in experts for array in half]
-    return pl.pallas_call(
-        functools.partial(place_kernel, halves),
-        in_specs=[pl.BlockSpec(memory_space=pltpu.SMEM)] + [pl.BlockSpec(memory_space=pl.ANY)] * len(held),
-        out_specs=pl.BlockSpec(memory_space=pl.ANY),
+    columns, rows = experts[0][keys[-1]].shape
+    held = [half[key] if key >= 0 else half[keys[-1]] for half in experts for key in keys]
+    extra = [] if rollout is None else [rollout]
+    far = pl.BlockSpec(memory_space=pl.ANY)
+    size = len(keys) * halves * columns * rows
+    return pl.pallas_call(
+        functools.partial(place_kernel, keys, halves),
+        in_specs=[pl.BlockSpec(memory_space=pltpu.SMEM)] + [far] * (len(held) + len(extra)),
+        out_specs=far,
         out_shape=jax.ShapeDtypeStruct((slots, halves * columns, rows), jnp.bfloat16),
         scratch_shapes=[pltpu.VMEM((columns, rows), jnp.bfloat16), pltpu.SemaphoreType.DMA((slots, halves))],
-        compiler_params=pltpu.CompilerParams(vmem_limit_bytes=VMEM_LIMIT),
-    )(slot_ids, *held)
+        input_output_aliases={1 + len(held): 0} if extra else {},
+        cost_estimate=pl.CostEstimate(flops=0, bytes_accessed=COST * size, transcendentals=0),
+        compiler_params=pltpu.CompilerParams(vmem_limit_bytes=VMEM_LIMIT),
+    )(slot_ids, *held, *extra)
 
 
 def total_over(partial, axis, apart, radix):
@@ -260,7 +256,15 @@
     weights = adam(entries, squares, turned, *states)
     columns = lax.all_to_all(weights, "fsdp", 0, 0, tiled=True)
     low, high = unpack(columns)
-    rollout = place(slot_ids, [gather_experts(low, 1), gather_experts(high, -1)])
+    halves = [{0: low}, {0: high}]
+    for half, onward in zip(halves, (1, -1)):
+        half[2], half[6] = shift(half[0], -1), shift(half[0], 1)
+        half[4] = shift(half[6] if onward > 0 else half[2], onward)
+        half[1], half[3], half[7] = other_core(half[0]), other_core(half[2]), other_core(half[6])
+    rollout = place(slot_ids, FIRST, halves)
+    for half in halves:
+        half[5] = other_core(half[4])
+    rollout = place(slot_ids, SECOND, halves, rollout)
     return jnp.swapaxes(rollout, 1, 2)
 
 

time: 113 us -> 112 us (level)
  waiting for transfers between devices: 17.9 us -> 13.4 us
  starting transfers between devices: 59 us -> 63.1 us
  blocking collectives: 25.6 us -> 23.8 us
    ppermute x6, waiting for transfers between devices: 5.27 us -> 0.04 us  [shift(): lax.ppermute(array, 'grp', [(i, (i + 2 * chips) % size) for i in range(si...]
    ppermute x8, starting transfers between devices: 20.7 us -> 25.8 us  [other_core(): lax.ppermute(array, 'grp', [(i, i ^ 1) for i in range(lax.axis_size('grp'...]
    all_to_all x1, blocking collectives: 25.6 us -> 23.8 us  [body(): columns = lax.all_to_all(weights, 'fsdp', 0, 0, tiled=True)]
    ppermute x8, waiting for transfers between devices: 1.64 us -> 0.02 us  [other_core(): lax.ppermute(array, 'grp', [(i, i ^ 1) for i in range(lax.axis_size('grp'...]
    ppermute x10, waiting for transfers between devices: 11 us -> 12.4 us  [total_over(): lax.ppermute(partial, axis, [(i, i ^ apart * k) for i in range(size)])]
    pallas_call x1 -> x2, Pallas kernels: 2.49 us -> 3.2 us  [place(): pl.pallas_call(functools.partial(place_kernel, keys, halves), in_specs=[p...]
  transfers between devices with their start and end apart: 26 -> 26, of which waited for: 10 -> 8; matrix products, arithmetic and copies ran while one was open for 0% -> 0% of each run, Pallas kernels for 2% -> 5%
where the time goes in v4:
time: 112 us; the launch traced here: 111 us
  starting transfers between devices  63.1 us (56%)
  blocking collectives  23.8 us (21%)
  waiting for transfers between devices  13.4 us (12%)
  Pallas kernels  10.9 us (10%)
    ppermute x8, starting transfers between devices, other_core(): lax.ppermute(array, 'grp', [(i, i ^ 1) for i in range(lax.axis_size('grp'...  25.8 us
    all_to_all x1, blocking collectives, body(): columns = lax.all_to_all(weights, 'fsdp', 0, 0, tiled=True)  23.8 us
    ppermute x10, starting transfers between devices, total_over(): lax.ppermute(partial, axis, [(i, i ^ apart * k) for i in range(size)])  12.5 us
    ppermute x10, waiting for transfers between devices, total_over(): lax.ppermute(partial, axis, [(i, i ^ apart * k) for i in range(size)])  12.4 us
    all_to_all x1, starting transfers between devices, body(): grad_here = lax.all_to_all(grad_blocks, 'fsdp', 0, 0, tiled=True)  11.9 us
    ppermute x6, starting transfers between devices, shift(): lax.ppermute(array, 'grp', [(i, (i + 2 * chips) % size) for i in range(si...  10.2 us
    pallas_call x2, Pallas kernels, place(): pl.pallas_call(functools.partial(place_kernel, keys, halves), in_specs=[p...  3.2 us
    ppermute x1, starting transfers between devices, body(): lax.ppermute(squares, axis, [(i, i ^ apart) for i in range(lax.axis_size(...  2.78 us
  transfers between devices with their start and end apart: 26, of which 8 were waited for; matrix products, arithmetic and copies ran while one was open for 0% of the time, Pallas kernels for 5%

profile of v4, /device:TPU:1, one launch (start us, length us, event | category | flops | bytes accessed | tf_op | source)
XLA Modules:
  0.0 111.4 jit_solution(1763169739323448943)
XLA Ops:
  0.0 2.3 %shard_map.55 = (bf16[32,112,128]{2,1,0:T(8,128)(2,1)}, f32[1,128]{1,0:T(1,128)S(1)}) custom-call(f32[224,2048]{1,0:T(8,128)} %bitcast.10), custom_call_target="tpu_custom_call" | custom-call | tf_op jit(solution)/shard_map/pallas_call | solution.py:71
  2.3 11.9 %all-to-all-start = ((bf16[32,112,128]{2,1,0:T(8,128)(2,1)}), bf16[32,112,128]{2,1,0:T(8,128)(2,1)S(1)}, u32[]{:S(2)}, u32[]{:S(2)}) async-start(bf16[32,112,128]{2,1,0:T(8,128)(2,1)} %get-tuple-element.16), calls=%async_computation | async-start | bytes 1835008 | tf_op jit(solution)/shard_map/all_to_all | solution.py:248
  17.4 2.6 %collective-permute-start.2 = (f32[1,128]{1,0:T(1,128)S(1)}, f32[1,128]{1,0:T(1,128)S(1)}, u32[]{:S(2)}, u32[]{:S(2)}) collective-permute-start(f32[1,128]{1,0:T(1,128)S(1)} %add.33), channel_id=1, source_target_pairs={{0,128},{32,160},{64,192},{96,224},{128,0},{160,32},{192,64},{224,... | collective-permute-start | bytes 1544 | tf_op jit(solution)/shard_map/ppermute | solution.py:240
  21.3 2.6 %collective-permute-done.3 = f32[1,128]{1,0:T(1,128)S(1)} collective-permute-done((f32[1,128]{1,0:T(1,128)S(1)}, f32[1,128]{1,0:T(1,128)S(1)}, u32[]{:S(2)}, u32[]{:S(2)}) %collective-permute-start.3) | collective-permute-done | bytes 544 | tf_op jit(solution)/shard_map/ppermute | solution.py:240
  23.9 1.5 %collective-permute-start.4 = (f32[1,128]{1,0:T(1,128)S(1)}, f32[1,128]{1,0:T(1,128)S(1)}, u32[]{:S(2)}, u32[]{:S(2)}) collective-permute-start(f32[1,128]{1,0:T(1,128)S(1)} %add_add_fusion.2), channel_id=1, source_target_pairs={{0,1},{1,0},{2,3},{3,2},{4,5},{5,4},{6,7},{7,6},{8,9},{9,8},{10,11... | collective-permute-start | bytes 1544 | tf_op jit(solution)/shard_map/ppermute | solution.py:240
  25.4 2.4 %collective-permute-start.5 = (f32[1,128]{1,0:T(1,128)S(1)}, f32[1,128]{1,0:T(1,128)S(1)}, u32[]{:S(2)}, u32[]{:S(2)}) collective-permute-start(f32[1,128]{1,0:T(1,128)S(1)} %add_add_fusion.2), channel_id=1, source_target_pairs={{0,2},{1,3},{2,0},{3,1},{4,6},{5,7},{6,4},{7,5},{8,10},{9,11},{10,... | collective-permute-start | bytes 1544 | tf_op jit(solution)/shard_map/ppermute | solution.py:240
  27.9 1.7 %collective-permute-done.5 = f32[1,128]{1,0:T(1,128)S(1)} collective-permute-done((f32[1,128]{1,0:T(1,128)S(1)}, f32[1,128]{1,0:T(1,128)S(1)}, u32[]{:S(2)}, u32[]{:S(2)}) %collective-permute-start.5) | collective-permute-done | bytes 544 | tf_op jit(solution)/shard_map/ppermute | solution.py:240
  29.6 2.1 %collective-permute-done.6 = f32[1,128]{1,0:T(1,128)S(1)} collective-permute-done((f32[1,128]{1,0:T(1,128)S(1)}, f32[1,128]{1,0:T(1,128)S(1)}, u32[]{:S(2)}, u32[]{:S(2)}) %collective-permute-start.6) | collective-permute-done | bytes 544 | tf_op jit(solution)/shard_map/ppermute | solution.py:240
  32.8 1.8 %collective-permute-start.8 = (f32[1,128]{1,0:T(1,128)S(1)}, f32[1,128]{1,0:T(1,128)S(1)}, u32[]{:S(2)}, u32[]{:S(2)}) collective-permute-start(f32[1,128]{1,0:T(1,128)S(1)} %add_add_fusion.1), channel_id=1, source_target_pairs={{0,8},{1,9},{2,10},{3,11},{4,12},{5,13},{6,14},{7,15},{8,0},{9,1},... | collective-permute-start | bytes 1544 | tf_op jit(solution)/shard_map/ppermute | solution.py:240
  36.4 2.8 %collective-permute-done.9 = f32[1,128]{1,0:T(1,128)S(1)} collective-permute-done((f32[1,128]{1,0:T(1,128)S(1)}, f32[1,128]{1,0:T(1,128)S(1)}, u32[]{:S(2)}, u32[]{:S(2)}) %collective-permute-start.9) | collective-permute-done | bytes 544 | tf_op jit(solution)/shard_map/ppermute | solution.py:240
  39.2 2.8 %collective-permute-start.10 = (f32[1,128]{1,0:T(1,128)S(1)}, f32[1,128]{1,0:T(1,128)S(1)}, u32[]{:S(2)}, u32[]{:S(2)}) collective-permute-start(f32[1,128]{1,0:T(1,128)S(1)} %add_add_fusion), channel_id=1, source_target_pairs={{0,16},{1,17},{2,18},{3,19},{4,20},{5,21},{6,22},{7,23},{8,24},{9,... | collective-permute-start | bytes 1544 | tf_op jit(solution)/shard_map/ppermute | solution.py:253
  42.0 2.6 %shard_map.56 = (f32[28,128,128]{2,1,0:T(8,128)S(1)}, f32[64,7168]{1,0:T(8,128)S(1)}, f32[64,7168]{1,0:T(8,128)S(1)}, f32[64,7168]{1,0:T(8,128)S(1)}) custom-call(bf16[32,112,128]{2,1,0:T(8,128)(2,1)S(1)} %all-to-all-done.grad_ref, f32[64,7168]{1,0:T(8,128)} %bitcast.11, f32[64,7168]{1,0:T(8,128)} %bitcast.12, f32[64,7168]{1,0:T(8,128)} %bitcast.13), custom_call_target="tpu_custom_call" | custom-call | tf_op jit(solution)/shard_map/pallas_call | solution.py:109
  45.5 2.1 %shard_map.57 = bf16[32,112,128]{2,1,0:T(8,128)(2,1)S(1)} custom-call(f32[1,128]{1,0:T(1,128)S(1)} %add.43.squares_ref, f32[28,128,128]{2,1,0:T(8,128)S(1)} %get-tuple-element.19.turned_ref, f32[64,7168]{1,0:T(8,128)S(1)} %get-tuple-element.20.master_ref, f32[64,7168]{1,0:T(8,128)S(1)} %get-tuple-element.21.first_ref, ...), custom_call_target="tpu_custom_call" | custom-call | tf_op jit(solution)/shard_map/pallas_call | solution.py:150
  47.6 23.8 %all_to_all.10.block_ref = bf16[32,112,128]{2,1,0:T(8,128)(2,1)S(1)} all-to-all(bf16[32,112,128]{2,1,0:T(8,128)(2,1)S(1)} %shard_map.57), channel_id=1, replica_groups=mesh['grp'=8,'fsdp'=32] {'fsdp'}, dimensions={0} | all-to-all | bytes 1835008 | tf_op jit(solution)/shard_map/all_to_all | solution.py:257
  72.0 3.0 %collective-permute-start.11 = (bf16[112,2048]{1,0:T(8,128)(2,1)S(1)}, bf16[112,2048]{1,0:T(8,128)(2,1)S(1)}, u32[]{:S(2)}, u32[]{:S(2)}) collective-permute-start(bf16[112,2048]{1,0:T(8,128)(2,1)S(1)} %get-tuple-element.23.refs_1_), channel_id=1, source_target_pairs={{0,64},{32,96},{64,128},{96,160},{128,192},{160,224},{192,0},{224,... | collective-permute-start | bytes 1376264 | tf_op jit(solution)/shard_map/ppermute | solution.py:185
  75.0 1.7 %collective-permute-start.19 = (bf16[112,2048]{1,0:T(8,128)(2,1)S(1)}, bf16[112,2048]{1,0:T(8,128)(2,1)S(1)}, u32[]{:S(2)}, u32[]{:S(2)}) collective-permute-start(bf16[112,2048]{1,0:T(8,128)(2,1)S(1)} %get-tuple-element.23.refs_1_), channel_id=1, source_target_pairs={{0,192},{32,224},{64,0},{96,32},{128,64},{160,96},{192,128},{224,1... | collective-permute-start | bytes 1376264 | tf_op jit(solution)/shard_map/ppermute | solution.py:185
  76.6 2.7 %collective-permute-start.14 = (bf16[112,2048]{1,0:T(8,128)(2,1)S(1)}, bf16[112,2048]{1,0:T(8,128)(2,1)S(1)}, u32[]{:S(2)}, u32[]{:S(2)}) collective-permute-start(bf16[112,2048]{1,0:T(8,128)(2,1)S(1)} %get-tuple-element.24.refs_8_), channel_id=1, source_target_pairs={{0,192},{32,224},{64,0},{96,32},{128,64},{160,96},{192,128},{224,1... | collective-permute-start | bytes 1376264 | tf_op jit(solution)/shard_map/ppermute | solution.py:185
  79.3 6.5 %collective-permute-start.18 = (bf16[112,2048]{1,0:T(8,128)(2,1)S(1)}, bf16[112,2048]{1,0:T(8,128)(2,1)S(1)}, u32[]{:S(2)}, u32[]{:S(2)}) collective-permute-start(bf16[112,2048]{1,0:T(8,128)(2,1)S(1)} %get-tuple-element.23.refs_1_), channel_id=1, source_target_pairs={{0,32},{32,0},{64,96},{96,64},{128,160},{160,128},{192,224},{224,1... | collective-permute-start | bytes 1376264 | tf_op jit(solution)/shard_map/ppermute | solution.py:189
  85.8 7.1 %collective-permute-start.23 = (bf16[112,2048]{1,0:T(8,128)(2,1)S(1)}, bf16[112,2048]{1,0:T(8,128)(2,1)S(1)}, u32[]{:S(2)}, u32[]{:S(2)}) collective-permute-start(bf16[112,2048]{1,0:T(8,128)(2,1)S(1)} %get-tuple-element.24.refs_8_), channel_id=1, source_target_pairs={{0,32},{32,0},{64,96},{96,64},{128,160},{160,128},{192,224},{224,1... | collective-permute-start | bytes 1376264 | tf_op jit(solution)/shard_map/ppermute | solution.py:189
  92.9 1.3 %collective-permute-start.12 = (bf16[112,2048]{1,0:T(8,128)(2,1)S(1)}, bf16[112,2048]{1,0:T(8,128)(2,1)S(1)}, u32[]{:S(2)}, u32[]{:S(2)}) collective-permute-start(bf16[112,2048]{1,0:T(8,128)(2,1)S(1)} %collective-permute-done.11.refs_5_), channel_id=1, source_target_pairs={{0,64},{32,96},{64,128},{96,160},{128,192},{160,224},{192,0},{224,... | collective-permute-start | bytes 1376264 | tf_op jit(solution)/shard_map/ppermute | solution.py:185
  94.3 1.5 %collective-permute-start.15 = (bf16[112,2048]{1,0:T(8,128)(2,1)S(1)}, bf16[112,2048]{1,0:T(8,128)(2,1)S(1)}, u32[]{:S(2)}, u32[]{:S(2)}) collective-permute-start(bf16[112,2048]{1,0:T(8,128)(2,1)S(1)} %collective-permute-done.14.refs_10_), channel_id=1, source_target_pairs={{0,192},{32,224},{64,0},{96,32},{128,64},{160,96},{192,128},{224,1... | collective-permute-start | bytes 1376264 | tf_op jit(solution)/shard_map/ppermute | solution.py:185
  95.8 5.7 %collective-permute-start.20 = (bf16[112,2048]{1,0:T(8,128)(2,1)S(1)}, bf16[112,2048]{1,0:T(8,128)(2,1)S(1)}, u32[]{:S(2)}, u32[]{:S(2)}) collective-permute-start(bf16[112,2048]{1,0:T(8,128)(2,1)S(1)} %collective-permute-done.19.refs_3_), channel_id=1, source_target_pairs={{0,32},{32,0},{64,96},{96,64},{128,160},{160,128},{192,224},{224,1... | collective-permute-start | bytes 1376264 | tf_op jit(solution)/shard_map/ppermute | solution.py:189
  102.1 5.9 %collective-permute-start.13 = (bf16[112,2048]{1,0:T(8,128)(2,1)S(1)}, bf16[112,2048]{1,0:T(8,128)(2,1)S(1)}, u32[]{:S(2)}, u32[]{:S(2)}) collective-permute-start(bf16[112,2048]{1,0:T(8,128)(2,1)S(1)} %collective-permute-done.12.refs_0_), channel_id=1, source_target_pairs={{0,32},{32,0},{64,96},{96,64},{128,160},{160,128},{192,224},{224,1... | collective-permute-start | bytes 1376264 | tf_op jit(solution)/shard_map/ppermute | solution.py:189
  108.0 2.5 %shard_map.59.refs_4_ = bf16[4,224,2048]{2,1,0:T(8,128)(2,1)} custom-call(s32[4]{0:T(128)S(1)} %bitcast.8, bf16[112,2048]{1,0:T(8,128)(2,1)S(1)} %collective-permute-done.17.refs_0_.refs_6_, bf16[112,2048]{1,0:T(8,128)(2,1)S(1)} %get-tuple-element.23.refs_1_, bf16[112,2048]{1,0:T(8,128)(2,1)S(1)} %collective-permute-done.18.refs_2_, ...), custom_call_target="tpu_custom_call" | custom-call | bytes 6422528 | tf_op jit(solution)/shard_map/pallas_call | solution.py:226
  (42 shorter events, 10.2 us)
Async XLA Ops:
  2.3 39.6 %all-to-all-start = ((bf16[32,112,128]{2,1,0:T(8,128)(2,1)}), bf16[32,112,128]{2,1,0:T(8,128)(2,1)S(1)}, u32[]{:S(2)}, u32[]{:S(2)}) async-start(bf16[32,112,128]{2,1,0:T(8,128)(2,1)} %get-tuple-element.16), calls=%async_computation | async-start | bytes 1835008 | tf_op jit(solution)/shard_map/all_to_all | solution.py:248
  16.1 3.9 %collective-permute-start.1 = (f32[1,128]{1,0:T(1,128)S(1)}, f32[1,128]{1,0:T(1,128)S(1)}, u32[]{:S(2)}, u32[]{:S(2)}) collective-permute-start(f32[1,128]{1,0:T(1,128)S(1)} %add.33), channel_id=1, source_target_pairs={{0,64},{32,96},{64,0},{96,32},{128,192},{160,224},{192,128},{224,1... | collective-permute-start | bytes 1544 | tf_op jit(solution)/shard_map/ppermute | solution.py:240
  17.4 3.9 %collective-permute-start.2 = (f32[1,128]{1,0:T(1,128)S(1)}, f32[1,128]{1,0:T(1,128)S(1)}, u32[]{:S(2)}, u32[]{:S(2)}) collective-permute-start(f32[1,128]{1,0:T(1,128)S(1)} %add.33), channel_id=1, source_target_pairs={{0,128},{32,160},{64,192},{96,224},{128,0},{160,32},{192,64},{224,... | collective-permute-start | bytes 1544 | tf_op jit(solution)/shard_map/ppermute | solution.py:240
  20.0 3.9 %collective-permute-start.3 = (f32[1,128]{1,0:T(1,128)S(1)}, f32[1,128]{1,0:T(1,128)S(1)}, u32[]{:S(2)}, u32[]{:S(2)}) collective-permute-start(f32[1,128]{1,0:T(1,128)S(1)} %add.33), channel_id=1, source_target_pairs={{0,192},{32,224},{64,128},{96,160},{128,64},{160,96},{192,0},{224,... | collective-permute-start | bytes 1544 | tf_op jit(solution)/shard_map/ppermute | solution.py:240
  23.9 4.0 %collective-permute-start.4 = (f32[1,128]{1,0:T(1,128)S(1)}, f32[1,128]{1,0:T(1,128)S(1)}, u32[]{:S(2)}, u32[]{:S(2)}) collective-permute-start(f32[1,128]{1,0:T(1,128)S(1)} %add_add_fusion.2), channel_id=1, source_target_pairs={{0,1},{1,0},{2,3},{3,2},{4,5},{5,4},{6,7},{7,6},{8,9},{9,8},{10,11... | collective-permute-start | bytes 1544 | tf_op jit(solution)/shard_map/ppermute | solution.py:240
  25.4 4.2 %collective-permute-start.5 = (f32[1,128]{1,0:T(1,128)S(1)}, f32[1,128]{1,0:T(1,128)S(1)}, u32[]{:S(2)}, u32[]{:S(2)}) collective-permute-start(f32[1,128]{1,0:T(1,128)S(1)} %add_add_fusion.2), channel_id=1, source_target_pairs={{0,2},{1,3},{2,0},{3,1},{4,6},{5,7},{6,4},{7,5},{8,10},{9,11},{10,... | collective-permute-start | bytes 1544 | tf_op jit(solution)/shard_map/ppermute | solution.py:240
  27.8 3.9 %collective-permute-start.6 = (f32[1,128]{1,0:T(1,128)S(1)}, f32[1,128]{1,0:T(1,128)S(1)}, u32[]{:S(2)}, u32[]{:S(2)}) collective-permute-start(f32[1,128]{1,0:T(1,128)S(1)} %add_add_fusion.2), channel_id=1, source_target_pairs={{0,3},{1,2},{2,1},{3,0},{4,7},{5,6},{6,5},{7,4},{8,11},{9,10},{10,... | collective-permute-start | bytes 1544 | tf_op jit(solution)/shard_map/ppermute | solution.py:240
  31.7 3.6 %collective-permute-start.7 = (f32[1,128]{1,0:T(1,128)S(1)}, f32[1,128]{1,0:T(1,128)S(1)}, u32[]{:S(2)}, u32[]{:S(2)}) collective-permute-start(f32[1,128]{1,0:T(1,128)S(1)} %add_add_fusion.1), channel_id=1, source_target_pairs={{0,4},{1,5},{2,6},{3,7},{4,0},{5,1},{6,2},{7,3},{8,12},{9,13},{10,... | collective-permute-start | bytes 1544 | tf_op jit(solution)/shard_map/ppermute | solution.py:240
  32.8 3.6 %collective-permute-start.8 = (f32[1,128]{1,0:T(1,128)S(1)}, f32[1,128]{1,0:T(1,128)S(1)}, u32[]{:S(2)}, u32[]{:S(2)}) collective-permute-start(f32[1,128]{1,0:T(1,128)S(1)} %add_add_fusion.1), channel_id=1, source_target_pairs={{0,8},{1,9},{2,10},{3,11},{4,12},{5,13},{6,14},{7,15},{8,0},{9,1},... | collective-permute-start | bytes 1544 | tf_op jit(solution)/shard_map/ppermute | solution.py:240
  34.7 4.5 %collective-permute-start.9 = (f32[1,128]{1,0:T(1,128)S(1)}, f32[1,128]{1,0:T(1,128)S(1)}, u32[]{:S(2)}, u32[]{:S(2)}) collective-permute-start(f32[1,128]{1,0:T(1,128)S(1)} %add_add_fusion.1), channel_id=1, source_target_pairs={{0,12},{1,13},{2,14},{3,15},{4,8},{5,9},{6,10},{7,11},{8,4},{9,5},... | collective-permute-start | bytes 1544 | tf_op jit(solution)/shard_map/ppermute | solution.py:240
  39.2 6.3 %collective-permute-start.10 = (f32[1,128]{1,0:T(1,128)S(1)}, f32[1,128]{1,0:T(1,128)S(1)}, u32[]{:S(2)}, u32[]{:S(2)}) collective-permute-start(f32[1,128]{1,0:T(1,128)S(1)} %add_add_fusion), channel_id=1, source_target_pairs={{0,16},{1,17},{2,18},{3,19},{4,20},{5,21},{6,22},{7,23},{8,24},{9,... | collective-permute-start | bytes 1544 | tf_op jit(solution)/shard_map/ppermute | solution.py:253
  72.0 13.8 %collective-permute-start.11 = (bf16[112,2048]{1,0:T(8,128)(2,1)S(1)}, bf16[112,2048]{1,0:T(8,128)(2,1)S(1)}, u32[]{:S(2)}, u32[]{:S(2)}) collective-permute-start(bf16[112,2048]{1,0:T(8,128)(2,1)S(1)} %get-tuple-element.23.refs_1_), channel_id=1, source_target_pairs={{0,64},{32,96},{64,128},{96,160},{128,192},{160,224},{192,0},{224,... | collective-permute-start | bytes 1376264 | tf_op jit(solution)/shard_map/ppermute | solution.py:185
  75.0 18.0 %collective-permute-start.19 = (bf16[112,2048]{1,0:T(8,128)(2,1)S(1)}, bf16[112,2048]{1,0:T(8,128)(2,1)S(1)}, u32[]{:S(2)}, u32[]{:S(2)}) collective-permute-start(bf16[112,2048]{1,0:T(8,128)(2,1)S(1)} %get-tuple-element.23.refs_1_), channel_id=1, source_target_pairs={{0,192},{32,224},{64,0},{96,32},{128,64},{160,96},{192,128},{224,1... | collective-permute-start | bytes 1376264 | tf_op jit(solution)/shard_map/ppermute | solution.py:185
  76.6 16.3 %collective-permute-start.21 = (bf16[112,2048]{1,0:T(8,128)(2,1)S(1)}, bf16[112,2048]{1,0:T(8,128)(2,1)S(1)}, u32[]{:S(2)}, u32[]{:S(2)}) collective-permute-start(bf16[112,2048]{1,0:T(8,128)(2,1)S(1)} %get-tuple-element.24.refs_8_), channel_id=1, source_target_pairs={{0,64},{32,96},{64,128},{96,160},{128,192},{160,224},{192,0},{224,... | collective-permute-start | bytes 1376264 | tf_op jit(solution)/shard_map/ppermute | solution.py:185
  76.6 17.6 %collective-permute-start.14 = (bf16[112,2048]{1,0:T(8,128)(2,1)S(1)}, bf16[112,2048]{1,0:T(8,128)(2,1)S(1)}, u32[]{:S(2)}, u32[]{:S(2)}) collective-permute-start(bf16[112,2048]{1,0:T(8,128)(2,1)S(1)} %get-tuple-element.24.refs_8_), channel_id=1, source_target_pairs={{0,192},{32,224},{64,0},{96,32},{128,64},{160,96},{192,128},{224,1... | collective-permute-start | bytes 1376264 | tf_op jit(solution)/shard_map/ppermute | solution.py:185
  79.3 16.5 %collective-permute-start.18 = (bf16[112,2048]{1,0:T(8,128)(2,1)S(1)}, bf16[112,2048]{1,0:T(8,128)(2,1)S(1)}, u32[]{:S(2)}, u32[]{:S(2)}) collective-permute-start(bf16[112,2048]{1,0:T(8,128)(2,1)S(1)} %get-tuple-element.23.refs_1_), channel_id=1, source_target_pairs={{0,32},{32,0},{64,96},{96,64},{128,160},{160,128},{192,224},{224,1... | collective-permute-start | bytes 1376264 | tf_op jit(solution)/shard_map/ppermute | solution.py:189
  85.8 15.7 %collective-permute-start.23 = (bf16[112,2048]{1,0:T(8,128)(2,1)S(1)}, bf16[112,2048]{1,0:T(8,128)(2,1)S(1)}, u32[]{:S(2)}, u32[]{:S(2)}) collective-permute-start(bf16[112,2048]{1,0:T(8,128)(2,1)S(1)} %get-tuple-element.24.refs_8_), channel_id=1, source_target_pairs={{0,32},{32,0},{64,96},{96,64},{128,160},{160,128},{192,224},{224,1... | collective-permute-start | bytes 1376264 | tf_op jit(solution)/shard_map/ppermute | solution.py:189
  92.9 8.7 %collective-permute-start.17 = (bf16[112,2048]{1,0:T(8,128)(2,1)S(1)}, bf16[112,2048]{1,0:T(8,128)(2,1)S(1)}, u32[]{:S(2)}, u32[]{:S(2)}) collective-permute-start(bf16[112,2048]{1,0:T(8,128)(2,1)S(1)} %collective-permute-done.11.refs_5_), channel_id=1, source_target_pairs={{0,32},{32,0},{64,96},{96,64},{128,160},{160,128},{192,224},{224,1... | collective-permute-start | bytes 1376264 | tf_op jit(solution)/shard_map/ppermute | solution.py:189
  92.9 9.1 %collective-permute-start.12 = (bf16[112,2048]{1,0:T(8,128)(2,1)S(1)}, bf16[112,2048]{1,0:T(8,128)(2,1)S(1)}, u32[]{:S(2)}, u32[]{:S(2)}) collective-permute-start(bf16[112,2048]{1,0:T(8,128)(2,1)S(1)} %collective-permute-done.11.refs_5_), channel_id=1, source_target_pairs={{0,64},{32,96},{64,128},{96,160},{128,192},{160,224},{192,0},{224,... | collective-permute-start | bytes 1376264 | tf_op jit(solution)/shard_map/ppermute | solution.py:185
  94.3 13.7 %collective-permute-start.15 = (bf16[112,2048]{1,0:T(8,128)(2,1)S(1)}, bf16[112,2048]{1,0:T(8,128)(2,1)S(1)}, u32[]{:S(2)}, u32[]{:S(2)}) collective-permute-start(bf16[112,2048]{1,0:T(8,128)(2,1)S(1)} %collective-permute-done.14.refs_10_), channel_id=1, source_target_pairs={{0,192},{32,224},{64,0},{96,32},{128,64},{160,96},{192,128},{224,1... | collective-permute-start | bytes 1376264 | tf_op jit(solution)/shard_map/ppermute | solution.py:185
  95.8 12.2 %collective-permute-start.20 = (bf16[112,2048]{1,0:T(8,128)(2,1)S(1)}, bf16[112,2048]{1,0:T(8,128)(2,1)S(1)}, u32[]{:S(2)}, u32[]{:S(2)}) collective-permute-start(bf16[112,2048]{1,0:T(8,128)(2,1)S(1)} %collective-permute-done.19.refs_3_), channel_id=1, source_target_pairs={{0,32},{32,0},{64,96},{96,64},{128,160},{160,128},{192,224},{224,1... | collective-permute-start | bytes 1376264 | tf_op jit(solution)/shard_map/ppermute | solution.py:189
  101.5 6.5 %collective-permute-start.22 = (bf16[112,2048]{1,0:T(8,128)(2,1)S(1)}, bf16[112,2048]{1,0:T(8,128)(2,1)S(1)}, u32[]{:S(2)}, u32[]{:S(2)}) collective-permute-start(bf16[112,2048]{1,0:T(8,128)(2,1)S(1)} %collective-permute-done.21.refs_12_), channel_id=1, source_target_pairs={{0,32},{32,0},{64,96},{96,64},{128,160},{160,128},{192,224},{224,1... | collective-permute-start | bytes 1376264 | tf_op jit(solution)/shard_map/ppermute | solution.py:189
  101.6 6.4 %collective-permute-start.24 = (bf16[112,2048]{1,0:T(8,128)(2,1)S(1)}, bf16[112,2048]{1,0:T(8,128)(2,1)S(1)}, u32[]{:S(2)}, u32[]{:S(2)}) collective-permute-start(bf16[112,2048]{1,0:T(8,128)(2,1)S(1)} %collective-permute-done.14.refs_10_), channel_id=1, source_target_pairs={{0,32},{32,0},{64,96},{96,64},{128,160},{160,128},{192,224},{224,1... | collective-permute-start | bytes 1376264 | tf_op jit(solution)/shard_map/ppermute | solution.py:189
  102.1 8.5 %collective-permute-start.13 = (bf16[112,2048]{1,0:T(8,128)(2,1)S(1)}, bf16[112,2048]{1,0:T(8,128)(2,1)S(1)}, u32[]{:S(2)}, u32[]{:S(2)}) collective-permute-start(bf16[112,2048]{1,0:T(8,128)(2,1)S(1)} %collective-permute-done.12.refs_0_), channel_id=1, source_target_pairs={{0,32},{32,0},{64,96},{96,64},{128,160},{160,128},{192,224},{224,1... | collective-permute-start | bytes 1376264 | tf_op jit(solution)/shard_map/ppermute | solution.py:189
  (3 other events, 64.9 us)

commit v5 on v4

--- a/solution.py
+++ b/solution.py
@@ -27,7 +27,7 @@
 FIRST = (-1, 0, 1, 2, 3, 6, 7)
 SECOND = (4, 5)
 COST = 2
-EXCHANGES = (("grp", 1, 2), ("grp", 2, 4), ("fsdp", 1, 4), ("fsdp", 4, 4), ("fsdp", 16, 2))
+EXCHANGES = (("grp", (1,)), ("grp", (2,)), ("grp", (6,)), ("fsdp", (1,)), ("fsdp", (3,)), ("fsdp", (4, 8, 12)), ("fsdp", (28,)))
 VMEM_LIMIT = 16 * 1024 * 1024
 
 
@@ -235,10 +235,9 @@
     )(slot_ids, *held, *extra)
 
 
-def total_over(partial, axis, apart, radix):
+def from_others(partial, axis, masks):
     size = lax.axis_size(axis)
-    others = [lax.ppermute(partial, axis, [(i, i ^ (apart * k)) for i in range(size)]) for k in range(1, radix)]
-    return sum(others, partial)
+    return [lax.ppermute(partial, axis, [(i, i ^ mask) for i in range(size)]) for mask in masks]
 
 
 def body(gradient, master, first_moment, second_moment, slot_expert):
@@ -246,13 +245,11 @@
     slot_ids = slot_expert.reshape(-1)
     grad_blocks, squares = pack(jnp.swapaxes(gradient[0], 0, 1))
     grad_here = lax.all_to_all(grad_blocks, "fsdp", 0, 0, tiled=True)
-    for axis, apart, radix in EXCHANGES[:-1]:
-        squares = total_over(squares, axis, apart, radix)
+    for axis, masks in EXCHANGES[:-1]:
+        squares = sum(from_others(squares, axis, masks), squares)
     turned, *states = turn(grad_here, master[0], first_moment[0], second_moment[0])
-    axis, apart, _ = EXCHANGES[-1]
-    others = lax.ppermute(squares, axis, [(i, i ^ apart) for i in range(lax.axis_size(axis))])
-    others, turned = lax.optimization_barrier((others, turned))
-    squares = squares + others
+    others, turned = lax.optimization_barrier((from_others(squares, *EXCHANGES[-1]), turned))
+    squares = sum(others, squares)
     weights = adam(entries, squares, turned, *states)
     columns = lax.all_to_all(weights, "fsdp", 0, 0, tiled=True)
     low, high = unpack(columns)

time: 112 us -> 110 us (0.982)
  starting transfers between devices: 63.1 us -> 60.9 us
  waiting for transfers between devices: 13.4 us -> 11.7 us
    ppermute x11 -> x9, waiting for transfers between devices: 13.3 us -> 10.3 us  [from_others(): lax.ppermute(partial, axis, [(i, i ^ mask) for i in range(size)])]
    ppermute x6, starting transfers between devices: 10.2 us -> 8.26 us  [shift(): lax.ppermute(array, 'grp', [(i, (i + 2 * chips) % size) for i in range(si...]
    ppermute x6, waiting for transfers between devices: 0.04 us -> 1.42 us  [shift(): lax.ppermute(array, 'grp', [(i, (i + 2 * chips) % size) for i in range(si...]
    ppermute x11 -> x9, starting transfers between devices: 15.3 us -> 15.5 us  [from_others(): lax.ppermute(partial, axis, [(i, i ^ mask) for i in range(size)])]
  transfers between devices with their start and end apart: 26 -> 24, of which waited for: 8 -> 9; matrix products, arithmetic and copies ran while one was open for 0% -> 0% of each run, Pallas kernels for 5% -> 5%
where the time goes in v5:
time: 110 us; the launch traced here: 109 us
  starting transfers between devices  60.9 us (55%)
  blocking collectives  24.9 us (23%)
  waiting for transfers between devices  11.7 us (11%)
  Pallas kernels  10.9 us (10%)
    ppermute x8, starting transfers between devices, other_core(): lax.ppermute(array, 'grp', [(i, i ^ 1) for i in range(lax.axis_size('grp'...  25.2 us
    all_to_all x1, blocking collectives, body(): columns = lax.all_to_all(weights, 'fsdp', 0, 0, tiled=True)  24.9 us
    ppermute x9, starting transfers between devices, from_others(): lax.ppermute(partial, axis, [(i, i ^ mask) for i in range(size)])  15.5 us
    all_to_all x1, starting transfers between devices, body(): grad_here = lax.all_to_all(grad_blocks, 'fsdp', 0, 0, tiled=True)  11.9 us
    ppermute x9, waiting for transfers between devices, from_others(): lax.ppermute(partial, axis, [(i, i ^ mask) for i in range(size)])  10.3 us
    ppermute x6, starting transfers between devices, shift(): lax.ppermute(array, 'grp', [(i, (i + 2 * chips) % size) for i in range(si...  8.26 us
    pallas_call x2, Pallas kernels, place(): pl.pallas_call(functools.partial(place_kernel, keys, halves), in_specs=[p...  3.2 us
    pallas_call x1, Pallas kernels, turn(): pl.pallas_call(turn_kernel, in_specs=[near, far, far, far], out_specs=[ne...  2.63 us
  transfers between devices with their start and end apart: 24, of which 9 were waited for; matrix products, arithmetic and copies ran while one was open for 0% of the time, Pallas kernels for 5%

profile of v5, /device:TPU:1, one launch (start us, length us, event | category | flops | bytes accessed | tf_op | source)
XLA Modules:
  0.0 108.7 jit_solution(2159977493209324946)
XLA Ops:
  0.0 2.3 %shard_map.55 = (bf16[32,112,128]{2,1,0:T(8,128)(2,1)}, f32[1,128]{1,0:T(1,128)S(1)}) custom-call(f32[224,2048]{1,0:T(8,128)} %bitcast.10), custom_call_target="tpu_custom_call" | custom-call | tf_op jit(solution)/shard_map/pallas_call | solution.py:71
  2.3 11.9 %all-to-all-start = ((bf16[32,112,128]{2,1,0:T(8,128)(2,1)}), bf16[32,112,128]{2,1,0:T(8,128)(2,1)S(1)}, u32[]{:S(2)}, u32[]{:S(2)}) async-start(bf16[32,112,128]{2,1,0:T(8,128)(2,1)} %get-tuple-element.16), calls=%async_computation | async-start | bytes 1835008 | tf_op jit(solution)/shard_map/all_to_all | solution.py:247
  16.1 1.3 %collective-permute-start.1 = (f32[1,128]{1,0:T(1,128)S(1)}, f32[1,128]{1,0:T(1,128)S(1)}, u32[]{:S(2)}, u32[]{:S(2)}) collective-permute-start(f32[1,128]{1,0:T(1,128)S(1)} %add.27), channel_id=1, source_target_pairs={{0,64},{32,96},{64,0},{96,32},{128,192},{160,224},{192,128},{224,1... | collective-permute-start | bytes 1544 | tf_op jit(solution)/shard_map/ppermute | solution.py:240
  17.4 1.4 %collective-permute-done.1 = f32[1,128]{1,0:T(1,128)S(1)} collective-permute-done((f32[1,128]{1,0:T(1,128)S(1)}, f32[1,128]{1,0:T(1,128)S(1)}, u32[]{:S(2)}, u32[]{:S(2)}) %collective-permute-start.1) | collective-permute-done | bytes 544 | tf_op jit(solution)/shard_map/ppermute | solution.py:240
  18.8 2.7 %collective-permute-start.2 = (f32[1,128]{1,0:T(1,128)S(1)}, f32[1,128]{1,0:T(1,128)S(1)}, u32[]{:S(2)}, u32[]{:S(2)}) collective-permute-start(f32[1,128]{1,0:T(1,128)S(1)} %add.28), channel_id=1, source_target_pairs={{0,192},{32,224},{64,128},{96,160},{128,64},{160,96},{192,0},{224,... | collective-permute-start | bytes 1544 | tf_op jit(solution)/shard_map/ppermute | solution.py:240
  22.7 1.5 %collective-permute-start.3 = (f32[1,128]{1,0:T(1,128)S(1)}, f32[1,128]{1,0:T(1,128)S(1)}, u32[]{:S(2)}, u32[]{:S(2)}) collective-permute-start(f32[1,128]{1,0:T(1,128)S(1)} %add.29), channel_id=1, source_target_pairs={{0,1},{1,0},{2,3},{3,2},{4,5},{5,4},{6,7},{7,6},{8,9},{9,8},{10,11... | collective-permute-start | bytes 1544 | tf_op jit(solution)/shard_map/ppermute | solution.py:240
  25.5 2.7 %collective-permute-start.4 = (f32[1,128]{1,0:T(1,128)S(1)}, f32[1,128]{1,0:T(1,128)S(1)}, u32[]{:S(2)}, u32[]{:S(2)}) collective-permute-start(f32[1,128]{1,0:T(1,128)S(1)} %add.30), channel_id=1, source_target_pairs={{0,3},{1,2},{2,1},{3,0},{4,7},{5,6},{6,5},{7,4},{8,11},{9,10},{10,... | collective-permute-start | bytes 1544 | tf_op jit(solution)/shard_map/ppermute | solution.py:240
  29.4 1.4 %collective-permute-start.5 = (f32[1,128]{1,0:T(1,128)S(1)}, f32[1,128]{1,0:T(1,128)S(1)}, u32[]{:S(2)}, u32[]{:S(2)}) collective-permute-start(f32[1,128]{1,0:T(1,128)S(1)} %add.31), channel_id=1, source_target_pairs={{0,4},{1,5},{2,6},{3,7},{4,0},{5,1},{6,2},{7,3},{8,12},{9,13},{10,... | collective-permute-start | bytes 1544 | tf_op jit(solution)/shard_map/ppermute | solution.py:240
  30.9 2.1 %collective-permute-start.6 = (f32[1,128]{1,0:T(1,128)S(1)}, f32[1,128]{1,0:T(1,128)S(1)}, u32[]{:S(2)}, u32[]{:S(2)}) collective-permute-start(f32[1,128]{1,0:T(1,128)S(1)} %add.31), channel_id=1, source_target_pairs={{0,8},{1,9},{2,10},{3,11},{4,12},{5,13},{6,14},{7,15},{8,0},{9,1},... | collective-permute-start | bytes 1544 | tf_op jit(solution)/shard_map/ppermute | solution.py:240
  34.4 3.0 %collective-permute-done.7 = f32[1,128]{1,0:T(1,128)S(1)} collective-permute-done((f32[1,128]{1,0:T(1,128)S(1)}, f32[1,128]{1,0:T(1,128)S(1)}, u32[]{:S(2)}, u32[]{:S(2)}) %collective-permute-start.7) | collective-permute-done | bytes 544 | tf_op jit(solution)/shard_map/ppermute | solution.py:240
  37.4 2.7 %collective-permute-start.8 = (f32[1,128]{1,0:T(1,128)S(1)}, f32[1,128]{1,0:T(1,128)S(1)}, u32[]{:S(2)}, u32[]{:S(2)}) collective-permute-start(f32[1,128]{1,0:T(1,128)S(1)} %add_add_fusion), channel_id=1, source_target_pairs={{0,28},{1,29},{2,30},{3,31},{4,24},{5,25},{6,26},{7,27},{8,20},{9,... | collective-permute-start | bytes 1544 | tf_op jit(solution)/shard_map/ppermute | solution.py:240
  40.1 2.6 %shard_map.56 = (f32[28,128,128]{2,1,0:T(8,128)S(1)}, f32[64,7168]{1,0:T(8,128)S(1)}, f32[64,7168]{1,0:T(8,128)S(1)}, f32[64,7168]{1,0:T(8,128)S(1)}) custom-call(bf16[32,112,128]{2,1,0:T(8,128)(2,1)S(1)} %all-to-all-done.grad_ref, f32[64,7168]{1,0:T(8,128)} %bitcast.11, f32[64,7168]{1,0:T(8,128)} %bitcast.12, f32[64,7168]{1,0:T(8,128)} %bitcast.13), custom_call_target="tpu_custom_call" | custom-call | tf_op jit(solution)/shard_map/pallas_call | solution.py:109
  42.8 2.1 %shard_map.57 = bf16[32,112,128]{2,1,0:T(8,128)(2,1)S(1)} custom-call(f32[1,128]{1,0:T(1,128)S(1)} %add.35.squares_ref, f32[28,128,128]{2,1,0:T(8,128)S(1)} %get-tuple-element.19.turned_ref, f32[64,7168]{1,0:T(8,128)S(1)} %get-tuple-element.20.master_ref, f32[64,7168]{1,0:T(8,128)S(1)} %get-tuple-element.21.first_ref, ...), custom_call_target="tpu_custom_call" | custom-call | tf_op jit(solution)/shard_map/pallas_call | solution.py:150
  44.9 24.9 %all_to_all.10.block_ref = bf16[32,112,128]{2,1,0:T(8,128)(2,1)S(1)} all-to-all(bf16[32,112,128]{2,1,0:T(8,128)(2,1)S(1)} %shard_map.57), channel_id=1, replica_groups=mesh['grp'=8,'fsdp'=32] {'fsdp'}, dimensions={0} | all-to-all | bytes 1835008 | tf_op jit(solution)/shard_map/all_to_all | solution.py:254
  70.4 2.2 %collective-permute-start.9 = (bf16[112,2048]{1,0:T(8,128)(2,1)S(1)}, bf16[112,2048]{1,0:T(8,128)(2,1)S(1)}, u32[]{:S(2)}, u32[]{:S(2)}) collective-permute-start(bf16[112,2048]{1,0:T(8,128)(2,1)S(1)} %get-tuple-element.23.refs_1_), channel_id=1, source_target_pairs={{0,64},{32,96},{64,128},{96,160},{128,192},{160,224},{192,0},{224,... | collective-permute-start | bytes 1376264 | tf_op jit(solution)/shard_map/ppermute | solution.py:185
  74.1 1.9 %collective-permute-start.12 = (bf16[112,2048]{1,0:T(8,128)(2,1)S(1)}, bf16[112,2048]{1,0:T(8,128)(2,1)S(1)}, u32[]{:S(2)}, u32[]{:S(2)}) collective-permute-start(bf16[112,2048]{1,0:T(8,128)(2,1)S(1)} %get-tuple-element.24.refs_8_), channel_id=1, source_target_pairs={{0,192},{32,224},{64,0},{96,32},{128,64},{160,96},{192,128},{224,1... | collective-permute-start | bytes 1376264 | tf_op jit(solution)/shard_map/ppermute | solution.py:185
  75.9 8.2 %collective-permute-start.16 = (bf16[112,2048]{1,0:T(8,128)(2,1)S(1)}, bf16[112,2048]{1,0:T(8,128)(2,1)S(1)}, u32[]{:S(2)}, u32[]{:S(2)}) collective-permute-start(bf16[112,2048]{1,0:T(8,128)(2,1)S(1)} %get-tuple-element.23.refs_1_), channel_id=1, source_target_pairs={{0,32},{32,0},{64,96},{96,64},{128,160},{160,128},{192,224},{224,1... | collective-permute-start | bytes 1376264 | tf_op jit(solution)/shard_map/ppermute | solution.py:189
  84.2 5.4 %collective-permute-start.21 = (bf16[112,2048]{1,0:T(8,128)(2,1)S(1)}, bf16[112,2048]{1,0:T(8,128)(2,1)S(1)}, u32[]{:S(2)}, u32[]{:S(2)}) collective-permute-start(bf16[112,2048]{1,0:T(8,128)(2,1)S(1)} %get-tuple-element.24.refs_8_), channel_id=1, source_target_pairs={{0,32},{32,0},{64,96},{96,64},{128,160},{160,128},{192,224},{224,1... | collective-permute-start | bytes 1376264 | tf_op jit(solution)/shard_map/ppermute | solution.py:189
  90.5 1.3 %collective-permute-start.10 = (bf16[112,2048]{1,0:T(8,128)(2,1)S(1)}, bf16[112,2048]{1,0:T(8,128)(2,1)S(1)}, u32[]{:S(2)}, u32[]{:S(2)}) collective-permute-start(bf16[112,2048]{1,0:T(8,128)(2,1)S(1)} %collective-permute-done.9.refs_5_), channel_id=1, source_target_pairs={{0,64},{32,96},{64,128},{96,160},{128,192},{160,224},{192,0},{224,... | collective-permute-start | bytes 1376264 | tf_op jit(solution)/shard_map/ppermute | solution.py:185
  91.8 1.4 %collective-permute-start.13 = (bf16[112,2048]{1,0:T(8,128)(2,1)S(1)}, bf16[112,2048]{1,0:T(8,128)(2,1)S(1)}, u32[]{:S(2)}, u32[]{:S(2)}) collective-permute-start(bf16[112,2048]{1,0:T(8,128)(2,1)S(1)} %collective-permute-done.12.refs_10_), channel_id=1, source_target_pairs={{0,192},{32,224},{64,0},{96,32},{128,64},{160,96},{192,128},{224,1... | collective-permute-start | bytes 1376264 | tf_op jit(solution)/shard_map/ppermute | solution.py:185
  93.1 4.6 %collective-permute-start.18 = (bf16[112,2048]{1,0:T(8,128)(2,1)S(1)}, bf16[112,2048]{1,0:T(8,128)(2,1)S(1)}, u32[]{:S(2)}, u32[]{:S(2)}) collective-permute-start(bf16[112,2048]{1,0:T(8,128)(2,1)S(1)} %collective-permute-done.17.refs_3_), channel_id=1, source_target_pairs={{0,32},{32,0},{64,96},{96,64},{128,160},{160,128},{192,224},{224,1... | collective-permute-start | bytes 1376264 | tf_op jit(solution)/shard_map/ppermute | solution.py:189
  98.2 1.4 %collective-permute-done.10.refs_0_ = bf16[112,2048]{1,0:T(8,128)(2,1)S(1)} collective-permute-done((bf16[112,2048]{1,0:T(8,128)(2,1)S(1)}, bf16[112,2048]{1,0:T(8,128)(2,1)S(1)}, u32[]{:S(2)}, u32[]{:S(2)}) %collective-permute-start.10) | collective-permute-done | bytes 458784 | tf_op jit(solution)/shard_map/ppermute | solution.py:185
  99.7 4.9 %collective-permute-start.11 = (bf16[112,2048]{1,0:T(8,128)(2,1)S(1)}, bf16[112,2048]{1,0:T(8,128)(2,1)S(1)}, u32[]{:S(2)}, u32[]{:S(2)}) collective-permute-start(bf16[112,2048]{1,0:T(8,128)(2,1)S(1)} %collective-permute-done.10.refs_0_), channel_id=1, source_target_pairs={{0,32},{32,0},{64,96},{96,64},{128,160},{160,128},{192,224},{224,1... | collective-permute-start | bytes 1376264 | tf_op jit(solution)/shard_map/ppermute | solution.py:189
  105.3 2.5 %shard_map.59.refs_4_ = bf16[4,224,2048]{2,1,0:T(8,128)(2,1)} custom-call(s32[4]{0:T(128)S(1)} %bitcast.8, bf16[112,2048]{1,0:T(8,128)(2,1)S(1)} %collective-permute-done.15.refs_0_.refs_6_, bf16[112,2048]{1,0:T(8,128)(2,1)S(1)} %get-tuple-element.23.refs_1_, bf16[112,2048]{1,0:T(8,128)(2,1)S(1)} %collective-permute-done.16.refs_2_, ...), custom_call_target="tpu_custom_call" | custom-call | bytes 6422528 | tf_op jit(solution)/shard_map/pallas_call | solution.py:226
  (40 shorter events, 11.9 us)
Async XLA Ops:
  2.3 37.8 %all-to-all-start = ((bf16[32,112,128]{2,1,0:T(8,128)(2,1)}), bf16[32,112,128]{2,1,0:T(8,128)(2,1)S(1)}, u32[]{:S(2)}, u32[]{:S(2)}) async-start(bf16[32,112,128]{2,1,0:T(8,128)(2,1)} %get-tuple-element.16), calls=%async_computation | async-start | bytes 1835008 | tf_op jit(solution)/shard_map/all_to_all | solution.py:247
  14.2 1.9 %collective-permute-start = (f32[1,128]{1,0:T(1,128)S(1)}, f32[1,128]{1,0:T(1,128)S(1)}, u32[]{:S(2)}, u32[]{:S(2)}) collective-permute-start(f32[1,128]{1,0:T(1,128)S(1)} %get-tuple-element.15), channel_id=1, source_target_pairs={{0,32},{32,0},{64,96},{96,64},{128,160},{160,128},{192,224},{224,1... | collective-permute-start | bytes 1544 | tf_op jit(solution)/shard_map/ppermute | solution.py:240
  16.1 2.7 %collective-permute-start.1 = (f32[1,128]{1,0:T(1,128)S(1)}, f32[1,128]{1,0:T(1,128)S(1)}, u32[]{:S(2)}, u32[]{:S(2)}) collective-permute-start(f32[1,128]{1,0:T(1,128)S(1)} %add.27), channel_id=1, source_target_pairs={{0,64},{32,96},{64,0},{96,32},{128,192},{160,224},{192,128},{224,1... | collective-permute-start | bytes 1544 | tf_op jit(solution)/shard_map/ppermute | solution.py:240
  18.8 4.0 %collective-permute-start.2 = (f32[1,128]{1,0:T(1,128)S(1)}, f32[1,128]{1,0:T(1,128)S(1)}, u32[]{:S(2)}, u32[]{:S(2)}) collective-permute-start(f32[1,128]{1,0:T(1,128)S(1)} %add.28), channel_id=1, source_target_pairs={{0,192},{32,224},{64,128},{96,160},{128,64},{160,96},{192,0},{224,... | collective-permute-start | bytes 1544 | tf_op jit(solution)/shard_map/ppermute | solution.py:240
  22.7 2.7 %collective-permute-start.3 = (f32[1,128]{1,0:T(1,128)S(1)}, f32[1,128]{1,0:T(1,128)S(1)}, u32[]{:S(2)}, u32[]{:S(2)}) collective-permute-start(f32[1,128]{1,0:T(1,128)S(1)} %add.29), channel_id=1, source_target_pairs={{0,1},{1,0},{2,3},{3,2},{4,5},{5,4},{6,7},{7,6},{8,9},{9,8},{10,11... | collective-permute-start | bytes 1544 | tf_op jit(solution)/shard_map/ppermute | solution.py:240
  25.5 4.0 %collective-permute-start.4 = (f32[1,128]{1,0:T(1,128)S(1)}, f32[1,128]{1,0:T(1,128)S(1)}, u32[]{:S(2)}, u32[]{:S(2)}) collective-permute-start(f32[1,128]{1,0:T(1,128)S(1)} %add.30), channel_id=1, source_target_pairs={{0,3},{1,2},{2,1},{3,0},{4,7},{5,6},{6,5},{7,4},{8,11},{9,10},{10,... | collective-permute-start | bytes 1544 | tf_op jit(solution)/shard_map/ppermute | solution.py:240
  29.4 4.4 %collective-permute-start.5 = (f32[1,128]{1,0:T(1,128)S(1)}, f32[1,128]{1,0:T(1,128)S(1)}, u32[]{:S(2)}, u32[]{:S(2)}) collective-permute-start(f32[1,128]{1,0:T(1,128)S(1)} %add.31), channel_id=1, source_target_pairs={{0,4},{1,5},{2,6},{3,7},{4,0},{5,1},{6,2},{7,3},{8,12},{9,13},{10,... | collective-permute-start | bytes 1544 | tf_op jit(solution)/shard_map/ppermute | solution.py:240
  30.9 3.5 %collective-permute-start.6 = (f32[1,128]{1,0:T(1,128)S(1)}, f32[1,128]{1,0:T(1,128)S(1)}, u32[]{:S(2)}, u32[]{:S(2)}) collective-permute-start(f32[1,128]{1,0:T(1,128)S(1)} %add.31), channel_id=1, source_target_pairs={{0,8},{1,9},{2,10},{3,11},{4,12},{5,13},{6,14},{7,15},{8,0},{9,1},... | collective-permute-start | bytes 1544 | tf_op jit(solution)/shard_map/ppermute | solution.py:240
  32.9 4.5 %collective-permute-start.7 = (f32[1,128]{1,0:T(1,128)S(1)}, f32[1,128]{1,0:T(1,128)S(1)}, u32[]{:S(2)}, u32[]{:S(2)}) collective-permute-start(f32[1,128]{1,0:T(1,128)S(1)} %add.31), channel_id=1, source_target_pairs={{0,12},{1,13},{2,14},{3,15},{4,8},{5,9},{6,10},{7,11},{8,4},{9,5},... | collective-permute-start | bytes 1544 | tf_op jit(solution)/shard_map/ppermute | solution.py:240
  37.4 5.3 %collective-permute-start.8 = (f32[1,128]{1,0:T(1,128)S(1)}, f32[1,128]{1,0:T(1,128)S(1)}, u32[]{:S(2)}, u32[]{:S(2)}) collective-permute-start(f32[1,128]{1,0:T(1,128)S(1)} %add_add_fusion), channel_id=1, source_target_pairs={{0,28},{1,29},{2,30},{3,31},{4,24},{5,25},{6,26},{7,27},{8,20},{9,... | collective-permute-start | bytes 1544 | tf_op jit(solution)/shard_map/ppermute | solution.py:240
  70.4 13.8 %collective-permute-start.9 = (bf16[112,2048]{1,0:T(8,128)(2,1)S(1)}, bf16[112,2048]{1,0:T(8,128)(2,1)S(1)}, u32[]{:S(2)}, u32[]{:S(2)}) collective-permute-start(bf16[112,2048]{1,0:T(8,128)(2,1)S(1)} %get-tuple-element.23.refs_1_), channel_id=1, source_target_pairs={{0,64},{32,96},{64,128},{96,160},{128,192},{160,224},{192,0},{224,... | collective-permute-start | bytes 1376264 | tf_op jit(solution)/shard_map/ppermute | solution.py:185
  72.6 17.0 %collective-permute-start.17 = (bf16[112,2048]{1,0:T(8,128)(2,1)S(1)}, bf16[112,2048]{1,0:T(8,128)(2,1)S(1)}, u32[]{:S(2)}, u32[]{:S(2)}) collective-permute-start(bf16[112,2048]{1,0:T(8,128)(2,1)S(1)} %get-tuple-element.23.refs_1_), channel_id=1, source_target_pairs={{0,192},{32,224},{64,0},{96,32},{128,64},{160,96},{192,128},{224,1... | collective-permute-start | bytes 1376264 | tf_op jit(solution)/shard_map/ppermute | solution.py:185
  73.3 17.2 %collective-permute-start.19 = (bf16[112,2048]{1,0:T(8,128)(2,1)S(1)}, bf16[112,2048]{1,0:T(8,128)(2,1)S(1)}, u32[]{:S(2)}, u32[]{:S(2)}) collective-permute-start(bf16[112,2048]{1,0:T(8,128)(2,1)S(1)} %get-tuple-element.24.refs_8_), channel_id=1, source_target_pairs={{0,64},{32,96},{64,128},{96,160},{128,192},{160,224},{192,0},{224,... | collective-permute-start | bytes 1376264 | tf_op jit(solution)/shard_map/ppermute | solution.py:185
  74.1 17.7 %collective-permute-start.12 = (bf16[112,2048]{1,0:T(8,128)(2,1)S(1)}, bf16[112,2048]{1,0:T(8,128)(2,1)S(1)}, u32[]{:S(2)}, u32[]{:S(2)}) collective-permute-start(bf16[112,2048]{1,0:T(8,128)(2,1)S(1)} %get-tuple-element.24.refs_8_), channel_id=1, source_target_pairs={{0,192},{32,224},{64,0},{96,32},{128,64},{160,96},{192,128},{224,1... | collective-permute-start | bytes 1376264 | tf_op jit(solution)/shard_map/ppermute | solution.py:185
  75.9 17.2 %collective-permute-start.16 = (bf16[112,2048]{1,0:T(8,128)(2,1)S(1)}, bf16[112,2048]{1,0:T(8,128)(2,1)S(1)}, u32[]{:S(2)}, u32[]{:S(2)}) collective-permute-start(bf16[112,2048]{1,0:T(8,128)(2,1)S(1)} %get-tuple-element.23.refs_1_), channel_id=1, source_target_pairs={{0,32},{32,0},{64,96},{96,64},{128,160},{160,128},{192,224},{224,1... | collective-permute-start | bytes 1376264 | tf_op jit(solution)/shard_map/ppermute | solution.py:189
  84.2 13.5 %collective-permute-start.21 = (bf16[112,2048]{1,0:T(8,128)(2,1)S(1)}, bf16[112,2048]{1,0:T(8,128)(2,1)S(1)}, u32[]{:S(2)}, u32[]{:S(2)}) collective-permute-start(bf16[112,2048]{1,0:T(8,128)(2,1)S(1)} %get-tuple-element.24.refs_8_), channel_id=1, source_target_pairs={{0,32},{32,0},{64,96},{96,64},{128,160},{160,128},{192,224},{224,1... | collective-permute-start | bytes 1376264 | tf_op jit(solution)/shard_map/ppermute | solution.py:189
  89.6 8.3 %collective-permute-start.15 = (bf16[112,2048]{1,0:T(8,128)(2,1)S(1)}, bf16[112,2048]{1,0:T(8,128)(2,1)S(1)}, u32[]{:S(2)}, u32[]{:S(2)}) collective-permute-start(bf16[112,2048]{1,0:T(8,128)(2,1)S(1)} %collective-permute-done.9.refs_5_), channel_id=1, source_target_pairs={{0,32},{32,0},{64,96},{96,64},{128,160},{160,128},{192,224},{224,1... | collective-permute-start | bytes 1376264 | tf_op jit(solution)/shard_map/ppermute | solution.py:189
  90.5 9.2 %collective-permute-start.10 = (bf16[112,2048]{1,0:T(8,128)(2,1)S(1)}, bf16[112,2048]{1,0:T(8,128)(2,1)S(1)}, u32[]{:S(2)}, u32[]{:S(2)}) collective-permute-start(bf16[112,2048]{1,0:T(8,128)(2,1)S(1)} %collective-permute-done.9.refs_5_), channel_id=1, source_target_pairs={{0,64},{32,96},{64,128},{96,160},{128,192},{160,224},{192,0},{224,... | collective-permute-start | bytes 1376264 | tf_op jit(solution)/shard_map/ppermute | solution.py:185
  91.8 12.8 %collective-permute-start.13 = (bf16[112,2048]{1,0:T(8,128)(2,1)S(1)}, bf16[112,2048]{1,0:T(8,128)(2,1)S(1)}, u32[]{:S(2)}, u32[]{:S(2)}) collective-permute-start(bf16[112,2048]{1,0:T(8,128)(2,1)S(1)} %collective-permute-done.12.refs_10_), channel_id=1, source_target_pairs={{0,192},{32,224},{64,0},{96,32},{128,64},{160,96},{192,128},{224,1... | collective-permute-start | bytes 1376264 | tf_op jit(solution)/shard_map/ppermute | solution.py:185
  93.1 12.1 %collective-permute-start.18 = (bf16[112,2048]{1,0:T(8,128)(2,1)S(1)}, bf16[112,2048]{1,0:T(8,128)(2,1)S(1)}, u32[]{:S(2)}, u32[]{:S(2)}) collective-permute-start(bf16[112,2048]{1,0:T(8,128)(2,1)S(1)} %collective-permute-done.17.refs_3_), channel_id=1, source_target_pairs={{0,32},{32,0},{64,96},{96,64},{128,160},{160,128},{192,224},{224,1... | collective-permute-start | bytes 1376264 | tf_op jit(solution)/shard_map/ppermute | solution.py:189
  97.7 7.6 %collective-permute-start.20 = (bf16[112,2048]{1,0:T(8,128)(2,1)S(1)}, bf16[112,2048]{1,0:T(8,128)(2,1)S(1)}, u32[]{:S(2)}, u32[]{:S(2)}) collective-permute-start(bf16[112,2048]{1,0:T(8,128)(2,1)S(1)} %collective-permute-done.19.refs_12_), channel_id=1, source_target_pairs={{0,32},{32,0},{64,96},{96,64},{128,160},{160,128},{192,224},{224,1... | collective-permute-start | bytes 1376264 | tf_op jit(solution)/shard_map/ppermute | solution.py:189
  97.8 7.5 %collective-permute-start.22 = (bf16[112,2048]{1,0:T(8,128)(2,1)S(1)}, bf16[112,2048]{1,0:T(8,128)(2,1)S(1)}, u32[]{:S(2)}, u32[]{:S(2)}) collective-permute-start(bf16[112,2048]{1,0:T(8,128)(2,1)S(1)} %collective-permute-done.12.refs_10_), channel_id=1, source_target_pairs={{0,32},{32,0},{64,96},{96,64},{128,160},{160,128},{192,224},{224,1... | collective-permute-start | bytes 1376264 | tf_op jit(solution)/shard_map/ppermute | solution.py:189
  99.7 8.2 %collective-permute-start.11 = (bf16[112,2048]{1,0:T(8,128)(2,1)S(1)}, bf16[112,2048]{1,0:T(8,128)(2,1)S(1)}, u32[]{:S(2)}, u32[]{:S(2)}) collective-permute-start(bf16[112,2048]{1,0:T(8,128)(2,1)S(1)} %collective-permute-done.10.refs_0_), channel_id=1, source_target_pairs={{0,32},{32,0},{64,96},{96,64},{128,160},{160,128},{192,224},{224,1... | collective-permute-start | bytes 1376264 | tf_op jit(solution)/shard_map/ppermute | solution.py:189
  104.6 3.2 %collective-permute-start.14 = (bf16[112,2048]{1,0:T(8,128)(2,1)S(1)}, bf16[112,2048]{1,0:T(8,128)(2,1)S(1)}, u32[]{:S(2)}, u32[]{:S(2)}) collective-permute-start(bf16[112,2048]{1,0:T(8,128)(2,1)S(1)} %collective-permute-done.13.refs_2_), channel_id=1, source_target_pairs={{0,32},{32,0},{64,96},{96,64},{128,160},{160,128},{192,224},{224,1... | collective-permute-start | bytes 1376264 | tf_op jit(solution)/shard_map/ppermute | solution.py:189
  (1 other events, 60.5 us)

commit v6 on v5

--- a/solution.py
+++ b/solution.py
@@ -27,7 +27,7 @@
 FIRST = (-1, 0, 1, 2, 3, 6, 7)
 SECOND = (4, 5)
 COST = 2
-EXCHANGES = (("grp", (1,)), ("grp", (2,)), ("grp", (6,)), ("fsdp", (1,)), ("fsdp", (3,)), ("fsdp", (4, 8, 12)), ("fsdp", (28,)))
+EXCHANGES = (("grp", (1,)), ("grp", (2,)), ("grp", (6,)), ("fsdp", (1,)), ("fsdp", (3,)), ("fsdp", (4, 28, 24)), ("fsdp", (8,)))
 VMEM_LIMIT = 16 * 1024 * 1024
 
 

time: 110 us -> 107 us (0.973); the launches traced: 109 us -> 107 us
  blocking collectives: 24.9 us -> 22.3 us
  starting transfers between devices: 60.9 us -> 62.3 us
    all_to_all x1, blocking collectives: 24.9 us -> 22.3 us  [body(): columns = lax.all_to_all(weights, 'fsdp', 0, 0, tiled=True)]
    ppermute x9, starting transfers between devices: 15.5 us -> 16.8 us  [from_others(): lax.ppermute(partial, axis, [(i, i ^ mask) for i in range(size)])]
  transfers between devices with their start and end apart: 24 -> 24, of which waited for: 9 -> 8; matrix products, arithmetic and copies ran while one was open for 0% -> 0% of each run, Pallas kernels for 5% -> 5%
where the time goes in v6:
time: 107 us
  starting transfers between devices  62.3 us (58%)
  blocking collectives  22.3 us (21%)
  Pallas kernels  11.5 us (11%)
  waiting for transfers between devices  10.8 us (10%)
    ppermute x8, starting transfers between devices, other_core(): lax.ppermute(array, 'grp', [(i, i ^ 1) for i in range(lax.axis_size('grp'...  25.4 us
    all_to_all x1, blocking collectives, body(): columns = lax.all_to_all(weights, 'fsdp', 0, 0, tiled=True)  22.3 us
    ppermute x9, starting transfers between devices, from_others(): lax.ppermute(partial, axis, [(i, i ^ mask) for i in range(size)])  16.8 us
    all_to_all x1, starting transfers between devices, body(): grad_here = lax.all_to_all(grad_blocks, 'fsdp', 0, 0, tiled=True)  11.9 us
    ppermute x9, waiting for transfers between devices, from_others(): lax.ppermute(partial, axis, [(i, i ^ mask) for i in range(size)])  9.91 us
    ppermute x6, starting transfers between devices, shift(): lax.ppermute(array, 'grp', [(i, (i + 2 * chips) % size) for i in range(si...  8.26 us
    pallas_call x2, Pallas kernels, place(): pl.pallas_call(functools.partial(place_kernel, keys, halves), in_specs=[p...  3.8 us
    pallas_call x1, Pallas kernels, turn(): pl.pallas_call(turn_kernel, in_specs=[near, far, far, far], out_specs=[ne...  2.63 us
  transfers between devices with their start and end apart: 24, of which 8 were waited for; matrix products, arithmetic and copies ran while one was open for 0% of the time, Pallas kernels for 5%

profile of v6, /device:TPU:1, one launch (start us, length us, event | category | flops | bytes accessed | tf_op | source)
XLA Modules:
  0.0 107.1 jit_solution(18356517451993584571)
XLA Ops:
  0.0 2.3 %shard_map.55 = (bf16[32,112,128]{2,1,0:T(8,128)(2,1)}, f32[1,128]{1,0:T(1,128)S(1)}) custom-call(f32[224,2048]{1,0:T(8,128)} %bitcast.10), custom_call_target="tpu_custom_call" | custom-call | tf_op jit(solution)/shard_map/pallas_call | solution.py:71
  2.3 11.9 %all-to-all-start = ((bf16[32,112,128]{2,1,0:T(8,128)(2,1)}), bf16[32,112,128]{2,1,0:T(8,128)(2,1)S(1)}, u32[]{:S(2)}, u32[]{:S(2)}) async-start(bf16[32,112,128]{2,1,0:T(8,128)(2,1)} %get-tuple-element.16), calls=%async_computation | async-start | bytes 1835008 | tf_op jit(solution)/shard_map/all_to_all | solution.py:247
  16.1 1.3 %collective-permute-start.1 = (f32[1,128]{1,0:T(1,128)S(1)}, f32[1,128]{1,0:T(1,128)S(1)}, u32[]{:S(2)}, u32[]{:S(2)}) collective-permute-start(f32[1,128]{1,0:T(1,128)S(1)} %add.27), channel_id=1, source_target_pairs={{0,64},{32,96},{64,0},{96,32},{128,192},{160,224},{192,128},{224,1... | collective-permute-start | bytes 1544 | tf_op jit(solution)/shard_map/ppermute | solution.py:240
  17.4 1.4 %collective-permute-done.1 = f32[1,128]{1,0:T(1,128)S(1)} collective-permute-done((f32[1,128]{1,0:T(1,128)S(1)}, f32[1,128]{1,0:T(1,128)S(1)}, u32[]{:S(2)}, u32[]{:S(2)}) %collective-permute-start.1) | collective-permute-done | bytes 544 | tf_op jit(solution)/shard_map/ppermute | solution.py:240
  18.8 2.7 %collective-permute-start.2 = (f32[1,128]{1,0:T(1,128)S(1)}, f32[1,128]{1,0:T(1,128)S(1)}, u32[]{:S(2)}, u32[]{:S(2)}) collective-permute-start(f32[1,128]{1,0:T(1,128)S(1)} %add.28), channel_id=1, source_target_pairs={{0,192},{32,224},{64,128},{96,160},{128,64},{160,96},{192,0},{224,... | collective-permute-start | bytes 1544 | tf_op jit(solution)/shard_map/ppermute | solution.py:240
  22.7 1.5 %collective-permute-start.3 = (f32[1,128]{1,0:T(1,128)S(1)}, f32[1,128]{1,0:T(1,128)S(1)}, u32[]{:S(2)}, u32[]{:S(2)}) collective-permute-start(f32[1,128]{1,0:T(1,128)S(1)} %add.29), channel_id=1, source_target_pairs={{0,1},{1,0},{2,3},{3,2},{4,5},{5,4},{6,7},{7,6},{8,9},{9,8},{10,11... | collective-permute-start | bytes 1544 | tf_op jit(solution)/shard_map/ppermute | solution.py:240
  25.5 2.7 %collective-permute-start.4 = (f32[1,128]{1,0:T(1,128)S(1)}, f32[1,128]{1,0:T(1,128)S(1)}, u32[]{:S(2)}, u32[]{:S(2)}) collective-permute-start(f32[1,128]{1,0:T(1,128)S(1)} %add.30), channel_id=1, source_target_pairs={{0,3},{1,2},{2,1},{3,0},{4,7},{5,6},{6,5},{7,4},{8,11},{9,10},{10,... | collective-permute-start | bytes 1544 | tf_op jit(solution)/shard_map/ppermute | solution.py:240
  29.4 1.4 %collective-permute-start.5 = (f32[1,128]{1,0:T(1,128)S(1)}, f32[1,128]{1,0:T(1,128)S(1)}, u32[]{:S(2)}, u32[]{:S(2)}) collective-permute-start(f32[1,128]{1,0:T(1,128)S(1)} %add.31), channel_id=1, source_target_pairs={{0,4},{1,5},{2,6},{3,7},{4,0},{5,1},{6,2},{7,3},{8,12},{9,13},{10,... | collective-permute-start | bytes 1544 | tf_op jit(solution)/shard_map/ppermute | solution.py:240
  30.9 2.4 %collective-permute-start.6 = (f32[1,128]{1,0:T(1,128)S(1)}, f32[1,128]{1,0:T(1,128)S(1)}, u32[]{:S(2)}, u32[]{:S(2)}) collective-permute-start(f32[1,128]{1,0:T(1,128)S(1)} %add.31), channel_id=1, source_target_pairs={{0,28},{1,29},{2,30},{3,31},{4,24},{5,25},{6,26},{7,27},{8,20},{9,... | collective-permute-start | bytes 1544 | tf_op jit(solution)/shard_map/ppermute | solution.py:240
  34.6 3.7 %collective-permute-done.7 = f32[1,128]{1,0:T(1,128)S(1)} collective-permute-done((f32[1,128]{1,0:T(1,128)S(1)}, f32[1,128]{1,0:T(1,128)S(1)}, u32[]{:S(2)}, u32[]{:S(2)}) %collective-permute-start.7) | collective-permute-done | bytes 544 | tf_op jit(solution)/shard_map/ppermute | solution.py:240
  38.2 2.8 %collective-permute-start.8 = (f32[1,128]{1,0:T(1,128)S(1)}, f32[1,128]{1,0:T(1,128)S(1)}, u32[]{:S(2)}, u32[]{:S(2)}) collective-permute-start(f32[1,128]{1,0:T(1,128)S(1)} %add_add_fusion), channel_id=1, source_target_pairs={{0,8},{1,9},{2,10},{3,11},{4,12},{5,13},{6,14},{7,15},{8,0},{9,1},... | collective-permute-start | bytes 1544 | tf_op jit(solution)/shard_map/ppermute | solution.py:240
  41.0 2.6 %shard_map.56 = (f32[28,128,128]{2,1,0:T(8,128)S(1)}, f32[64,7168]{1,0:T(8,128)S(1)}, f32[64,7168]{1,0:T(8,128)S(1)}, f32[64,7168]{1,0:T(8,128)S(1)}) custom-call(bf16[32,112,128]{2,1,0:T(8,128)(2,1)S(1)} %all-to-all-done.grad_ref, f32[64,7168]{1,0:T(8,128)} %bitcast.11, f32[64,7168]{1,0:T(8,128)} %bitcast.12, f32[64,7168]{1,0:T(8,128)} %bitcast.13), custom_call_target="tpu_custom_call" | custom-call | tf_op jit(solution)/shard_map/pallas_call | solution.py:109
  43.7 2.1 %shard_map.57 = bf16[32,112,128]{2,1,0:T(8,128)(2,1)S(1)} custom-call(f32[1,128]{1,0:T(1,128)S(1)} %add.35.squares_ref, f32[28,128,128]{2,1,0:T(8,128)S(1)} %get-tuple-element.19.turned_ref, f32[64,7168]{1,0:T(8,128)S(1)} %get-tuple-element.20.master_ref, f32[64,7168]{1,0:T(8,128)S(1)} %get-tuple-element.21.first_ref, ...), custom_call_target="tpu_custom_call" | custom-call | tf_op jit(solution)/shard_map/pallas_call | solution.py:150
  45.8 22.3 %all_to_all.10.block_ref = bf16[32,112,128]{2,1,0:T(8,128)(2,1)S(1)} all-to-all(bf16[32,112,128]{2,1,0:T(8,128)(2,1)S(1)} %shard_map.57), channel_id=1, replica_groups=mesh['grp'=8,'fsdp'=32] {'fsdp'}, dimensions={0} | all-to-all | bytes 1835008 | tf_op jit(solution)/shard_map/all_to_all | solution.py:254
  68.6 1.9 %collective-permute-start.9 = (bf16[112,2048]{1,0:T(8,128)(2,1)S(1)}, bf16[112,2048]{1,0:T(8,128)(2,1)S(1)}, u32[]{:S(2)}, u32[]{:S(2)}) collective-permute-start(bf16[112,2048]{1,0:T(8,128)(2,1)S(1)} %get-tuple-element.23.refs_1_), channel_id=1, source_target_pairs={{0,64},{32,96},{64,128},{96,160},{128,192},{160,224},{192,0},{224,... | collective-permute-start | bytes 1376264 | tf_op jit(solution)/shard_map/ppermute | solution.py:185
  72.0 2.2 %collective-permute-start.12 = (bf16[112,2048]{1,0:T(8,128)(2,1)S(1)}, bf16[112,2048]{1,0:T(8,128)(2,1)S(1)}, u32[]{:S(2)}, u32[]{:S(2)}) collective-permute-start(bf16[112,2048]{1,0:T(8,128)(2,1)S(1)} %get-tuple-element.24.refs_8_), channel_id=1, source_target_pairs={{0,192},{32,224},{64,0},{96,32},{128,64},{160,96},{192,128},{224,1... | collective-permute-start | bytes 1376264 | tf_op jit(solution)/shard_map/ppermute | solution.py:185
  74.2 9.5 %collective-permute-start.16 = (bf16[112,2048]{1,0:T(8,128)(2,1)S(1)}, bf16[112,2048]{1,0:T(8,128)(2,1)S(1)}, u32[]{:S(2)}, u32[]{:S(2)}) collective-permute-start(bf16[112,2048]{1,0:T(8,128)(2,1)S(1)} %get-tuple-element.23.refs_1_), channel_id=1, source_target_pairs={{0,32},{32,0},{64,96},{96,64},{128,160},{160,128},{192,224},{224,1... | collective-permute-start | bytes 1376264 | tf_op jit(solution)/shard_map/ppermute | solution.py:189
  83.8 4.1 %collective-permute-start.21 = (bf16[112,2048]{1,0:T(8,128)(2,1)S(1)}, bf16[112,2048]{1,0:T(8,128)(2,1)S(1)}, u32[]{:S(2)}, u32[]{:S(2)}) collective-permute-start(bf16[112,2048]{1,0:T(8,128)(2,1)S(1)} %get-tuple-element.24.refs_8_), channel_id=1, source_target_pairs={{0,32},{32,0},{64,96},{96,64},{128,160},{160,128},{192,224},{224,1... | collective-permute-start | bytes 1376264 | tf_op jit(solution)/shard_map/ppermute | solution.py:189
  88.4 1.3 %collective-permute-start.10 = (bf16[112,2048]{1,0:T(8,128)(2,1)S(1)}, bf16[112,2048]{1,0:T(8,128)(2,1)S(1)}, u32[]{:S(2)}, u32[]{:S(2)}) collective-permute-start(bf16[112,2048]{1,0:T(8,128)(2,1)S(1)} %collective-permute-done.9.refs_5_), channel_id=1, source_target_pairs={{0,64},{32,96},{64,128},{96,160},{128,192},{160,224},{192,0},{224,... | collective-permute-start | bytes 1376264 | tf_op jit(solution)/shard_map/ppermute | solution.py:185
  89.7 1.4 %collective-permute-start.13 = (bf16[112,2048]{1,0:T(8,128)(2,1)S(1)}, bf16[112,2048]{1,0:T(8,128)(2,1)S(1)}, u32[]{:S(2)}, u32[]{:S(2)}) collective-permute-start(bf16[112,2048]{1,0:T(8,128)(2,1)S(1)} %collective-permute-done.12.refs_10_), channel_id=1, source_target_pairs={{0,192},{32,224},{64,0},{96,32},{128,64},{160,96},{192,128},{224,1... | collective-permute-start | bytes 1376264 | tf_op jit(solution)/shard_map/ppermute | solution.py:185
  91.1 5.0 %collective-permute-start.18 = (bf16[112,2048]{1,0:T(8,128)(2,1)S(1)}, bf16[112,2048]{1,0:T(8,128)(2,1)S(1)}, u32[]{:S(2)}, u32[]{:S(2)}) collective-permute-start(bf16[112,2048]{1,0:T(8,128)(2,1)S(1)} %collective-permute-done.17.refs_3_), channel_id=1, source_target_pairs={{0,32},{32,0},{64,96},{96,64},{128,160},{160,128},{192,224},{224,1... | collective-permute-start | bytes 1376264 | tf_op jit(solution)/shard_map/ppermute | solution.py:189
  97.4 5.2 %collective-permute-start.11 = (bf16[112,2048]{1,0:T(8,128)(2,1)S(1)}, bf16[112,2048]{1,0:T(8,128)(2,1)S(1)}, u32[]{:S(2)}, u32[]{:S(2)}) collective-permute-start(bf16[112,2048]{1,0:T(8,128)(2,1)S(1)} %collective-permute-done.10.refs_0_), channel_id=1, source_target_pairs={{0,32},{32,0},{64,96},{96,64},{128,160},{160,128},{192,224},{224,1... | collective-permute-start | bytes 1376264 | tf_op jit(solution)/shard_map/ppermute | solution.py:189
  103.1 2.2 %shard_map.59.refs_4_ = bf16[4,224,2048]{2,1,0:T(8,128)(2,1)} custom-call(s32[4]{0:T(128)S(1)} %bitcast.8, bf16[112,2048]{1,0:T(8,128)(2,1)S(1)} %collective-permute-done.15.refs_0_.refs_6_, bf16[112,2048]{1,0:T(8,128)(2,1)S(1)} %get-tuple-element.23.refs_1_, bf16[112,2048]{1,0:T(8,128)(2,1)S(1)} %collective-permute-done.16.refs_2_, ...), custom_call_target="tpu_custom_call" | custom-call | bytes 6422528 | tf_op jit(solution)/shard_map/pallas_call | solution.py:226
  105.4 1.6 %shard_map.60 = bf16[4,224,2048]{2,1,0:T(8,128)(2,1)} custom-call(s32[4]{0:T(128)S(1)} %bitcast.9, bf16[112,2048]{1,0:T(8,128)(2,1)S(1)} %collective-permute-done.10.refs_0_, bf16[112,2048]{1,0:T(8,128)(2,1)S(1)} %collective-permute-done.11.refs_1_, bf16[112,2048]{1,0:T(8,128)(2,1)S(1)} %collective-permute-done.13.refs_2_, ...), custom_call_target="tpu_custom_call", output_to_operand_aliasing={{}: (5, {})} | custom-call | bytes 1835008 | tf_op jit(solution)/shard_map/pallas_call | solution.py:226
  (40 shorter events, 11.3 us)
Async XLA Ops:
  2.3 38.7 %all-to-all-start = ((bf16[32,112,128]{2,1,0:T(8,128)(2,1)}), bf16[32,112,128]{2,1,0:T(8,128)(2,1)S(1)}, u32[]{:S(2)}, u32[]{:S(2)}) async-start(bf16[32,112,128]{2,1,0:T(8,128)(2,1)} %get-tuple-element.16), calls=%async_computation | async-start | bytes 1835008 | tf_op jit(solution)/shard_map/all_to_all | solution.py:247
  14.2 1.9 %collective-permute-start = (f32[1,128]{1,0:T(1,128)S(1)}, f32[1,128]{1,0:T(1,128)S(1)}, u32[]{:S(2)}, u32[]{:S(2)}) collective-permute-start(f32[1,128]{1,0:T(1,128)S(1)} %get-tuple-element.15), channel_id=1, source_target_pairs={{0,32},{32,0},{64,96},{96,64},{128,160},{160,128},{192,224},{224,1... | collective-permute-start | bytes 1544 | tf_op jit(solution)/shard_map/ppermute | solution.py:240
  16.1 2.7 %collective-permute-start.1 = (f32[1,128]{1,0:T(1,128)S(1)}, f32[1,128]{1,0:T(1,128)S(1)}, u32[]{:S(2)}, u32[]{:S(2)}) collective-permute-start(f32[1,128]{1,0:T(1,128)S(1)} %add.27), channel_id=1, source_target_pairs={{0,64},{32,96},{64,0},{96,32},{128,192},{160,224},{192,128},{224,1... | collective-permute-start | bytes 1544 | tf_op jit(solution)/shard_map/ppermute | solution.py:240
  18.8 4.0 %collective-permute-start.2 = (f32[1,128]{1,0:T(1,128)S(1)}, f32[1,128]{1,0:T(1,128)S(1)}, u32[]{:S(2)}, u32[]{:S(2)}) collective-permute-start(f32[1,128]{1,0:T(1,128)S(1)} %add.28), channel_id=1, source_target_pairs={{0,192},{32,224},{64,128},{96,160},{128,64},{160,96},{192,0},{224,... | collective-permute-start | bytes 1544 | tf_op jit(solution)/shard_map/ppermute | solution.py:240
  22.7 2.7 %collective-permute-start.3 = (f32[1,128]{1,0:T(1,128)S(1)}, f32[1,128]{1,0:T(1,128)S(1)}, u32[]{:S(2)}, u32[]{:S(2)}) collective-permute-start(f32[1,128]{1,0:T(1,128)S(1)} %add.29), channel_id=1, source_target_pairs={{0,1},{1,0},{2,3},{3,2},{4,5},{5,4},{6,7},{7,6},{8,9},{9,8},{10,11... | collective-permute-start | bytes 1544 | tf_op jit(solution)/shard_map/ppermute | solution.py:240
  25.5 4.0 %collective-permute-start.4 = (f32[1,128]{1,0:T(1,128)S(1)}, f32[1,128]{1,0:T(1,128)S(1)}, u32[]{:S(2)}, u32[]{:S(2)}) collective-permute-start(f32[1,128]{1,0:T(1,128)S(1)} %add.30), channel_id=1, source_target_pairs={{0,3},{1,2},{2,1},{3,0},{4,7},{5,6},{6,5},{7,4},{8,11},{9,10},{10,... | collective-permute-start | bytes 1544 | tf_op jit(solution)/shard_map/ppermute | solution.py:240
  29.4 4.8 %collective-permute-start.5 = (f32[1,128]{1,0:T(1,128)S(1)}, f32[1,128]{1,0:T(1,128)S(1)}, u32[]{:S(2)}, u32[]{:S(2)}) collective-permute-start(f32[1,128]{1,0:T(1,128)S(1)} %add.31), channel_id=1, source_target_pairs={{0,4},{1,5},{2,6},{3,7},{4,0},{5,1},{6,2},{7,3},{8,12},{9,13},{10,... | collective-permute-start | bytes 1544 | tf_op jit(solution)/shard_map/ppermute | solution.py:240
  30.9 3.7 %collective-permute-start.6 = (f32[1,128]{1,0:T(1,128)S(1)}, f32[1,128]{1,0:T(1,128)S(1)}, u32[]{:S(2)}, u32[]{:S(2)}) collective-permute-start(f32[1,128]{1,0:T(1,128)S(1)} %add.31), channel_id=1, source_target_pairs={{0,28},{1,29},{2,30},{3,31},{4,24},{5,25},{6,26},{7,27},{8,20},{9,... | collective-permute-start | bytes 1544 | tf_op jit(solution)/shard_map/ppermute | solution.py:240
  33.3 4.9 %collective-permute-start.7 = (f32[1,128]{1,0:T(1,128)S(1)}, f32[1,128]{1,0:T(1,128)S(1)}, u32[]{:S(2)}, u32[]{:S(2)}) collective-permute-start(f32[1,128]{1,0:T(1,128)S(1)} %add.31), channel_id=1, source_target_pairs={{0,24},{1,25},{2,26},{3,27},{4,28},{5,29},{6,30},{7,31},{8,16},{9,... | collective-permute-start | bytes 1544 | tf_op jit(solution)/shard_map/ppermute | solution.py:240
  38.2 5.4 %collective-permute-start.8 = (f32[1,128]{1,0:T(1,128)S(1)}, f32[1,128]{1,0:T(1,128)S(1)}, u32[]{:S(2)}, u32[]{:S(2)}) collective-permute-start(f32[1,128]{1,0:T(1,128)S(1)} %add_add_fusion), channel_id=1, source_target_pairs={{0,8},{1,9},{2,10},{3,11},{4,12},{5,13},{6,14},{7,15},{8,0},{9,1},... | collective-permute-start | bytes 1544 | tf_op jit(solution)/shard_map/ppermute | solution.py:240
  68.6 15.1 %collective-permute-start.9 = (bf16[112,2048]{1,0:T(8,128)(2,1)S(1)}, bf16[112,2048]{1,0:T(8,128)(2,1)S(1)}, u32[]{:S(2)}, u32[]{:S(2)}) collective-permute-start(bf16[112,2048]{1,0:T(8,128)(2,1)S(1)} %get-tuple-element.23.refs_1_), channel_id=1, source_target_pairs={{0,64},{32,96},{64,128},{96,160},{128,192},{160,224},{192,0},{224,... | collective-permute-start | bytes 1376264 | tf_op jit(solution)/shard_map/ppermute | solution.py:185
  70.5 17.3 %collective-permute-start.17 = (bf16[112,2048]{1,0:T(8,128)(2,1)S(1)}, bf16[112,2048]{1,0:T(8,128)(2,1)S(1)}, u32[]{:S(2)}, u32[]{:S(2)}) collective-permute-start(bf16[112,2048]{1,0:T(8,128)(2,1)S(1)} %get-tuple-element.23.refs_1_), channel_id=1, source_target_pairs={{0,192},{32,224},{64,0},{96,32},{128,64},{160,96},{192,128},{224,1... | collective-permute-start | bytes 1376264 | tf_op jit(solution)/shard_map/ppermute | solution.py:185
  71.6 16.8 %collective-permute-start.19 = (bf16[112,2048]{1,0:T(8,128)(2,1)S(1)}, bf16[112,2048]{1,0:T(8,128)(2,1)S(1)}, u32[]{:S(2)}, u32[]{:S(2)}) collective-permute-start(bf16[112,2048]{1,0:T(8,128)(2,1)S(1)} %get-tuple-element.24.refs_8_), channel_id=1, source_target_pairs={{0,64},{32,96},{64,128},{96,160},{128,192},{160,224},{192,0},{224,... | collective-permute-start | bytes 1376264 | tf_op jit(solution)/shard_map/ppermute | solution.py:185
  72.0 17.7 %collective-permute-start.12 = (bf16[112,2048]{1,0:T(8,128)(2,1)S(1)}, bf16[112,2048]{1,0:T(8,128)(2,1)S(1)}, u32[]{:S(2)}, u32[]{:S(2)}) collective-permute-start(bf16[112,2048]{1,0:T(8,128)(2,1)S(1)} %get-tuple-element.24.refs_8_), channel_id=1, source_target_pairs={{0,192},{32,224},{64,0},{96,32},{128,64},{160,96},{192,128},{224,1... | collective-permute-start | bytes 1376264 | tf_op jit(solution)/shard_map/ppermute | solution.py:185
  74.2 16.8 %collective-permute-start.16 = (bf16[112,2048]{1,0:T(8,128)(2,1)S(1)}, bf16[112,2048]{1,0:T(8,128)(2,1)S(1)}, u32[]{:S(2)}, u32[]{:S(2)}) collective-permute-start(bf16[112,2048]{1,0:T(8,128)(2,1)S(1)} %get-tuple-element.23.refs_1_), channel_id=1, source_target_pairs={{0,32},{32,0},{64,96},{96,64},{128,160},{160,128},{192,224},{224,1... | collective-permute-start | bytes 1376264 | tf_op jit(solution)/shard_map/ppermute | solution.py:189
  83.8 12.2 %collective-permute-start.21 = (bf16[112,2048]{1,0:T(8,128)(2,1)S(1)}, bf16[112,2048]{1,0:T(8,128)(2,1)S(1)}, u32[]{:S(2)}, u32[]{:S(2)}) collective-permute-start(bf16[112,2048]{1,0:T(8,128)(2,1)S(1)} %get-tuple-element.24.refs_8_), channel_id=1, source_target_pairs={{0,32},{32,0},{64,96},{96,64},{128,160},{160,128},{192,224},{224,1... | collective-permute-start | bytes 1376264 | tf_op jit(solution)/shard_map/ppermute | solution.py:189
  87.9 8.3 %collective-permute-start.15 = (bf16[112,2048]{1,0:T(8,128)(2,1)S(1)}, bf16[112,2048]{1,0:T(8,128)(2,1)S(1)}, u32[]{:S(2)}, u32[]{:S(2)}) collective-permute-start(bf16[112,2048]{1,0:T(8,128)(2,1)S(1)} %collective-permute-done.9.refs_5_), channel_id=1, source_target_pairs={{0,32},{32,0},{64,96},{96,64},{128,160},{160,128},{192,224},{224,1... | collective-permute-start | bytes 1376264 | tf_op jit(solution)/shard_map/ppermute | solution.py:189
  88.4 9.0 %collective-permute-start.10 = (bf16[112,2048]{1,0:T(8,128)(2,1)S(1)}, bf16[112,2048]{1,0:T(8,128)(2,1)S(1)}, u32[]{:S(2)}, u32[]{:S(2)}) collective-permute-start(bf16[112,2048]{1,0:T(8,128)(2,1)S(1)} %collective-permute-done.9.refs_5_), channel_id=1, source_target_pairs={{0,64},{32,96},{64,128},{96,160},{128,192},{160,224},{192,0},{224,... | collective-permute-start | bytes 1376264 | tf_op jit(solution)/shard_map/ppermute | solution.py:185
  89.7 12.9 %collective-permute-start.13 = (bf16[112,2048]{1,0:T(8,128)(2,1)S(1)}, bf16[112,2048]{1,0:T(8,128)(2,1)S(1)}, u32[]{:S(2)}, u32[]{:S(2)}) collective-permute-start(bf16[112,2048]{1,0:T(8,128)(2,1)S(1)} %collective-permute-done.12.refs_10_), channel_id=1, source_target_pairs={{0,192},{32,224},{64,0},{96,32},{128,64},{160,96},{192,128},{224,1... | collective-permute-start | bytes 1376264 | tf_op jit(solution)/shard_map/ppermute | solution.py:185
  91.1 12.1 %collective-permute-start.18 = (bf16[112,2048]{1,0:T(8,128)(2,1)S(1)}, bf16[112,2048]{1,0:T(8,128)(2,1)S(1)}, u32[]{:S(2)}, u32[]{:S(2)}) collective-permute-start(bf16[112,2048]{1,0:T(8,128)(2,1)S(1)} %collective-permute-done.17.refs_3_), channel_id=1, source_target_pairs={{0,32},{32,0},{64,96},{96,64},{128,160},{160,128},{192,224},{224,1... | collective-permute-start | bytes 1376264 | tf_op jit(solution)/shard_map/ppermute | solution.py:189
  96.0 7.1 %collective-permute-start.20 = (bf16[112,2048]{1,0:T(8,128)(2,1)S(1)}, bf16[112,2048]{1,0:T(8,128)(2,1)S(1)}, u32[]{:S(2)}, u32[]{:S(2)}) collective-permute-start(bf16[112,2048]{1,0:T(8,128)(2,1)S(1)} %collective-permute-done.19.refs_12_), channel_id=1, source_target_pairs={{0,32},{32,0},{64,96},{96,64},{128,160},{160,128},{192,224},{224,1... | collective-permute-start | bytes 1376264 | tf_op jit(solution)/shard_map/ppermute | solution.py:189
  96.1 7.0 %collective-permute-start.22 = (bf16[112,2048]{1,0:T(8,128)(2,1)S(1)}, bf16[112,2048]{1,0:T(8,128)(2,1)S(1)}, u32[]{:S(2)}, u32[]{:S(2)}) collective-permute-start(bf16[112,2048]{1,0:T(8,128)(2,1)S(1)} %collective-permute-done.12.refs_10_), channel_id=1, source_target_pairs={{0,32},{32,0},{64,96},{96,64},{128,160},{160,128},{192,224},{224,1... | collective-permute-start | bytes 1376264 | tf_op jit(solution)/shard_map/ppermute | solution.py:189
  97.4 8.0 %collective-permute-start.11 = (bf16[112,2048]{1,0:T(8,128)(2,1)S(1)}, bf16[112,2048]{1,0:T(8,128)(2,1)S(1)}, u32[]{:S(2)}, u32[]{:S(2)}) collective-permute-start(bf16[112,2048]{1,0:T(8,128)(2,1)S(1)} %collective-permute-done.10.refs_0_), channel_id=1, source_target_pairs={{0,32},{32,0},{64,96},{96,64},{128,160},{160,128},{192,224},{224,1... | collective-permute-start | bytes 1376264 | tf_op jit(solution)/shard_map/ppermute | solution.py:189
  102.6 2.8 %collective-permute-start.14 = (bf16[112,2048]{1,0:T(8,128)(2,1)S(1)}, bf16[112,2048]{1,0:T(8,128)(2,1)S(1)}, u32[]{:S(2)}, u32[]{:S(2)}) collective-permute-start(bf16[112,2048]{1,0:T(8,128)(2,1)S(1)} %collective-permute-done.13.refs_2_), channel_id=1, source_target_pairs={{0,32},{32,0},{64,96},{96,64},{128,160},{160,128},{192,224},{224,1... | collective-permute-start | bytes 1376264 | tf_op jit(solution)/shard_map/ppermute | solution.py:189
  (1 other events, 57.4 us)
